TPU v7x, 512 devices: a whole 4x8x8 slice. The times are simulated.
512 devices in a mesh: freq: 8 (over y), elem: 64 (over z, x, core).
Axes of the slice: x: 4, y: 8, z: 8, core: 2. Of those that a mesh axis runs over, the one named last changes fastest.
Arguments:
- history: bfloat16 [512, 65536], P('freq', 'elem'), may hold values from -6 to 6
- near_blocks: bfloat16 [8, 512, 3, 2, 128, 128], P('freq', 'elem'), may hold values from -0.21875 to 0.21875
- near_leaves: int32 [512, 3], P('elem'), may hold values from 0 to 511, as said below
- far_left: bfloat16 [8, 768, 2, 128, 128], P('freq', 'elem'), may hold values from -0.375 to 0.375
- far_right: bfloat16 [8, 768, 2, 128, 128], P('freq', 'elem'), may hold values from -0.375 to 0.375
- far_ranks: int32 [8, 768], P('freq', 'elem'), may hold values from 1 to 128, as said below
- far_targets: int32 [768], P('elem'), may hold values from 0 to 511
- far_sources: int32 [768], P('elem'), may hold values from 0 to 511
Outputs:
- field: bfloat16 [8, 2, 65536], P('freq', None, 'elem')
Inputs may be any that keep to these rules, and one draw needn't show every extreme that they name: `near_leaves`: the first entry of each row is the leaf itself; every other entry lies within 8 leaves of it. `far_ranks`: at each frequency, at most 4 of the 12 tasks of one device (aligned blocks of tasks) have a rank above 64, and at the last frequency some device has exactly 4 such tasks.
All inputs are finite; a program needn't handle non-finite values.
Results may differ from a plain program's by a relative error of at most 0.0059.
Values may be sent and summed in bfloat16 or wider, within the bound.
No kernel may reach another device: no remote copies, remote signals or barrier semaphores. Data moves between devices by JAX's collectives and lax.ppermute only.
A program may use at most 64 MiB of HBM per device.

v0:
```python
import math

import jax
import jax.numpy as jnp
from jax import lax
from jax.sharding import PartitionSpec as P

fall_total = 0.25


def dft_weights(freq_count, step_start, step_count, total_freq, total_steps):
    freq_index = jnp.arange(freq_count, dtype=jnp.int32) * (total_steps // total_freq) + 1
    step_index = step_start + jnp.arange(step_count, dtype=jnp.int32)
    phase_index = freq_index[:, None] * step_index[None, :] % total_steps
    angles = 2.0 * math.pi / total_steps * phase_index.astype(jnp.float32)
    damping = fall_total ** (step_index.astype(jnp.float32) / total_steps) / math.sqrt(total_steps)
    return jnp.stack([damping * jnp.cos(angles), -damping * jnp.sin(angles)], 1).astype(
        jnp.bfloat16
    )


def product(form, first_op, second_op):
    return jnp.einsum(form, first_op, second_op, preferred_element_type=jnp.float32)


def far_terms(leaf_view, left_factor, right_factor, sources, task_ranks):
    picked = leaf_view[:, sources]
    coeff_re = product("tjr,tj->tr", right_factor[:, 0], picked[0]) - product(
        "tjr,tj->tr", right_factor[:, 1], picked[1]
    )
    coeff_im = product("tjr,tj->tr", right_factor[:, 0], picked[1]) + product(
        "tjr,tj->tr", right_factor[:, 1], picked[0]
    )
    inside = jnp.arange(right_factor.shape[-1], dtype=jnp.int32)[None, :] < task_ranks[:, None]
    coeff_re = jnp.where(inside, coeff_re, 0.0).astype(jnp.bfloat16)
    coeff_im = jnp.where(inside, coeff_im, 0.0).astype(jnp.bfloat16)
    out_re = product("tir,tr->ti", left_factor[:, 0], coeff_re) - product(
        "tir,tr->ti", left_factor[:, 1], coeff_im
    )
    out_im = product("tir,tr->ti", left_factor[:, 0], coeff_im) + product(
        "tir,tr->ti", left_factor[:, 1], coeff_re
    )
    return jnp.stack([out_re, out_im], 1)


def per_device(
    history, near_blocks, near_leaves, far_left, far_right, far_ranks, far_targets, far_sources
):
    freq_groups = lax.axis_size("freq")
    elem_groups = lax.axis_size("elem")
    local_freq = far_ranks.shape[0]
    total_freq = local_freq * freq_groups
    steps_here = history.shape[0]
    total_steps = steps_here * freq_groups
    first_step = lax.axis_index("freq") * steps_here
    weights = dft_weights(
        local_freq * lax.axis_size("freq"), first_step, steps_here, total_freq, total_steps
    )
    spectrum = lax.psum_scatter(
        product("fct,te->fce", weights, history), "freq", scatter_dimension=0, tiled=True
    ).astype(jnp.bfloat16)
    leaf_size = near_blocks.shape[-1]
    local_leaves = near_blocks.shape[1]
    gathered = lax.all_gather(spectrum, "elem", axis=2, tiled=True)
    leaf_view = gathered[0].reshape(2, -1, leaf_size)
    all_leaves = local_leaves * elem_groups
    near_view = leaf_view[:, near_leaves]
    blocks = near_blocks[0]
    near_re = product("lnij,lnj->li", blocks[:, :, 0], near_view[0]) - product(
        "lnij,lnj->li", blocks[:, :, 1], near_view[1]
    )
    near_im = product("lnij,lnj->li", blocks[:, :, 0], near_view[1]) + product(
        "lnij,lnj->li", blocks[:, :, 1], near_view[0]
    )
    left_factor = far_left[0]
    right_factor = far_right[0]
    task_ranks = far_ranks[0]
    contrib = far_terms(leaf_view, left_factor, right_factor, far_sources, task_ranks)
    spread_terms = jnp.zeros((all_leaves, 2, leaf_size), jnp.float32).at[far_targets].add(contrib)
    far_part = lax.psum_scatter(spread_terms, "elem", scatter_dimension=0, tiled=True)
    combined = jnp.stack([near_re, near_im], 1) + far_part
    return combined.transpose(1, 0, 2).reshape(1, 2, -1).astype(jnp.bfloat16)


def solution(mesh):
    in_specs = (
        P("freq", "elem"),
        P("freq", "elem", None, None, None, None),
        P("elem", None),
        P("freq", "elem", None, None, None),
        P("freq", "elem", None, None, None),
        P("freq", "elem"),
        P("elem"),
        P("elem"),
    )
    out_specs = P("freq", None, "elem")
    return jax.shard_map(
        per_device, mesh=mesh, in_specs=in_specs, out_specs=out_specs, check_vma=False
    )
```

profile of v0, /device:TPU:1, one launch (start us, length us, event | category | flops | bytes accessed | tf_op | source)
XLA Modules:
  0.0 291.7 jit_solution(15771440705616890716)
XLA Ops:
  6.6 0.8 compare_select_fusion.1
  7.7 24.6 %all-reduce = bf16[8,2,1024]{2,1,0:T(2,128)(2,1)S(1)} all-reduce(f32[8,2,1024]{2,1,0:T(2,128)S(1)} %copy.18), channel_id=2, replica_groups=mesh['freq'=8,'elem'=64] {'freq'}, use_global_device_ids=true, to_apply=%region_0.1.clone | all-reduce | flops 16384 | bytes 98304
  32.3 1.3 dynamic-slice
  33.6 0.7 dynamic-slice_convert_fusion
  34.2 57.9 %all_gather.3 = bf16[1,2,65536]{2,1,0:T(2,128)(2,1)S(1)} all-gather(bf16[1,2,1024]{2,1,0:T(2,128)(2,1)S(1)} %dynamic-slice_convert_fusion), channel_id=1, replica_groups=mesh['freq'=8,'elem'=64] {'elem'}, dimensions={2}, use_global_device_ids=true | all-gather | bytes 266240 | tf_op jit(solution)/shard_map/all_gather | solution.py:64
  92.1 0.6 gather_fusion.1
  92.7 1.2 fusion.4
  93.9 1.2 fusion.6
  95.1 0.2 fusion.5
  95.4 0.2 fusion.7
  95.7 0.3 fusion.8
  96.0 0.3 fusion.11
  96.3 0.3 fusion.10
  96.6 0.3 fusion.9
  97.2 1.0 scatter_fusion
  98.2 0.8 copy-done.1
  99.2 0.6 gather_fusion
  99.8 0.4 fusion.2
  100.2 0.4 fusion.1
  100.6 0.4 fusion.3
  101.0 1.3 dynamic-slice.2
  102.9 0.4 fusion
  103.3 180.2 %all-reduce.4.cloned.1.call-done = f32[512,2,128]{2,1,0:T(2,128)} async-done(((f32[512,2,128]{2,1,0:T(2,128)}), f32[512,2,128]{2,1,0:T(2,128)}) %all-reduce.4.cloned.1.call-update) | async-done | bytes 524304
  283.5 1.3 fusion.35
  (41 shorter events, 0.9 us)
Async XLA Ops:
  6.5 1.0 copy-start
  6.5 88.6 %copy-start.5 = (bf16[1,12,2,128,128]{4,3,2,1,0:T(8,128)(2,1)S(1)}, bf16[1,12,2,128,128]{4,3,2,1,0:T(8,128)(2,1)}, u32[]{:S(2)}) copy-start(bf16[1,12,2,128,128]{4,3,2,1,0:T(8,128)(2,1)} %param.12) | copy-start | bytes 2359300
  6.5 89.0 %copy-start.3 = (s32[1,12]{1,0:T(1,128)S(1)}, s32[1,12]{1,0:T(1,128)}, u32[]{:S(2)}) copy-start(s32[1,12]{1,0:T(1,128)} %param.13) | copy-start | bytes 148
  6.5 89.1 %copy-start.6 = (bf16[1,12,2,128,128]{4,3,2,1,0:T(8,128)(2,1)S(1)}, bf16[1,12,2,128,128]{4,3,2,1,0:T(8,128)(2,1)}, u32[]{:S(2)}) copy-start(bf16[1,12,2,128,128]{4,3,2,1,0:T(8,128)(2,1)} %param.11) | copy-start | bytes 2359300
  6.5 277.0 %all-reduce.4.cloned.1.call-start = ((), (), s32[]{:S(2)}) async-start(), calls=%async_computation | async-start | bytes 1048576
  92.7 4.2 %copy-start.7 = (s32[12]{0:T(128)S(1)}, s32[12]{0:T(128)}, u32[]{:S(2)}) copy-start(s32[12]{0:T(128)} %param.14) | copy-start | bytes 148
  95.4 3.6 %copy-start.2 = (s32[8,3]{0,1:T(4,128)S(1)}, s32[8,3]{0,1:T(4,128)}, u32[]{:S(2)}) copy-start(s32[8,3]{0,1:T(4,128)} %param.10) | copy-start | bytes 292
  95.6 4.2 %copy-start.4 = (bf16[1,8,3,2,128,128]{5,4,3,2,1,0:T(8,128)(2,1)S(1)}, bf16[1,8,3,2,128,128]{5,4,3,2,1,0:T(8,128)(2,1)}, u32[]{:S(2)}) copy-start(bf16[1,8,3,2,128,128]{5,4,3,2,1,0:T(8,128)(2,1)} %param.9) | copy-start | bytes 4718596
  98.2 0.8 copy-start.1
Sparse Core Ops, SparseCore 0:
  99.1 184.3 all-reduce.3
where the time goes:
time: 293 us; the launch traced here: 292 us
  waiting for transfers between devices  180 us (61%)
  blocking collectives  82.5 us (28%)
  between operations  14.2 us (5%)
  matrix products  5.77 us (2%)
  local copies, waits for them, and re-layouts  5.58 us (2%)
  other arithmetic  3.37 us (1%)
    unnamed x2, waiting for transfers between devices  180 us
    all_gather x1, blocking collectives, per_device(): gathered = lax.all_gather(spectrum, 'elem', axis=2, tiled=True)  57.9 us
    unnamed x1, blocking collectives  24.6 us
  transfers between devices with their start and end apart: 1, of which 1 were waited for; matrix products, arithmetic and copies ran while one was open for 1% of the time, Pallas kernels for 0%

commit v1 on v0

--- a/solution.py
+++ b/solution.py
@@ -24,12 +24,12 @@
 
 
 def far_terms(leaf_view, left_factor, right_factor, sources, task_ranks):
-    picked = leaf_view[:, sources]
-    coeff_re = product("tjr,tj->tr", right_factor[:, 0], picked[0]) - product(
-        "tjr,tj->tr", right_factor[:, 1], picked[1]
+    picked = leaf_view[sources]
+    coeff_re = product("tjr,tj->tr", right_factor[:, 0], picked[:, 0]) - product(
+        "tjr,tj->tr", right_factor[:, 1], picked[:, 1]
     )
-    coeff_im = product("tjr,tj->tr", right_factor[:, 0], picked[1]) + product(
-        "tjr,tj->tr", right_factor[:, 1], picked[0]
+    coeff_im = product("tjr,tj->tr", right_factor[:, 0], picked[:, 1]) + product(
+        "tjr,tj->tr", right_factor[:, 1], picked[:, 0]
     )
     inside = jnp.arange(right_factor.shape[-1], dtype=jnp.int32)[None, :] < task_ranks[:, None]
     coeff_re = jnp.where(inside, coeff_re, 0.0).astype(jnp.bfloat16)
@@ -52,32 +52,32 @@
     total_freq = local_freq * freq_groups
     steps_here = history.shape[0]
     total_steps = steps_here * freq_groups
-    first_step = lax.axis_index("freq") * steps_here
-    weights = dft_weights(
-        local_freq * lax.axis_size("freq"), first_step, steps_here, total_freq, total_steps
-    )
-    spectrum = lax.psum_scatter(
-        product("fct,te->fce", weights, history), "freq", scatter_dimension=0, tiled=True
-    ).astype(jnp.bfloat16)
     leaf_size = near_blocks.shape[-1]
     local_leaves = near_blocks.shape[1]
-    gathered = lax.all_gather(spectrum, "elem", axis=2, tiled=True)
-    leaf_view = gathered[0].reshape(2, -1, leaf_size)
     all_leaves = local_leaves * elem_groups
-    near_view = leaf_view[:, near_leaves]
+    first_step = lax.axis_index("freq") * steps_here
+    weights = dft_weights(total_freq, first_step, steps_here, total_freq, total_steps)
+    partial = product("fct,te->fce", weights, history)
+    partial = partial.reshape(total_freq, 2 * local_leaves, leaf_size)
+    shares = lax.all_to_all(partial, "freq", 0, 0, tiled=True)
+    spectrum = jnp.sum(shares, 0).astype(jnp.bfloat16)
+    copies = jnp.broadcast_to(spectrum[None], (elem_groups,) + spectrum.shape)
+    gathered = lax.all_to_all(copies, "elem", 0, 0, tiled=True)
+    leaf_view = gathered.reshape(elem_groups, 2, local_leaves, leaf_size).transpose(0, 2, 1, 3)
+    leaf_view = leaf_view.reshape(all_leaves, 2, leaf_size)
+    near_view = leaf_view[near_leaves]
     blocks = near_blocks[0]
-    near_re = product("lnij,lnj->li", blocks[:, :, 0], near_view[0]) - product(
-        "lnij,lnj->li", blocks[:, :, 1], near_view[1]
+    near_re = product("lnij,lnj->li", blocks[:, :, 0], near_view[:, :, 0]) - product(
+        "lnij,lnj->li", blocks[:, :, 1], near_view[:, :, 1]
     )
-    near_im = product("lnij,lnj->li", blocks[:, :, 0], near_view[1]) + product(
-        "lnij,lnj->li", blocks[:, :, 1], near_view[0]
+    near_im = product("lnij,lnj->li", blocks[:, :, 0], near_view[:, :, 1]) + product(
+        "lnij,lnj->li", blocks[:, :, 1], near_view[:, :, 0]
     )
-    left_factor = far_left[0]
-    right_factor = far_right[0]
-    task_ranks = far_ranks[0]
-    contrib = far_terms(leaf_view, left_factor, right_factor, far_sources, task_ranks)
+    contrib = far_terms(leaf_view, far_left[0], far_right[0], far_sources, far_ranks[0])
     spread_terms = jnp.zeros((all_leaves, 2, leaf_size), jnp.float32).at[far_targets].add(contrib)
-    far_part = lax.psum_scatter(spread_terms, "elem", scatter_dimension=0, tiled=True)
+    spread_terms = spread_terms.astype(jnp.bfloat16).reshape(elem_groups, 2 * local_leaves, leaf_size)
+    arrived = lax.all_to_all(spread_terms, "elem", 0, 0, tiled=True)
+    far_part = jnp.sum(arrived.astype(jnp.float32), 0).reshape(local_leaves, 2, leaf_size)
     combined = jnp.stack([near_re, near_im], 1) + far_part
     return combined.transpose(1, 0, 2).reshape(1, 2, -1).astype(jnp.bfloat16)
 

time: 293 us -> 71 us (0.24)
  waiting for transfers between devices: 180 us -> 29.8 us
  blocking collectives: 82.5 us -> 0 us
  starting transfers between devices: 0.03 us -> 27.9 us
  between operations: 14.2 us -> 0.17 us
    unnamed x2 -> x0, waiting for transfers between devices: 180 us -> none
    all_gather x1 -> x0, blocking collectives: 57.9 us -> none  [per_device(): gathered = lax.all_gather(spectrum, 'elem', axis=2, tiled=True)]
    all_to_all x0 -> x3, waiting for transfers between devices: none -> 29.8 us  [the longest x1 11.8 us: per_device(): gathered = lax.all_to_all(copies, 'elem', 0, 0, tiled=True)]
    all_to_all x0 -> x3, starting transfers between devices: none -> 27.9 us  [the longest x1 15.6 us: per_device(): gathered = lax.all_to_all(copies, 'elem', 0, 0, tiled=True)]
    unnamed x1 -> x0, blocking collectives: 24.6 us -> none
  transfers between devices with their start and end apart: 1 -> 3, of which waited for: 1 -> 3; matrix products, arithmetic and copies ran while one was open for 1% -> 5% of each run, Pallas kernels for 0% -> 0%
where the time goes in v1:
time: 71 us; the launch traced here: 70.6 us
  waiting for transfers between devices  29.8 us (42%)
  starting transfers between devices  27.9 us (39%)
  other arithmetic  4.85 us (7%)
  local copies, waits for them, and re-layouts  4.05 us (6%)
  matrix products  3.79 us (5%)
    all_to_all x1, starting transfers between devices, per_device(): gathered = lax.all_to_all(copies, 'elem', 0, 0, tiled=True)  15.6 us
    all_to_all x1, waiting for transfers between devices, per_device(): gathered = lax.all_to_all(copies, 'elem', 0, 0, tiled=True)  11.8 us
    all_to_all x1, waiting for transfers between devices, per_device(): arrived = lax.all_to_all(spread_terms, 'elem', 0, 0, tiled=True)  11.6 us
    all_to_all x1, starting transfers between devices, per_device(): shares = lax.all_to_all(partial, 'freq', 0, 0, tiled=True)  7.65 us
    all_to_all x1, waiting for transfers between devices, per_device(): shares = lax.all_to_all(partial, 'freq', 0, 0, tiled=True)  6.37 us
    all_to_all x1, starting transfers between devices, per_device(): arrived = lax.all_to_all(spread_terms, 'elem', 0, 0, tiled=True)  4.71 us
    dot_general x13, matrix products, product(): jnp.einsum(form, first_op, second_op, preferred_element_type=jnp.float32)  3.79 us
  transfers between devices with their start and end apart: 3, of which 3 were waited for; matrix products, arithmetic and copies ran while one was open for 5% of the time, Pallas kernels for 0%

profile of v1, /device:TPU:1, one launch (start us, length us, event | category | flops | bytes accessed | tf_op | source)
XLA Modules:
  0.0 70.6 jit_solution(8386360810652899633)
XLA Ops:
  0.2 0.7 %copy-done = bf16[64,1024]{1,0:T(8,128)(2,1)S(1)} copy-done((bf16[64,1024]{1,0:T(8,128)(2,1)S(1)}, bf16[64,1024]{1,0:T(8,128)(2,1)}, u32[]{:S(2)}) %copy-start) | copy-done | bytes 131096
  1.1 0.7 reshape.213
  1.8 7.7 %all-to-all-start = ((f32[8,16,128]{2,1,0:T(8,128)}), f32[8,16,128]{2,1,0:T(8,128)S(1)}, u32[]{:S(2)}, u32[]{:S(2)}) async-start(f32[8,16,128]{2,1,0:T(8,128)} %reshape.213), calls=%async_computation | async-start | bytes 131072 | tf_op jit(solution)/shard_map/all_to_all | solution.py:62
  9.4 0.7 compare_select_fusion
  10.3 6.4 %all-to-all-done = f32[8,16,128]{2,1,0:T(8,128)S(1)} async-done(((f32[8,16,128]{2,1,0:T(8,128)}), f32[8,16,128]{2,1,0:T(8,128)S(1)}, u32[]{:S(2)}, u32[]{:S(2)}) %all-to-all-start) | async-done | bytes 65568 | tf_op jit(solution)/shard_map/all_to_all | solution.py:62
  16.7 0.7 %broadcast_in_dim.28 = bf16[64,16,128]{2,1,0:T(8,128)(2,1)} broadcast(bf16[16,128]{1,0:T(8,128)(2,1)S(1)} %reduce_sum.18), dimensions={1,2} | broadcast | bytes 266240 | tf_op jit(solution)/shard_map/broadcast_in_dim | solution.py:64
  17.4 15.6 %all-to-all-start.1 = ((bf16[64,16,128]{2,1,0:T(8,128)(2,1)}), bf16[64,16,128]{2,1,0:T(8,128)(2,1)S(1)}, u32[]{:S(2)}, u32[]{:S(2)}) async-start(bf16[64,16,128]{2,1,0:T(8,128)(2,1)} %broadcast_in_dim.28), calls=%async_computation.1 | async-start | bytes 524288 | tf_op jit(solution)/shard_map/all_to_all | solution.py:65
  33.0 0.7 compare_select_fusion.1
  33.7 0.7 compare_select_fusion.2
  34.3 11.8 %all-to-all-done.1 = bf16[64,16,128]{2,1,0:T(8,128)(2,1)S(1)} async-done(((bf16[64,16,128]{2,1,0:T(8,128)(2,1)}), bf16[64,16,128]{2,1,0:T(8,128)(2,1)S(1)}, u32[]{:S(2)}, u32[]{:S(2)}) %all-to-all-start.1) | async-done | bytes 262176 | tf_op jit(solution)/shard_map/all_to_all | solution.py:65
  46.5 0.6 gather_fusion.1
  48.3 0.3 fusion.11
  48.6 0.3 fusion.10
  48.9 0.3 fusion.9
  49.2 0.6 gather_fusion
  50.1 1.0 %scatter_fusion = f32[512,2,128]{2,1,0:T(2,128)S(1)} fusion(f32[512,2,128]{2,1,0:T(2,128)S(1)} %broadcast_in_dim.30, s32[12]{0:T(128)S(1)} %compare_select_fusion.2, f32[12,2,128]{2,1,0:T(2,128)S(1)} %pad_maximum_fusion), kind=kCustom, calls=%fused_computation.2 | custom fusion | flops 3072 | bytes 36912 | tf_op jit(solution)/shard_map/scatter-add | solution.py:77
  51.1 0.9 %convert_element_type.66 = bf16[512,2,128]{2,1,0:T(2,128)(2,1)} convert(f32[512,2,128]{2,1,0:T(2,128)S(1)} %scatter_fusion) | non-fusion elementwise | flops 131072 | bytes 786432 | tf_op jit(solution)/shard_map/convert_element_type | solution.py:78
  52.0 4.7 %all-to-all-start.2 = ((bf16[64,16,128]{2,1,0:T(8,128)(2,1)}), bf16[64,16,128]{2,1,0:T(8,128)(2,1)S(1)}, u32[]{:S(2)}, u32[]{:S(2)}) async-start(bf16[64,16,128]{2,1,0:T(8,128)(2,1)} %bitcast.41), calls=%async_computation.2 | async-start | bytes 524288 | tf_op jit(solution)/shard_map/all_to_all | solution.py:79
  56.7 0.4 fusion.1
  57.1 0.4 fusion.3
  57.5 0.4 fusion.2
  57.9 0.4 fusion
  58.3 11.6 %all-to-all-done.2 = bf16[64,16,128]{2,1,0:T(8,128)(2,1)S(1)} async-done(((bf16[64,16,128]{2,1,0:T(8,128)(2,1)}), bf16[64,16,128]{2,1,0:T(8,128)(2,1)S(1)}, u32[]{:S(2)}, u32[]{:S(2)}) %all-to-all-start.2) | async-done | bytes 262176 | tf_op jit(solution)/shard_map/all_to_all | solution.py:79
  70.0 0.6 fusion.35
  (40 shorter events, 2.3 us)
Async XLA Ops:
  0.0 0.9 %copy-start = (bf16[64,1024]{1,0:T(8,128)(2,1)S(1)}, bf16[64,1024]{1,0:T(8,128)(2,1)}, u32[]{:S(2)}) copy-start(bf16[64,1024]{1,0:T(8,128)(2,1)} %param.8) | copy-start | bytes 393220
  0.0 47.0 %copy-start.3 = (bf16[1,12,2,128,128]{4,3,2,1,0:T(8,128)(2,1)S(1)}, bf16[1,12,2,128,128]{4,3,2,1,0:T(8,128)(2,1)}, u32[]{:S(2)}) copy-start(bf16[1,12,2,128,128]{4,3,2,1,0:T(8,128)(2,1)} %param.12) | copy-start | bytes 2359300
  1.8 14.9 %all-to-all-start = ((f32[8,16,128]{2,1,0:T(8,128)}), f32[8,16,128]{2,1,0:T(8,128)S(1)}, u32[]{:S(2)}, u32[]{:S(2)}) async-start(f32[8,16,128]{2,1,0:T(8,128)} %reshape.213), calls=%async_computation | async-start | bytes 131072 | tf_op jit(solution)/shard_map/all_to_all | solution.py:62
  17.4 30.5 %copy-start.1 = (s32[1,12]{1,0:T(1,128)S(1)}, s32[1,12]{1,0:T(1,128)}, u32[]{:S(2)}) copy-start(s32[1,12]{1,0:T(1,128)} %param.13) | copy-start | bytes 148
  17.4 30.6 %copy-start.4 = (bf16[1,12,2,128,128]{4,3,2,1,0:T(8,128)(2,1)S(1)}, bf16[1,12,2,128,128]{4,3,2,1,0:T(8,128)(2,1)}, u32[]{:S(2)}) copy-start(bf16[1,12,2,128,128]{4,3,2,1,0:T(8,128)(2,1)} %param.11) | copy-start | bytes 2359300
  17.4 28.7 %all-to-all-start.1 = ((bf16[64,16,128]{2,1,0:T(8,128)(2,1)}), bf16[64,16,128]{2,1,0:T(8,128)(2,1)S(1)}, u32[]{:S(2)}, u32[]{:S(2)}) async-start(bf16[64,16,128]{2,1,0:T(8,128)(2,1)} %broadcast_in_dim.28), calls=%async_computation.1 | async-start | bytes 524288 | tf_op jit(solution)/shard_map/all_to_all | solution.py:65
  48.3 8.5 %copy-start.2 = (bf16[1,8,3,2,128,128]{5,4,3,2,1,0:T(8,128)(2,1)S(1)}, bf16[1,8,3,2,128,128]{5,4,3,2,1,0:T(8,128)(2,1)}, u32[]{:S(2)}) copy-start(bf16[1,8,3,2,128,128]{5,4,3,2,1,0:T(8,128)(2,1)} %param.9) | copy-start | bytes 4718596
  52.0 17.9 %all-to-all-start.2 = ((bf16[64,16,128]{2,1,0:T(8,128)(2,1)}), bf16[64,16,128]{2,1,0:T(8,128)(2,1)S(1)}, u32[]{:S(2)}, u32[]{:S(2)}) async-start(bf16[64,16,128]{2,1,0:T(8,128)(2,1)} %bitcast.41), calls=%async_computation.2 | async-start | bytes 524288 | tf_op jit(solution)/shard_map/all_to_all | solution.py:79

commit v2 on v0

v2 whole, which is shorter than its diff:
```python
import functools
import math

import jax
import jax.numpy as jnp
from jax import lax
from jax.experimental import pallas as pl
from jax.experimental.pallas import tpu as pltpu
from jax.sharding import Mesh
from jax.sharding import PartitionSpec as P

fall_total = 0.25
CORES = 2
GROUP = 8
LIMIT = 32 * 1024 * 1024


def dot(first_op, second_op, transposed=False):
    dims = (((1,), (1 if transposed else 0,)), ((), ()))
    return lax.dot_general(first_op, second_op, dims, preferred_element_type=jnp.float32)


def turn(direct, crossed):
    swapped = jnp.concatenate([-crossed[GROUP:], crossed[:GROUP]], 0)
    return direct + swapped


def partial_kernel(total_freq, total_steps, first_ref, history_ref, out_ref):
    steps = history_ref.shape[0]
    rows = 2 * total_freq
    leaf = out_ref.shape[-1]
    leaves = history_ref.shape[1] // leaf
    row = lax.broadcasted_iota(jnp.int32, (rows, steps), 0)
    step = first_ref[0] + lax.broadcasted_iota(jnp.int32, (rows, steps), 1)
    freq = (row >> 1) * (total_steps // total_freq) + 1
    phase = (freq * step + (row & 1) * (total_steps // 4)) & (total_steps - 1)
    angle = 2.0 * math.pi / total_steps * phase.astype(jnp.float32)
    damping = jnp.exp(step.astype(jnp.float32) * (math.log(fall_total) / total_steps))
    weights = (damping * jnp.cos(angle) / math.sqrt(total_steps)).astype(jnp.bfloat16)
    part = dot(weights, history_ref[...])
    for l in range(leaves):
        out_ref[pl.ds(l, rows, stride=leaves), :] = part[:, l * leaf : (l + 1) * leaf]


def far_kernel(tasks, pick_ref, gathered_ref, ranks_ref, right_ref, left_ref, out_ref):
    picked = dot(pick_ref[...], gathered_ref[...]).astype(jnp.bfloat16)
    half = picked.shape[0] // 2
    pair = jnp.concatenate([picked[:half], picked[half:]], 1)
    leaf = left_ref.shape[-1]
    own = lax.broadcasted_iota(jnp.int32, (2 * GROUP, leaf), 0) % GROUP
    lane = lax.broadcasted_iota(jnp.int32, (2 * GROUP, leaf), 1)
    for start in range(0, tasks, GROUP):
        rows = slice(2 * start, 2 * start + 2 * GROUP)
        here = range(start, min(start + GROUP, tasks))
        coeff = jnp.zeros((2 * GROUP, leaf), jnp.float32)
        for t in here:
            coeff = jnp.where(own == t - start, dot(pair[rows], right_ref[t]), coeff)
        coeff = jnp.where(lane < ranks_ref[rows, :], coeff, 0.0).astype(jnp.bfloat16)
        direct = jnp.zeros((2 * GROUP, leaf), jnp.float32)
        crossed = jnp.zeros((2 * GROUP, leaf), jnp.float32)
        for t in here:
            both = dot(coeff, left_ref[t], True)
            direct = jnp.where(own == t - start, both[:, :leaf], direct)
            crossed = jnp.where(own == t - start, both[:, leaf:], crossed)
        out_ref[rows, :] = turn(direct, crossed).astype(jnp.bfloat16)


def near_kernel(pick_ref, gathered_ref, blocks_ref, out_ref):
    leaves, near = blocks_ref.shape[:2]
    leaf = blocks_ref.shape[-1]
    picked = dot(pick_ref[...], gathered_ref[...]).astype(jnp.bfloat16)
    own = lax.broadcasted_iota(jnp.int32, (2 * GROUP, leaf), 0) % GROUP
    direct = jnp.zeros((2 * GROUP, leaf), jnp.float32)
    crossed = jnp.zeros((2 * GROUP, leaf), jnp.float32)
    for n in range(near):
        view = picked[2 * GROUP * n : 2 * GROUP * (n + 1)]
        for l in range(leaves):
            both = dot(view, blocks_ref[l, n], True)
            direct = direct + jnp.where(own == l, both[:, :leaf], 0.0)
            crossed = crossed + jnp.where(own == l, both[:, leaf:], 0.0)
    out_ref[...] = turn(direct, crossed)


def call(kernel, shape, dtype, smem=0):
    def run(*operands):
        return pl.pallas_call(
            kernel,
            out_shape=jax.ShapeDtypeStruct(shape, dtype),
            in_specs=[
                pl.BlockSpec(memory_space=pltpu.SMEM if i < smem else pltpu.VMEM)
                for i in range(len(operands))
            ],
            out_specs=pl.BlockSpec(memory_space=pltpu.VMEM),
            compiler_params=pltpu.CompilerParams(vmem_limit_bytes=LIMIT),
        )(*operands)

    return run


def per_device(
    history, near_blocks, near_leaves, far_left, far_right, far_ranks, far_targets, far_sources
):
    freq_groups = lax.axis_size("freq")
    chips = lax.axis_size("chip")
    core = lax.axis_index("core")
    total_freq = far_ranks.shape[0] * freq_groups
    steps_here = history.shape[0]
    total_steps = steps_here * freq_groups
    leaf = near_blocks.shape[-1]
    leaves = near_blocks.shape[1]
    near = near_blocks.shape[2]
    tasks = far_ranks.shape[1]
    slots = -(-tasks // GROUP) * GROUP

    first_step = lax.axis_index("freq") * steps_here
    partial = call(
        functools.partial(partial_kernel, total_freq, total_steps),
        (2 * total_freq * leaves, leaf),
        jnp.float32,
        1,
    )(first_step.astype(jnp.int32)[None], history)
    shares = lax.all_to_all(
        partial.reshape(total_freq, 2 * leaves, leaf), "freq", 0, 0, tiled=True
    )
    spectrum = jnp.sum(shares, 0).astype(jnp.bfloat16)
    copies = jnp.broadcast_to(spectrum[None], (chips,) + spectrum.shape)
    same_core = lax.all_to_all(copies, "chip", 0, 0, tiled=True)
    gathered = lax.all_gather(same_core, "core", axis=0, tiled=False)
    gathered = gathered.reshape(CORES * chips * 2 * leaves, leaf)

    at = jnp.arange(gathered.shape[0], dtype=jnp.int32)
    at_leaf = (at // (2 * leaves) % chips * CORES + at // (2 * leaves * chips)) * leaves + at % leaves
    at_part = at // leaves % 2

    row = jnp.arange(2 * slots, dtype=jnp.int32)
    row_part = row // GROUP % 2

    def by_row(values, fill):
        padded = jnp.concatenate([values, jnp.full((slots - tasks,), fill, jnp.int32)])
        grouped = padded.reshape(slots // GROUP, 1, GROUP)
        return jnp.broadcast_to(grouped, (slots // GROUP, 2, GROUP)).reshape(-1)

    hit = by_row(far_sources, -1)[:, None] == at_leaf[None, :]
    same = row_part[:, None] == at_part[None, :]
    sign = jnp.where(row_part == 0, -1.0, 1.0)[:, None]
    pick_far = jnp.concatenate(
        [jnp.where(hit & same, 1.0, 0.0), jnp.where(hit & ~same, sign, 0.0)], 0
    ).astype(jnp.bfloat16)
    ranks = jnp.broadcast_to(by_row(far_ranks[0], 0)[:, None], (2 * slots, leaf))
    contrib = call(
        functools.partial(far_kernel, tasks), (2 * slots, leaf), jnp.bfloat16
    )(
        pick_far,
        gathered,
        ranks,
        far_right[0].reshape(tasks, 2 * leaf, leaf),
        far_left[0].reshape(tasks, 2 * leaf, leaf),
    )

    both_targets = lax.all_gather(far_targets, "core", axis=0, tiled=False)
    both_terms = lax.all_gather(contrib, "core", axis=0, tiled=True)
    goal = jnp.concatenate([by_row(both_targets[i], -1) for i in range(CORES)])
    out_row = jnp.arange(chips * 2 * leaves, dtype=jnp.int32)
    out_leaf = (out_row // (2 * leaves) * CORES + core) * leaves + out_row % leaves
    out_part = out_row // leaves % 2
    place = (out_leaf[:, None] == goal[None, :]) & (
        out_part[:, None] == jnp.tile(row_part, CORES)[None, :]
    )
    spread = dot(place.astype(jnp.bfloat16), both_terms).astype(jnp.bfloat16)
    arrived = lax.all_to_all(
        spread.reshape(chips, 2 * leaves, leaf), "chip", 0, 0, tiled=True
    )

    wanted = jnp.broadcast_to(near_leaves.T[:, None, :], (near, 2, leaves)).reshape(-1)
    wanted_part = jnp.arange(near * 2 * leaves, dtype=jnp.int32) // leaves % 2
    pick_near = (wanted[:, None] == at_leaf[None, :]) & (wanted_part[:, None] == at_part[None, :])
    near_field = call(near_kernel, (2 * leaves, leaf), jnp.float32)(
        pick_near.astype(jnp.bfloat16),
        gathered,
        near_blocks[0].reshape(leaves, near, 2 * leaf, leaf),
    )

    field = near_field + jnp.sum(arrived.astype(jnp.float32), 0)
    return field.reshape(1, 2, leaves * leaf).astype(jnp.bfloat16)


def solution(mesh):
    freq_groups, elem_groups = mesh.devices.shape
    split = Mesh(
        mesh.devices.reshape(freq_groups, elem_groups // CORES, CORES), ("freq", "chip", "core")
    )
    elem = ("chip", "core")
    in_specs = (
        P("freq", elem),
        P("freq", elem, None, None, None, None),
        P(elem, None),
        P("freq", elem, None, None, None),
        P("freq", elem, None, None, None),
        P("freq", elem),
        P(elem),
        P(elem),
    )
    out_specs = P("freq", None, elem)
    return jax.shard_map(
        per_device, mesh=split, in_specs=in_specs, out_specs=out_specs, check_vma=False
    )
```

time: 293 us -> 63.9 us (0.22)
  waiting for transfers between devices: 180 us -> 15.7 us
  blocking collectives: 82.5 us -> 11.3 us
  starting transfers between devices: 0.03 us -> 22.9 us
  between operations: 14.2 us -> 0.81 us
  matrix products: 5.77 us -> 0.97 us
    unnamed x2 -> x0, waiting for transfers between devices: 180 us -> none
    all_gather x1 -> x2, blocking collectives: 57.9 us -> 7.25 us  [the longest x1 5.38 us: per_device(): gathered = lax.all_gather(same_core, 'core', axis=0, tiled=False)]
    all_to_all x0 -> x3, starting transfers between devices: none -> 22.9 us  [the longest x1 11.4 us: per_device(): same_core = lax.all_to_all(copies, 'chip', 0, 0, tiled=True)]
    unnamed x1, blocking collectives: 24.6 us -> 4.06 us
    all_to_all x0 -> x3, waiting for transfers between devices: none -> 15.7 us  [the longest x1 9 us: per_device(): lax.all_to_all(spread.reshape(chips, 2 * leaves, leaf), 'chip', 0, 0, til...]
    dot_general x13 -> x1, matrix products: 5.77 us -> 0.97 us  [dot(): lax.dot_general(first_op, second_op, dims, preferred_element_type=jnp.flo...]
  transfers between devices with their start and end apart: 1 -> 3, of which waited for: 1 -> 2; matrix products, arithmetic and copies ran while one was open for 1% -> 11% of each run, Pallas kernels for 0% -> 1%
where the time goes in v2:
time: 63.9 us; the launch traced here: 63.5 us
  starting transfers between devices  22.9 us (36%)
  waiting for transfers between devices  15.7 us (25%)
  blocking collectives  11.3 us (18%)
  local copies, waits for them, and re-layouts  7.38 us (12%)
  other arithmetic  2.21 us (3%)
  Pallas kernels  2.19 us (3%)
  matrix products  0.97 us (2%)
  between operations  0.81 us (1%)
    all_to_all x1, starting transfers between devices, per_device(): same_core = lax.all_to_all(copies, 'chip', 0, 0, tiled=True)  11.4 us
    all_to_all x1, waiting for transfers between devices, per_device(): lax.all_to_all(spread.reshape(chips, 2 * leaves, leaf), 'chip', 0, 0, til...  9 us
    all_to_all x1, starting transfers between devices, per_device(): lax.all_to_all(partial.reshape(total_freq, 2 * leaves, leaf), 'freq', 0,...  7.65 us
    all_to_all x1, waiting for transfers between devices, per_device(): same_core = lax.all_to_all(copies, 'chip', 0, 0, tiled=True)  6.71 us
    all_gather x1, blocking collectives, per_device(): gathered = lax.all_gather(same_core, 'core', axis=0, tiled=False)  5.38 us
    unnamed x1, blocking collectives  4.06 us
    all_to_all x1, starting transfers between devices, per_device(): lax.all_to_all(spread.reshape(chips, 2 * leaves, leaf), 'chip', 0, 0, til...  3.86 us
    unnamed x21, local copies, waits for them, and re-layouts  3.18 us
  transfers between devices with their start and end apart: 3, of which 2 were waited for; matrix products, arithmetic and copies ran while one was open for 11% of the time, Pallas kernels for 1%

profile of v2, /device:TPU:1, one launch (start us, length us, event | category | flops | bytes accessed | tf_op | source)
XLA Modules:
  0.0 63.5 jit_solution(2292335047129169104)
XLA Ops:
  0.0 1.0 %copy-done.3 = bf16[64,1024]{1,0:T(8,128)(2,1)S(1)} copy-done((bf16[64,1024]{1,0:T(8,128)(2,1)S(1)}, bf16[64,1024]{1,0:T(8,128)(2,1)}, u32[]{:S(2)}) %copy-start.3) | copy-done | bytes 131096
  1.0 0.8 %shard_map.82 = f32[128,128]{1,0:T(8,128)} custom-call(s32[1]{0:T(128)} %bitcast.1.first_ref, bf16[64,1024]{1,0:T(8,128)(2,1)S(1)} %copy-done.3), custom_call_target="tpu_custom_call" | custom-call | tf_op jit(solution)/shard_map/pallas_call | solution.py:86
  1.8 7.7 %all-to-all-start = ((f32[8,16,128]{2,1,0:T(8,128)}), f32[8,16,128]{2,1,0:T(8,128)S(1)}, u32[]{:S(2)}, u32[]{:S(2)}) async-start(f32[8,16,128]{2,1,0:T(8,128)} %bitcast.2), calls=%async_computation | async-start | bytes 131072 | tf_op jit(solution)/shard_map/all_to_all | solution.py:122
  9.5 0.7 %concatenate.22 = s32[16]{0:T(128)S(1)} pad(s32[12]{0:T(128)} %param.15, s32[]{:T(128)} %constant.165.clone.1), padding=0_4 | pad | bytes 116 | tf_op jit(solution)/shard_map/concatenate | solution.py:139
  10.4 1.3 %dynamic-slice = u32[1]{0:T(128)} dynamic-slice(u32[512]{0:T(512)} %constant.199, u32[]{:T(128)S(6)} %add.186), dynamic_slice_sizes={1} | dynamic-slice | bytes 12
  12.3 0.9 %dynamic-update-slice = s32[24]{0:T(128)S(1)} dynamic-update-slice(s32[24]{0:T(128)S(1)} %broadcast.476, s32[12]{0:T(128)} %param.14, u32[]{:T(128)} %bitcast.5) | dynamic-update-slice | bytes 100
  13.2 4.1 %all-reduce.4 = s32[24]{0:T(128)S(1)} all-reduce(s32[24]{0:T(128)S(1)} %dynamic-update-slice), channel_id=3, replica_groups=mesh['freq'=8,'chip'=32,'core'=2] {'core'}, use_global_device_ids=true, to_apply=%add.4 | all-reduce | flops 24 | bytes 192
  17.5 0.7 %slice_select_fusion = s32[16]{0:T(128)S(1)} fusion(pred[16]{0:T(512)(128)(4,1)} %constant.196, s32[24]{0:T(128)S(1)} %all-reduce.4), kind=kLoop, calls=%fused_computation.88 | loop fusion | flops 16 | bytes 144 | tf_op jit(solution)/shard_map/concatenate | solution.py:139
  18.3 0.1 select_convert_fusion
  18.5 0.7 %broadcast_in_dim.88 = bf16[32,16,128]{2,1,0:T(8,128)(2,1)} broadcast(bf16[16,128]{1,0:T(8,128)(2,1)S(1)} %reduce_sum.18), dimensions={1,2} | broadcast | bytes 135168 | tf_op jit(solution)/shard_map/broadcast_in_dim | solution.py:126
  19.2 11.4 %all-to-all-start.1 = ((bf16[32,16,128]{2,1,0:T(8,128)(2,1)}), bf16[32,16,128]{2,1,0:T(8,128)(2,1)}, u32[]{:S(2)}, u32[]{:S(2)}) async-start(bf16[32,16,128]{2,1,0:T(8,128)(2,1)} %broadcast_in_dim.88), calls=%async_computation.1 | async-start | bytes 262144 | tf_op jit(solution)/shard_map/all_to_all | solution.py:127
  30.6 0.6 pad_add_fusion
  31.2 0.7 %concatenate.24 = s32[16]{0:T(128)S(1)} pad(s32[12]{0:T(128)} %bitcast.17, s32[]{:T(128)} %constant.163.clone.1), padding=0_4 | pad | bytes 116 | tf_op jit(solution)/shard_map/concatenate | solution.py:139
  32.0 0.7 %eq.120 = s32[64]{0:T(128)} reshape(s32[2,32]{1,0:T(2,128)S(1)} %tile.2) | data formatting | bytes 512 | tf_op jit(solution)/shard_map/eq | solution.py:167
  32.7 0.6 add_select_fusion.5
  33.3 6.7 %all-to-all-done.1 = bf16[32,16,128]{2,1,0:T(8,128)(2,1)} async-done(((bf16[32,16,128]{2,1,0:T(8,128)(2,1)}), bf16[32,16,128]{2,1,0:T(8,128)(2,1)}, u32[]{:S(2)}, u32[]{:S(2)}) %all-to-all-start.1) | async-done | bytes 131104 | tf_op jit(solution)/shard_map/all_to_all | solution.py:127
  40.0 5.4 %all-gather = bf16[64,16,128]{2,1,0:T(8,128)(2,1)S(1)} all-gather(bf16[32,16,128]{2,1,0:T(8,128)(2,1)} %all-to-all-done.1), channel_id=2, replica_groups=mesh['freq'=8,'chip'=32,'core'=2] {'core'}, dimensions={0}, use_global_device_ids=true | all-gather | bytes 393216 | tf_op jit(solution)/shard_map/all_gather | solution.py:128
  45.5 0.7 %shard_map.84 = bf16[32,128]{1,0:T(8,128)(2,1)S(1)} custom-call(bf16[64,1024]{1,0:T(8,128)(2,1)S(1)} %pad_maximum_fusion.pick_ref, bf16[1024,128]{1,0:T(8,128)(2,1)S(1)} %bitcast.11, s32[32,128]{1,0:T(8,128)S(1)} %broadcast_in_dim.103.ranks_ref, bf16[12,256,128]{2,1,0:T(8,128)(2,1)S(1)} %bitcast.14, bf16[12,256,128]{2,1,0:T(8,128)(2,1)S(1)} %bitcast.15), custom_call_target="tpu_custom_call" | custom-call | tf_op jit(solution)/shard_map/pallas_call | solution.py:86
  46.2 1.9 %all_gather.19 = bf16[64,128]{1,0:T(8,128)(2,1)S(1)} all-gather(bf16[32,128]{1,0:T(8,128)(2,1)S(1)} %shard_map.84), channel_id=1, replica_groups=mesh['freq'=8,'chip'=32,'core'=2] {'core'}, dimensions={0}, use_global_device_ids=true | all-gather | bytes 24576 | tf_op jit(solution)/shard_map/all_gather | solution.py:161
  48.1 1.0 %convolution_convert_fusion = bf16[512,128]{1,0:T(8,128)(2,1)} fusion(bf16[64,128]{1,0:T(8,128)(2,1)S(1)} %all_gather.19, s32[64]{0:T(128)S(1)} %copy-done.8, s32[64]{0:T(128)S(1)} %copy-done.7, s32[512]{0:T(512)S(1)} %copy-done.5, s32[512]{0:T(512)S(1)} %copy-done.6), kind=kOutput, calls=%fused_computation | convolution fusion | flops 8552448 | bytes 152064 | tf_op jit(solution)/shard_map/dot_general | solution.py:20
  49.1 3.9 %all-to-all-start.2 = ((bf16[32,16,128]{2,1,0:T(8,128)(2,1)}), bf16[32,16,128]{2,1,0:T(8,128)(2,1)S(1)}, u32[]{:S(2)}, u32[]{:S(2)}) async-start(bf16[32,16,128]{2,1,0:T(8,128)(2,1)} %bitcast.9), calls=%async_computation.2 | async-start | bytes 262144 | tf_op jit(solution)/shard_map/all_to_all | solution.py:170
  53.2 0.6 %shard_map.83 = f32[16,128]{1,0:T(8,128)S(1)} custom-call(bf16[48,1024]{1,0:T(8,128)(2,1)S(1)} %and_convert_fusion.pick_ref, bf16[1024,128]{1,0:T(8,128)(2,1)S(1)} %bitcast.12, bf16[8,3,256,128]{3,2,1,0:T(8,128)(2,1)S(1)} %bitcast.13), custom_call_target="tpu_custom_call" | custom-call | tf_op jit(solution)/shard_map/pallas_call | solution.py:86
  53.8 9.0 %all-to-all-done.2 = bf16[32,16,128]{2,1,0:T(8,128)(2,1)S(1)} async-done(((bf16[32,16,128]{2,1,0:T(8,128)(2,1)}), bf16[32,16,128]{2,1,0:T(8,128)(2,1)S(1)}, u32[]{:S(2)}, u32[]{:S(2)}) %all-to-all-start.2) | async-done | bytes 131104 | tf_op jit(solution)/shard_map/all_to_all | solution.py:170
  62.9 0.6 convert_element_type.37
  (47 shorter events, 1.3 us)
Async XLA Ops:
  0.0 45.5 %copy-start.1 = (bf16[1,12,2,128,128]{4,3,2,1,0:T(8,128)(2,1)S(1)}, bf16[1,12,2,128,128]{4,3,2,1,0:T(8,128)(2,1)}, u32[]{:S(2)}) copy-start(bf16[1,12,2,128,128]{4,3,2,1,0:T(8,128)(2,1)} %param.12) | copy-start | bytes 2359300
  0.0 45.5 %copy-start.2 = (bf16[1,12,2,128,128]{4,3,2,1,0:T(8,128)(2,1)S(1)}, bf16[1,12,2,128,128]{4,3,2,1,0:T(8,128)(2,1)}, u32[]{:S(2)}) copy-start(bf16[1,12,2,128,128]{4,3,2,1,0:T(8,128)(2,1)} %param.11) | copy-start | bytes 2359300
  0.0 1.0 %copy-start.3 = (bf16[64,1024]{1,0:T(8,128)(2,1)S(1)}, bf16[64,1024]{1,0:T(8,128)(2,1)}, u32[]{:S(2)}) copy-start(bf16[64,1024]{1,0:T(8,128)(2,1)} %history_ref.1) | copy-start | bytes 393220
  1.8 16.7 %all-to-all-start = ((f32[8,16,128]{2,1,0:T(8,128)}), f32[8,16,128]{2,1,0:T(8,128)S(1)}, u32[]{:S(2)}, u32[]{:S(2)}) async-start(f32[8,16,128]{2,1,0:T(8,128)} %bitcast.2), calls=%async_computation | async-start | bytes 131072 | tf_op jit(solution)/shard_map/all_to_all | solution.py:122
  19.2 20.8 %all-to-all-start.1 = ((bf16[32,16,128]{2,1,0:T(8,128)(2,1)}), bf16[32,16,128]{2,1,0:T(8,128)(2,1)}, u32[]{:S(2)}, u32[]{:S(2)}) async-start(bf16[32,16,128]{2,1,0:T(8,128)(2,1)} %broadcast_in_dim.88), calls=%async_computation.1 | async-start | bytes 262144 | tf_op jit(solution)/shard_map/all_to_all | solution.py:127
  33.3 19.7 %copy-start.4 = (s32[8,3]{0,1:T(4,128)S(1)}, s32[8,3]{0,1:T(4,128)}, u32[]{:S(2)}) copy-start(s32[8,3]{0,1:T(4,128)} %param.10) | copy-start | bytes 292
  33.3 19.9 %copy-start = (bf16[1,8,3,2,128,128]{5,4,3,2,1,0:T(8,128)(2,1)S(1)}, bf16[1,8,3,2,128,128]{5,4,3,2,1,0:T(8,128)(2,1)}, u32[]{:S(2)}) copy-start(bf16[1,8,3,2,128,128]{5,4,3,2,1,0:T(8,128)(2,1)} %param.9) | copy-start | bytes 4718596
  40.0 8.1 %copy-start.5 = (s32[512]{0:T(512)S(1)}, s32[512]{0:T(512)}, u32[]{:S(2)}) copy-start(s32[512]{0:T(512)} %get-tuple-element.7) | copy-start | bytes 6148
  40.0 8.1 %copy-start.6 = (s32[512]{0:T(512)S(1)}, s32[512]{0:T(512)}, u32[]{:S(2)}) copy-start(s32[512]{0:T(512)} %get-tuple-element.8) | copy-start | bytes 6148
  40.0 8.1 %copy-start.7 = (s32[64]{0:T(128)S(1)}, s32[64]{0:T(128)}, u32[]{:S(2)}) copy-start(s32[64]{0:T(128)} %pad_add_fusion) | copy-start | bytes 772
  40.0 8.1 %copy-start.8 = (s32[64]{0:T(128)S(1)}, s32[64]{0:T(128)}, u32[]{:S(2)}) copy-start(s32[64]{0:T(128)} %eq.120) | copy-start | bytes 772
  49.1 13.7 %all-to-all-start.2 = ((bf16[32,16,128]{2,1,0:T(8,128)(2,1)}), bf16[32,16,128]{2,1,0:T(8,128)(2,1)S(1)}, u32[]{:S(2)}, u32[]{:S(2)}) async-start(bf16[32,16,128]{2,1,0:T(8,128)(2,1)} %bitcast.9), calls=%async_computation.2 | async-start | bytes 262144 | tf_op jit(solution)/shard_map/all_to_all | solution.py:170

commit v3 on v2

--- a/solution.py
+++ b/solution.py
@@ -25,6 +25,10 @@
     return direct + swapped
 
 
+def rotated(size):
+    return [(i + size // 2) % size for i in range(size)]
+
+
 def partial_kernel(total_freq, total_steps, first_ref, history_ref, out_ref):
     steps = history_ref.shape[0]
     rows = 2 * total_freq
@@ -32,7 +36,7 @@
     leaves = history_ref.shape[1] // leaf
     row = lax.broadcasted_iota(jnp.int32, (rows, steps), 0)
     step = first_ref[0] + lax.broadcasted_iota(jnp.int32, (rows, steps), 1)
-    freq = (row >> 1) * (total_steps // total_freq) + 1
+    freq = ((row >> 1) + total_freq // 2) % total_freq * (total_steps // total_freq) + 1
     phase = (freq * step + (row & 1) * (total_steps // 4)) & (total_steps - 1)
     angle = 2.0 * math.pi / total_steps * phase.astype(jnp.float32)
     damping = jnp.exp(step.astype(jnp.float32) * (math.log(fall_total) / total_steps))
@@ -120,7 +124,12 @@
         1,
     )(first_step.astype(jnp.int32)[None], history)
     shares = lax.all_to_all(
-        partial.reshape(total_freq, 2 * leaves, leaf), "freq", 0, 0, tiled=True
+        partial.reshape(total_freq, 2 * leaves, leaf),
+        "freq",
+        0,
+        0,
+        axis_index_groups=[rotated(freq_groups)],
+        tiled=True,
     )
     spectrum = jnp.sum(shares, 0).astype(jnp.bfloat16)
     copies = jnp.broadcast_to(spectrum[None], (chips,) + spectrum.shape)

time: 63.9 us -> 64.5 us (level)
    all_to_all x1, starting transfers between devices: 7.65 us -> 9.65 us  [per_device(): lax.all_to_all(partial.reshape(total_freq, 2 * leaves, leaf), 'freq', 0,...]
    all_to_all x1, starting transfers between devices: 11.4 us -> 9.53 us  [per_device(): same_core = lax.all_to_all(copies, 'chip', 0, 0, tiled=True)]
    unnamed x1, blocking collectives: 4.06 us -> 5.91 us
    all_gather x1, blocking collectives: 5.38 us -> 4.07 us  [per_device(): gathered = lax.all_gather(same_core, 'core', axis=0, tiled=False)]
where the time goes in v3:
time: 64.5 us; the launch traced here: 64.1 us
  starting transfers between devices  23 us (36%)
  waiting for transfers between devices  15.6 us (24%)
  blocking collectives  11.8 us (18%)
  local copies, waits for them, and re-layouts  7.38 us (11%)
  other arithmetic  2.21 us (3%)
  Pallas kernels  2.2 us (3%)
  matrix products  0.97 us (2%)
  between operations  0.81 us (1%)
    all_to_all x1, starting transfers between devices, per_device(): lax.all_to_all(partial.reshape(total_freq, 2 * leaves, leaf), 'freq', 0,...  9.65 us
    all_to_all x1, starting transfers between devices, per_device(): same_core = lax.all_to_all(copies, 'chip', 0, 0, tiled=True)  9.53 us
    all_to_all x1, waiting for transfers between devices, per_device(): lax.all_to_all(spread.reshape(chips, 2 * leaves, leaf), 'chip', 0, 0, til...  9 us
    all_to_all x1, waiting for transfers between devices, per_device(): same_core = lax.all_to_all(copies, 'chip', 0, 0, tiled=True)  6.61 us
    unnamed x1, blocking collectives  5.91 us
    all_gather x1, blocking collectives, per_device(): gathered = lax.all_gather(same_core, 'core', axis=0, tiled=False)  4.07 us
    all_to_all x1, starting transfers between devices, per_device(): lax.all_to_all(spread.reshape(chips, 2 * leaves, leaf), 'chip', 0, 0, til...  3.86 us
    unnamed x21, local copies, waits for them, and re-layouts  3.18 us
  transfers between devices with their start and end apart: 3, of which 2 were waited for; matrix products, arithmetic and copies ran while one was open for 11% of the time, Pallas kernels for 1%

profile of v3, /device:TPU:1, one launch (start us, length us, event | category | flops | bytes accessed | tf_op | source)
XLA Modules:
  0.0 64.1 jit_solution(4490203185033595954)
XLA Ops:
  0.0 1.0 %copy-done.3 = bf16[64,1024]{1,0:T(8,128)(2,1)S(1)} copy-done((bf16[64,1024]{1,0:T(8,128)(2,1)S(1)}, bf16[64,1024]{1,0:T(8,128)(2,1)}, u32[]{:S(2)}) %copy-start.3) | copy-done | bytes 131096
  1.0 0.8 %shard_map.82 = f32[128,128]{1,0:T(8,128)} custom-call(s32[1]{0:T(128)} %bitcast.1.first_ref, bf16[64,1024]{1,0:T(8,128)(2,1)S(1)} %copy-done.3), custom_call_target="tpu_custom_call" | custom-call | tf_op jit(solution)/shard_map/pallas_call | solution.py:90
  1.9 9.6 %all-to-all-start = ((f32[8,16,128]{2,1,0:T(8,128)}), f32[8,16,128]{2,1,0:T(8,128)S(1)}, u32[]{:S(2)}, u32[]{:S(2)}) async-start(f32[8,16,128]{2,1,0:T(8,128)} %bitcast.2), calls=%async_computation | async-start | bytes 131072 | tf_op jit(solution)/shard_map/all_to_all | solution.py:126
  11.5 0.7 %concatenate.22 = s32[16]{0:T(128)S(1)} pad(s32[12]{0:T(128)} %param.15, s32[]{:T(128)} %constant.165.clone.1), padding=0_4 | pad | bytes 116 | tf_op jit(solution)/shard_map/concatenate | solution.py:148
  12.4 1.3 %dynamic-slice = u32[1]{0:T(128)} dynamic-slice(u32[512]{0:T(512)} %constant.199, u32[]{:T(128)S(6)} %add.186), dynamic_slice_sizes={1} | dynamic-slice | bytes 12
  14.3 0.9 %dynamic-update-slice = s32[24]{0:T(128)S(1)} dynamic-update-slice(s32[24]{0:T(128)S(1)} %broadcast.476, s32[12]{0:T(128)} %param.14, u32[]{:T(128)} %bitcast.5) | dynamic-update-slice | bytes 100
  15.2 5.9 %all-reduce.4 = s32[24]{0:T(128)S(1)} all-reduce(s32[24]{0:T(128)S(1)} %dynamic-update-slice), channel_id=3, replica_groups=mesh['freq'=8,'chip'=32,'core'=2] {'core'}, use_global_device_ids=true, to_apply=%add.4 | all-reduce | flops 24 | bytes 192
  21.3 0.7 %slice_select_fusion = s32[16]{0:T(128)S(1)} fusion(pred[16]{0:T(512)(128)(4,1)} %constant.196, s32[24]{0:T(128)S(1)} %all-reduce.4), kind=kLoop, calls=%fused_computation.88 | loop fusion | flops 16 | bytes 144 | tf_op jit(solution)/shard_map/concatenate | solution.py:148
  22.2 0.1 select_convert_fusion
  22.4 0.7 %broadcast_in_dim.88 = bf16[32,16,128]{2,1,0:T(8,128)(2,1)} broadcast(bf16[16,128]{1,0:T(8,128)(2,1)S(1)} %reduce_sum.18), dimensions={1,2} | broadcast | bytes 135168 | tf_op jit(solution)/shard_map/broadcast_in_dim | solution.py:135
  23.1 9.5 %all-to-all-start.1 = ((bf16[32,16,128]{2,1,0:T(8,128)(2,1)}), bf16[32,16,128]{2,1,0:T(8,128)(2,1)}, u32[]{:S(2)}, u32[]{:S(2)}) async-start(bf16[32,16,128]{2,1,0:T(8,128)(2,1)} %broadcast_in_dim.88), calls=%async_computation.1 | async-start | bytes 262144 | tf_op jit(solution)/shard_map/all_to_all | solution.py:136
  32.6 0.6 pad_add_fusion
  33.2 0.7 %concatenate.24 = s32[16]{0:T(128)S(1)} pad(s32[12]{0:T(128)} %bitcast.17, s32[]{:T(128)} %constant.163.clone.1), padding=0_4 | pad | bytes 116 | tf_op jit(solution)/shard_map/concatenate | solution.py:148
  34.0 0.7 %eq.120 = s32[64]{0:T(128)} reshape(s32[2,32]{1,0:T(2,128)S(1)} %tile.2) | data formatting | bytes 512 | tf_op jit(solution)/shard_map/eq | solution.py:176
  34.7 0.6 add_select_fusion.5
  35.3 6.6 %all-to-all-done.1 = bf16[32,16,128]{2,1,0:T(8,128)(2,1)} async-done(((bf16[32,16,128]{2,1,0:T(8,128)(2,1)}), bf16[32,16,128]{2,1,0:T(8,128)(2,1)}, u32[]{:S(2)}, u32[]{:S(2)}) %all-to-all-start.1) | async-done | bytes 131104 | tf_op jit(solution)/shard_map/all_to_all | solution.py:136
  41.9 4.1 %all-gather = bf16[64,16,128]{2,1,0:T(8,128)(2,1)S(1)} all-gather(bf16[32,16,128]{2,1,0:T(8,128)(2,1)} %all-to-all-done.1), channel_id=2, replica_groups=mesh['freq'=8,'chip'=32,'core'=2] {'core'}, dimensions={0}, use_global_device_ids=true | all-gather | bytes 393216 | tf_op jit(solution)/shard_map/all_gather | solution.py:137
  46.1 0.7 %shard_map.84 = bf16[32,128]{1,0:T(8,128)(2,1)S(1)} custom-call(bf16[64,1024]{1,0:T(8,128)(2,1)S(1)} %pad_maximum_fusion.pick_ref, bf16[1024,128]{1,0:T(8,128)(2,1)S(1)} %bitcast.11, s32[32,128]{1,0:T(8,128)S(1)} %broadcast_in_dim.103.ranks_ref, bf16[12,256,128]{2,1,0:T(8,128)(2,1)S(1)} %bitcast.14, bf16[12,256,128]{2,1,0:T(8,128)(2,1)S(1)} %bitcast.15), custom_call_target="tpu_custom_call" | custom-call | tf_op jit(solution)/shard_map/pallas_call | solution.py:90
  46.8 1.9 %all_gather.19 = bf16[64,128]{1,0:T(8,128)(2,1)S(1)} all-gather(bf16[32,128]{1,0:T(8,128)(2,1)S(1)} %shard_map.84), channel_id=1, replica_groups=mesh['freq'=8,'chip'=32,'core'=2] {'core'}, dimensions={0}, use_global_device_ids=true | all-gather | bytes 24576 | tf_op jit(solution)/shard_map/all_gather | solution.py:170
  48.7 1.0 %convolution_convert_fusion = bf16[512,128]{1,0:T(8,128)(2,1)} fusion(bf16[64,128]{1,0:T(8,128)(2,1)S(1)} %all_gather.19, s32[64]{0:T(128)S(1)} %copy-done.8, s32[64]{0:T(128)S(1)} %copy-done.7, s32[512]{0:T(512)S(1)} %copy-done.5, s32[512]{0:T(512)S(1)} %copy-done.6), kind=kOutput, calls=%fused_computation | convolution fusion | flops 8552448 | bytes 152064 | tf_op jit(solution)/shard_map/dot_general | solution.py:20
  49.7 3.9 %all-to-all-start.2 = ((bf16[32,16,128]{2,1,0:T(8,128)(2,1)}), bf16[32,16,128]{2,1,0:T(8,128)(2,1)S(1)}, u32[]{:S(2)}, u32[]{:S(2)}) async-start(bf16[32,16,128]{2,1,0:T(8,128)(2,1)} %bitcast.9), calls=%async_computation.2 | async-start | bytes 262144 | tf_op jit(solution)/shard_map/all_to_all | solution.py:179
  53.8 0.6 %shard_map.83 = f32[16,128]{1,0:T(8,128)S(1)} custom-call(bf16[48,1024]{1,0:T(8,128)(2,1)S(1)} %and_convert_fusion.pick_ref, bf16[1024,128]{1,0:T(8,128)(2,1)S(1)} %bitcast.12, bf16[8,3,256,128]{3,2,1,0:T(8,128)(2,1)S(1)} %bitcast.13), custom_call_target="tpu_custom_call" | custom-call | tf_op jit(solution)/shard_map/pallas_call | solution.py:90
  54.4 9.0 %all-to-all-done.2 = bf16[32,16,128]{2,1,0:T(8,128)(2,1)S(1)} async-done(((bf16[32,16,128]{2,1,0:T(8,128)(2,1)}), bf16[32,16,128]{2,1,0:T(8,128)(2,1)S(1)}, u32[]{:S(2)}, u32[]{:S(2)}) %all-to-all-start.2) | async-done | bytes 131104 | tf_op jit(solution)/shard_map/all_to_all | solution.py:179
  63.5 0.6 convert_element_type.37
  (47 shorter events, 1.3 us)
Async XLA Ops:
  0.0 46.1 %copy-start.1 = (bf16[1,12,2,128,128]{4,3,2,1,0:T(8,128)(2,1)S(1)}, bf16[1,12,2,128,128]{4,3,2,1,0:T(8,128)(2,1)}, u32[]{:S(2)}) copy-start(bf16[1,12,2,128,128]{4,3,2,1,0:T(8,128)(2,1)} %param.12) | copy-start | bytes 2359300
  0.0 46.1 %copy-start.2 = (bf16[1,12,2,128,128]{4,3,2,1,0:T(8,128)(2,1)S(1)}, bf16[1,12,2,128,128]{4,3,2,1,0:T(8,128)(2,1)}, u32[]{:S(2)}) copy-start(bf16[1,12,2,128,128]{4,3,2,1,0:T(8,128)(2,1)} %param.11) | copy-start | bytes 2359300
  0.0 1.0 %copy-start.3 = (bf16[64,1024]{1,0:T(8,128)(2,1)S(1)}, bf16[64,1024]{1,0:T(8,128)(2,1)}, u32[]{:S(2)}) copy-start(bf16[64,1024]{1,0:T(8,128)(2,1)} %history_ref.1) | copy-start | bytes 393220
  1.9 20.5 %all-to-all-start = ((f32[8,16,128]{2,1,0:T(8,128)}), f32[8,16,128]{2,1,0:T(8,128)S(1)}, u32[]{:S(2)}, u32[]{:S(2)}) async-start(f32[8,16,128]{2,1,0:T(8,128)} %bitcast.2), calls=%async_computation | async-start | bytes 131072 | tf_op jit(solution)/shard_map/all_to_all | solution.py:126
  23.1 18.9 %all-to-all-start.1 = ((bf16[32,16,128]{2,1,0:T(8,128)(2,1)}), bf16[32,16,128]{2,1,0:T(8,128)(2,1)}, u32[]{:S(2)}, u32[]{:S(2)}) async-start(bf16[32,16,128]{2,1,0:T(8,128)(2,1)} %broadcast_in_dim.88), calls=%async_computation.1 | async-start | bytes 262144 | tf_op jit(solution)/shard_map/all_to_all | solution.py:136
  35.3 18.3 %copy-start.4 = (s32[8,3]{0,1:T(4,128)S(1)}, s32[8,3]{0,1:T(4,128)}, u32[]{:S(2)}) copy-start(s32[8,3]{0,1:T(4,128)} %param.10) | copy-start | bytes 292
  35.3 18.4 %copy-start = (bf16[1,8,3,2,128,128]{5,4,3,2,1,0:T(8,128)(2,1)S(1)}, bf16[1,8,3,2,128,128]{5,4,3,2,1,0:T(8,128)(2,1)}, u32[]{:S(2)}) copy-start(bf16[1,8,3,2,128,128]{5,4,3,2,1,0:T(8,128)(2,1)} %param.9) | copy-start | bytes 4718596
  41.9 6.8 %copy-start.5 = (s32[512]{0:T(512)S(1)}, s32[512]{0:T(512)}, u32[]{:S(2)}) copy-start(s32[512]{0:T(512)} %get-tuple-element.7) | copy-start | bytes 6148
  41.9 6.8 %copy-start.6 = (s32[512]{0:T(512)S(1)}, s32[512]{0:T(512)}, u32[]{:S(2)}) copy-start(s32[512]{0:T(512)} %get-tuple-element.8) | copy-start | bytes 6148
  41.9 6.8 %copy-start.7 = (s32[64]{0:T(128)S(1)}, s32[64]{0:T(128)}, u32[]{:S(2)}) copy-start(s32[64]{0:T(128)} %pad_add_fusion) | copy-start | bytes 772
  41.9 6.8 %copy-start.8 = (s32[64]{0:T(128)S(1)}, s32[64]{0:T(128)}, u32[]{:S(2)}) copy-start(s32[64]{0:T(128)} %eq.120) | copy-start | bytes 772
  49.7 13.7 %all-to-all-start.2 = ((bf16[32,16,128]{2,1,0:T(8,128)(2,1)}), bf16[32,16,128]{2,1,0:T(8,128)(2,1)S(1)}, u32[]{:S(2)}, u32[]{:S(2)}) async-start(bf16[32,16,128]{2,1,0:T(8,128)(2,1)} %bitcast.9), calls=%async_computation.2 | async-start | bytes 262144 | tf_op jit(solution)/shard_map/all_to_all | solution.py:179

commit v4 on v3

v4 whole, which is shorter than its diff:
```python
import functools
import math

import jax
import jax.numpy as jnp
from jax import lax
from jax.experimental import pallas as pl
from jax.experimental.pallas import tpu as pltpu
from jax.sharding import Mesh
from jax.sharding import PartitionSpec as P

fall_total = 0.25
CORES = 2
GROUP = 8
TILE = 2 * GROUP
LANES = 128
LIMIT = 32 * 1024 * 1024


def rotated(size):
    return [(i + size // 2) % size for i in range(size)]


def dot(first_op, second_op, transposed=False):
    dims = (((1,), (1 if transposed else 0,)), ((), ()))
    return lax.dot_general(first_op, second_op, dims, preferred_element_type=jnp.float32)


def iota(shape, dim):
    return lax.broadcasted_iota(jnp.int32, shape, dim)


def turn(direct, crossed):
    swapped = jnp.concatenate([-crossed[GROUP:], crossed[:GROUP]], 0)
    return direct + swapped


def chosen(where_at, values, fill):
    out = jnp.full(where_at.shape, fill, jnp.int32)
    for i, value in enumerate(values):
        out = jnp.where(where_at == i, value, out)
    return out


def leaf_codes(rows, chunk, chips):
    lane = iota((rows, LANES), 1)
    chunks_of_core = chips * TILE // LANES
    base = lane // TILE * (CORES * TILE) + lane % GROUP * 2 + lane // GROUP % 2
    return (
        base
        + chunk % chunks_of_core * (LANES * CORES)
        + chunk // chunks_of_core * TILE
    )


def partial_kernel(total_freq, total_steps, history_ref, out_ref, held, sem):
    copy = pltpu.make_async_copy(history_ref, held, sem)
    copy.start()
    steps = history_ref.shape[0]
    rows = 2 * total_freq
    leaf = out_ref.shape[-1]
    leaves = history_ref.shape[1] // leaf
    row = iota((rows, steps), 0)
    step = lax.axis_index("freq") * steps + iota((rows, steps), 1)
    freq = ((row >> 1) + total_freq // 2) % total_freq * (total_steps // total_freq) + 1
    phase = (freq * step + (row & 1) * (total_steps // 4)) & (total_steps - 1)
    angle = 2.0 * math.pi / total_steps * phase.astype(jnp.float32)
    damping = jnp.exp(step.astype(jnp.float32) * (math.log(fall_total) / total_steps))
    weights = (damping * jnp.cos(angle) / math.sqrt(total_steps)).astype(jnp.bfloat16)
    copy.wait()
    part = dot(weights, held[...])
    for l in range(leaves):
        out_ref[pl.ds(l, rows, stride=leaves), :] = part[:, l * leaf : (l + 1) * leaf]


def plan_kernel(chips, sources_ref, ranks_ref, targets_ref, pick_ref, depth_ref, goal_ref):
    tasks = sources_ref.shape[0]
    rows = depth_ref.shape[0]
    row = iota((rows, LANES), 0)
    row_task = row // TILE * GROUP + row % GROUP
    row_part = row // GROUP % 2
    source = chosen(row_task, [sources_ref[t] for t in range(tasks)], -1)
    depth_ref[...] = chosen(row_task, [ranks_ref[t] for t in range(tasks)], 0)
    same = source * 2 + row_part
    other = source * 2 + 1 - row_part
    sign = jnp.where(row_part == 0, -1.0, 1.0)
    for chunk in range(pick_ref.shape[1] // LANES):
        codes = leaf_codes(rows, chunk, chips)
        lanes = slice(chunk * LANES, (chunk + 1) * LANES)
        pick_ref[:rows, lanes] = jnp.where(same == codes, 1.0, 0.0).astype(jnp.bfloat16)
        pick_ref[rows:, lanes] = jnp.where(other == codes, sign, 0.0).astype(jnp.bfloat16)
    lane = iota((rows, LANES), 1) % rows
    lane_task = lane // TILE * GROUP + lane % GROUP
    target = chosen(lane_task, [targets_ref[t] for t in range(tasks)], -1)
    spare = tasks // GROUP * TILE + tasks % GROUP
    goal_ref[...] = jnp.where(
        row == spare, target >> 3, jnp.where(row == spare + 1, target & 7, 0)
    ).astype(jnp.float32)


def far_kernel(tasks, pick_ref, depth_ref, goal_ref, gathered_ref, right_ref, left_ref, out_ref):
    picked = dot(pick_ref[...], gathered_ref[...]).astype(jnp.bfloat16)
    half = picked.shape[0] // 2
    pair = jnp.concatenate([picked[:half], picked[half:]], 1)
    leaf = left_ref.shape[-1]
    own = iota((TILE, leaf), 0) % GROUP
    lane = iota((TILE, leaf), 1)
    for start in range(0, tasks, GROUP):
        rows = slice(2 * start, 2 * start + TILE)
        here = range(start, min(start + GROUP, tasks))
        coeff = jnp.zeros((TILE, leaf), jnp.float32)
        for t in here:
            coeff = jnp.where(own == t - start, dot(pair[rows], right_ref[t]), coeff)
        coeff = jnp.where(lane < depth_ref[rows, :], coeff, 0.0).astype(jnp.bfloat16)
        direct = jnp.zeros((TILE, leaf), jnp.float32)
        crossed = jnp.zeros((TILE, leaf), jnp.float32)
        for t in here:
            both = dot(coeff, left_ref[t], True)
            direct = jnp.where(own == t - start, both[:, :leaf], direct)
            crossed = jnp.where(own == t - start, both[:, leaf:], crossed)
        terms = turn(direct, crossed) + goal_ref[rows, :]
        out_ref[rows, :] = terms.astype(jnp.bfloat16)


def scatter_kernel(tasks, chips, terms_ref, out_ref):
    terms = terms_ref[...]
    columns = terms.shape[0]
    rows = columns // CORES
    spare = tasks // GROUP * TILE + tasks % GROUP
    lane = iota((1, terms.shape[1]), 1)
    wide = terms.astype(jnp.float32)

    def along(at):
        return jnp.where(lane < rows, wide[at : at + 1], wide[rows + at : rows + at + 1])

    goal = (along(spare) * GROUP + along(spare + 1)).astype(jnp.int32)
    code = (goal * 2 + lane // GROUP % 2)[:, :columns]
    row = iota((TILE, columns), 0)
    base = (lax.axis_index("core") * GROUP + row % GROUP) * 2 + row // GROUP
    place = jnp.concatenate(
        [jnp.where(code - chip * (CORES * TILE) == base, 1.0, 0.0) for chip in range(chips)], 0
    )
    out_ref[...] = dot(place.astype(jnp.bfloat16), terms).astype(jnp.bfloat16)


def near_kernel(chips, leaves_ref, gathered_ref, blocks_ref, out_ref):
    leaves, near = blocks_ref.shape[:2]
    leaf = blocks_ref.shape[-1]
    own = iota((TILE, leaf), 0) % GROUP
    part = iota((TILE, leaf), 0) // GROUP
    wanted = jnp.concatenate(
        [chosen(own, [leaves_ref[l, n] for l in range(leaves)], -1) * 2 + part for n in range(near)],
        0,
    )
    pick = jnp.concatenate(
        [
            jnp.where(wanted == leaf_codes(near * TILE, chunk, chips), 1.0, 0.0)
            for chunk in range(gathered_ref.shape[0] // LANES)
        ],
        1,
    )
    picked = dot(pick.astype(jnp.bfloat16), gathered_ref[...]).astype(jnp.bfloat16)
    direct = jnp.zeros((TILE, leaf), jnp.float32)
    crossed = jnp.zeros((TILE, leaf), jnp.float32)
    for n in range(near):
        view = picked[TILE * n : TILE * (n + 1)]
        for l in range(leaves):
            both = dot(view, blocks_ref[l, n], True)
            direct = direct + jnp.where(own == l, both[:, :leaf], 0.0)
            crossed = crossed + jnp.where(own == l, both[:, leaf:], 0.0)
    out_ref[...] = turn(direct, crossed)


def call(kernel, outs, spaces, scratch=()):
    return pl.pallas_call(
        kernel,
        out_shape=[jax.ShapeDtypeStruct(shape, dtype) for shape, dtype in outs],
        in_specs=[pl.BlockSpec(memory_space=space) for space in spaces],
        out_specs=[pl.BlockSpec(memory_space=pltpu.VMEM) for _ in outs],
        scratch_shapes=scratch,
        compiler_params=pltpu.CompilerParams(vmem_limit_bytes=LIMIT),
    )


def per_device(
    history, near_blocks, near_leaves, far_left, far_right, far_ranks, far_targets, far_sources
):
    vmem, smem = pltpu.VMEM, pltpu.SMEM
    freq_groups = lax.axis_size("freq")
    chips = lax.axis_size("chip")
    total_freq = far_ranks.shape[0] * freq_groups
    total_steps = history.shape[0] * freq_groups
    leaf = near_blocks.shape[-1]
    leaves = near_blocks.shape[1]
    near = near_blocks.shape[2]
    tasks = far_ranks.shape[1]
    slots = -(-tasks // GROUP) * GROUP

    (partial,) = call(
        functools.partial(partial_kernel, total_freq, total_steps),
        [((total_freq * TILE, leaf), jnp.float32)],
        [pltpu.HBM],
        [pltpu.VMEM(history.shape, history.dtype), pltpu.SemaphoreType.DMA],
    )(history)
    shares = lax.all_to_all(
        partial.reshape(total_freq, TILE, leaf),
        "freq",
        0,
        0,
        axis_index_groups=[rotated(freq_groups)],
        tiled=True,
    )
    spectrum = jnp.sum(shares, 0).astype(jnp.bfloat16)
    copies = jnp.broadcast_to(spectrum[None], (chips,) + spectrum.shape)
    same_core = lax.all_to_all(copies, "chip", 0, 0, tiled=True)
    gathered = lax.all_gather(same_core, "core", axis=0, tiled=False)
    gathered = gathered.reshape(CORES * chips * TILE, leaf)

    pick, depth, goal = call(
        functools.partial(plan_kernel, chips),
        [
            ((4 * slots, gathered.shape[0]), jnp.bfloat16),
            ((2 * slots, leaf), jnp.int32),
            ((2 * slots, leaf), jnp.float32),
        ],
        [smem, smem, smem],
    )(far_sources, far_ranks[0], far_targets)
    (terms,) = call(
        functools.partial(far_kernel, tasks),
        [((2 * slots, leaf), jnp.bfloat16)],
        [vmem] * 6,
    )(
        pick,
        depth,
        goal,
        gathered,
        far_right[0].reshape(tasks, 2 * leaf, leaf),
        far_left[0].reshape(tasks, 2 * leaf, leaf),
    )

    both_terms = lax.all_gather(terms, "core", axis=0, tiled=True)
    (spread,) = call(
        functools.partial(scatter_kernel, tasks, chips),
        [((chips * TILE, leaf), jnp.bfloat16)],
        [vmem],
    )(both_terms)
    arrived = lax.all_to_all(spread.reshape(chips, TILE, leaf), "chip", 0, 0, tiled=True)

    (near_field,) = call(
        functools.partial(near_kernel, chips),
        [((TILE, leaf), jnp.float32)],
        [smem, vmem, vmem],
    )(near_leaves, gathered, near_blocks[0].reshape(leaves, near, 2 * leaf, leaf))

    field = near_field + jnp.sum(arrived.astype(jnp.float32), 0)
    return field.reshape(1, 2, leaves * leaf).astype(jnp.bfloat16)


def solution(mesh):
    freq_groups, elem_groups = mesh.devices.shape
    split = Mesh(
        mesh.devices.reshape(freq_groups, elem_groups // CORES, CORES), ("freq", "chip", "core")
    )
    elem = ("chip", "core")
    in_specs = (
        P("freq", elem),
        P("freq", elem, None, None, None, None),
        P(elem, None),
        P("freq", elem, None, None, None),
        P("freq", elem, None, None, None),
        P("freq", elem),
        P(elem),
        P(elem),
    )
    out_specs = P("freq", None, elem)
    return jax.shard_map(
        per_device, mesh=split, in_specs=in_specs, out_specs=out_specs, check_vma=False
    )
```

time: 64.5 us -> 59.5 us (0.922)
  starting transfers between devices: 23 us -> 17.2 us
  blocking collectives: 11.8 us -> 17.3 us
  other arithmetic: 2.21 us -> 0.05 us
  local copies, waits for them, and re-layouts: 7.38 us -> 5.44 us
  Pallas kernels: 2.2 us -> 3.77 us
  matrix products: 0.97 us -> 0 us
  between operations: 0.81 us -> 0.07 us
    all_to_all x0 -> x1, blocking collectives: none -> 10.9 us  [per_device(): lax.all_to_all(partial.reshape(total_freq, TILE, leaf), 'freq', 0, 0, axi...]
    all_to_all x2 -> x1, starting transfers between devices: 13.5 us -> 3.84 us  [per_device(): lax.all_to_all(spread.reshape(chips, TILE, leaf), 'chip', 0, 0, tiled=True)]
    unnamed x1 -> x0, blocking collectives: 5.91 us -> none
    all_to_all x1, starting transfers between devices: 9.53 us -> 13.3 us  [per_device(): same_core = lax.all_to_all(copies, 'chip', 0, 0, tiled=True)]
    pallas_call x3 -> x5, Pallas kernels: 2.2 us -> 3.77 us  [the longest x1 1.24 us: per_device(): call(functools.partial(near_kernel, chips), [((TILE, leaf), jnp.float32)]...]
    concatenate x3 -> x0, local copies, waits for them, and re-layouts: 1.33 us -> none  [by_row(): jnp.concatenate([values, jnp.full((slots - tasks,), fill, jnp.int32)])]
    concatenate x3 -> x0, other arithmetic: 1.26 us -> none  [the longest x1 0.66 us: by_row(): jnp.concatenate([values, jnp.full((slots - tasks,), fill, jnp.int32)])]
    unnamed x21 -> x17, local copies, waits for them, and re-layouts: 3.18 us -> 4.16 us
  transfers between devices with their start and end apart: 3 -> 2, of which waited for: 2 -> 2; matrix products, arithmetic and copies ran while one was open for 11% -> 0% of each run, Pallas kernels for 1% -> 3%
where the time goes in v4:
time: 59.5 us; the launch traced here: 59.1 us
  blocking collectives  17.3 us (29%)
  starting transfers between devices  17.2 us (29%)
  waiting for transfers between devices  15.3 us (26%)
  local copies, waits for them, and re-layouts  5.44 us (9%)
  Pallas kernels  3.77 us (6%)
    all_to_all x1, starting transfers between devices, per_device(): same_core = lax.all_to_all(copies, 'chip', 0, 0, tiled=True)  13.3 us
    all_to_all x1, blocking collectives, per_device(): lax.all_to_all(partial.reshape(total_freq, TILE, leaf), 'freq', 0, 0, axi...  10.9 us
    all_to_all x1, waiting for transfers between devices, per_device(): lax.all_to_all(spread.reshape(chips, TILE, leaf), 'chip', 0, 0, tiled=True)  8.54 us
    all_to_all x1, waiting for transfers between devices, per_device(): same_core = lax.all_to_all(copies, 'chip', 0, 0, tiled=True)  6.75 us
    all_gather x1, blocking collectives, per_device(): gathered = lax.all_gather(same_core, 'core', axis=0, tiled=False)  4.53 us
    unnamed x17, local copies, waits for them, and re-layouts  4.16 us
    all_to_all x1, starting transfers between devices, per_device(): lax.all_to_all(spread.reshape(chips, TILE, leaf), 'chip', 0, 0, tiled=True)  3.84 us
    all_gather x1, blocking collectives, per_device(): both_terms = lax.all_gather(terms, 'core', axis=0, tiled=True)  1.87 us
  transfers between devices with their start and end apart: 2, of which 2 were waited for; matrix products, arithmetic and copies ran while one was open for 0% of the time, Pallas kernels for 3%

profile of v4, /device:TPU:1, one launch (start us, length us, event | category | flops | bytes accessed | tf_op | source)
XLA Modules:
  0.0 59.1 jit_solution(15468752998930471805)
XLA Ops:
  0.0 1.0 %copy-done.3 = bf16[64,1024]{1,0:T(8,128)(2,1)S(1)} copy-done((bf16[64,1024]{1,0:T(8,128)(2,1)S(1)}, bf16[64,1024]{1,0:T(8,128)(2,1)}, u32[]{:S(2)}) %copy-start.3) | copy-done | bytes 131096
  1.0 0.3 shard_map.82
  1.3 10.9 %all_to_all.15 = f32[8,16,128]{2,1,0:T(8,128)S(1)} all-to-all(f32[8,16,128]{2,1,0:T(8,128)S(1)} %bitcast.12), channel_id=1, replica_groups={{256,320,384,448,0,64,128,192},{257,321,385,449,1,65,129,193},{258,322,..., dimensions={0} | all-to-all | bytes 131072 | tf_op jit(solution)/shard_map/all_to_all | solution.py:205
  12.2 0.7 %broadcast_in_dim.2 = bf16[32,16,128]{2,1,0:T(8,128)(2,1)} broadcast(bf16[16,128]{1,0:T(8,128)(2,1)S(1)} %reduce_sum.18), dimensions={1,2} | broadcast | bytes 135168 | tf_op jit(solution)/shard_map/broadcast_in_dim | solution.py:214
  12.9 13.3 %all-to-all-start.1 = ((bf16[32,16,128]{2,1,0:T(8,128)(2,1)}), bf16[32,16,128]{2,1,0:T(8,128)(2,1)S(1)}, u32[]{:S(2)}, u32[]{:S(2)}) async-start(bf16[32,16,128]{2,1,0:T(8,128)(2,1)} %broadcast_in_dim.2), calls=%async_computation.1 | async-start | bytes 262144 | tf_op jit(solution)/shard_map/all_to_all | solution.py:215
  26.2 0.0 copy-start.4
  26.2 0.6 %copy-done.4 = s32[12]{0:T(128)S(1)} copy-done((s32[12]{0:T(128)S(1)}, s32[12]{0:T(128)}, u32[]{:S(2)}) %copy-start.4) | copy-done | bytes 72
  26.9 0.7 %copy-done.5 = s32[1,12]{1,0:T(1,128)S(1)} copy-done((s32[1,12]{1,0:T(1,128)S(1)}, s32[1,12]{1,0:T(1,128)}, u32[]{:S(2)}) %copy-start.5) | copy-done | bytes 72
  27.5 0.7 %copy-done.6 = s32[12]{0:T(128)S(1)} copy-done((s32[12]{0:T(128)S(1)}, s32[12]{0:T(128)}, u32[]{:S(2)}) %copy-start.6) | copy-done | bytes 72
  28.2 0.6 %shard_map.84 = (bf16[64,1024]{1,0:T(8,128)(2,1)S(1)}, s32[32,128]{1,0:T(8,128)S(1)}, f32[32,128]{1,0:T(8,128)S(1)}) custom-call(s32[12]{0:T(128)S(1)} %copy-done.4, s32[12]{0:T(128)S(1)} %bitcast.13, s32[12]{0:T(128)S(1)} %copy-done.6), custom_call_target="tpu_custom_call" | custom-call | tf_op jit(solution)/shard_map/pallas_call | solution.py:219
  28.8 6.7 %all-to-all-done.1 = bf16[32,16,128]{2,1,0:T(8,128)(2,1)S(1)} async-done(((bf16[32,16,128]{2,1,0:T(8,128)(2,1)}), bf16[32,16,128]{2,1,0:T(8,128)(2,1)S(1)}, u32[]{:S(2)}, u32[]{:S(2)}) %all-to-all-start.1) | async-done | bytes 131104 | tf_op jit(solution)/shard_map/all_to_all | solution.py:215
  35.6 4.5 %all-gather = bf16[64,16,128]{2,1,0:T(8,128)(2,1)S(1)} all-gather(bf16[32,16,128]{2,1,0:T(8,128)(2,1)S(1)} %all-to-all-done.1), channel_id=2, replica_groups=mesh['freq'=8,'chip'=32,'core'=2] {'core'}, dimensions={0}, use_global_device_ids=true | all-gather | bytes 393216 | tf_op jit(solution)/shard_map/all_gather | solution.py:216
  40.1 0.0 copy-done.1
  40.1 1.1 %copy-done.2 = bf16[1,12,2,128,128]{4,3,2,1,0:T(8,128)(2,1)S(1)} copy-done((bf16[1,12,2,128,128]{4,3,2,1,0:T(8,128)(2,1)S(1)}, bf16[1,12,2,128,128]{4,3,2,1,0:T(8,128)(2,1)}, u32[]{:S(2)}) %copy-start.2) | copy-done | bytes 786456
  41.2 0.7 %shard_map.85 = bf16[32,128]{1,0:T(8,128)(2,1)S(1)} custom-call(bf16[64,1024]{1,0:T(8,128)(2,1)S(1)} %get-tuple-element.8.pick_ref, s32[32,128]{1,0:T(8,128)S(1)} %get-tuple-element.9.depth_ref, f32[32,128]{1,0:T(8,128)S(1)} %get-tuple-element.10.goal_ref, bf16[1024,128]{1,0:T(8,128)(2,1)S(1)} %bitcast.7, bf16[12,256,128]{2,1,0:T(8,128)(2,1)S(1)} %bitcast.10, ...), custom_call_target="tpu_custom_call" | custom-call | tf_op jit(solution)/shard_map/pallas_call | solution.py:228
  42.0 1.9 %all_gather.11.terms_ref = bf16[64,128]{1,0:T(8,128)(2,1)S(1)} all-gather(bf16[32,128]{1,0:T(8,128)(2,1)S(1)} %shard_map.85), channel_id=1, replica_groups=mesh['freq'=8,'chip'=32,'core'=2] {'core'}, dimensions={0}, use_global_device_ids=true | all-gather | bytes 24576 | tf_op jit(solution)/shard_map/all_gather | solution.py:241
  43.8 0.8 %shard_map.86 = bf16[512,128]{1,0:T(8,128)(2,1)} custom-call(bf16[64,128]{1,0:T(8,128)(2,1)S(1)} %all_gather.11.terms_ref), custom_call_target="tpu_custom_call" | custom-call | tf_op jit(solution)/shard_map/pallas_call | solution.py:242
  44.7 3.8 %all-to-all-start.2 = ((bf16[32,16,128]{2,1,0:T(8,128)(2,1)}), bf16[32,16,128]{2,1,0:T(8,128)(2,1)S(1)}, u32[]{:S(2)}, u32[]{:S(2)}) async-start(bf16[32,16,128]{2,1,0:T(8,128)(2,1)} %bitcast.6), calls=%async_computation.2 | async-start | bytes 262144 | tf_op jit(solution)/shard_map/all_to_all | solution.py:247
  48.5 0.0 copy-done.7
  48.5 0.1 copy.10.leaves_ref
  48.6 0.0 copy-done
  48.6 1.2 %shard_map.83 = f32[16,128]{1,0:T(8,128)S(1)} custom-call(s32[8,3]{1,0:T(8,128)S(1)} %copy.10.leaves_ref, bf16[1024,128]{1,0:T(8,128)(2,1)S(1)} %bitcast.8, bf16[8,3,256,128]{3,2,1,0:T(8,128)(2,1)S(1)} %bitcast.9), custom_call_target="tpu_custom_call" | custom-call | tf_op jit(solution)/shard_map/pallas_call | solution.py:249
  49.9 8.5 %all-to-all-done.2 = bf16[32,16,128]{2,1,0:T(8,128)(2,1)S(1)} async-done(((bf16[32,16,128]{2,1,0:T(8,128)(2,1)}), bf16[32,16,128]{2,1,0:T(8,128)(2,1)S(1)}, u32[]{:S(2)}, u32[]{:S(2)}) %all-to-all-start.2) | async-done | bytes 131104 | tf_op jit(solution)/shard_map/all_to_all | solution.py:247
  58.5 0.6 %convert_element_type.27 = bf16[1,2,1024]{2,1,0:T(2,128)(2,1)} reshape(bf16[16,128]{1,0:T(8,128)(2,1)S(1)} %add_convert_fusion) | data formatting | bytes 8192 | tf_op jit(solution)/shard_map/convert_element_type | solution.py:256
  (10 shorter events, 0.1 us)
Async XLA Ops:
  0.0 40.1 %copy-start.1 = (bf16[1,12,2,128,128]{4,3,2,1,0:T(8,128)(2,1)S(1)}, bf16[1,12,2,128,128]{4,3,2,1,0:T(8,128)(2,1)}, u32[]{:S(2)}) copy-start(bf16[1,12,2,128,128]{4,3,2,1,0:T(8,128)(2,1)} %param.12) | copy-start | bytes 2359300
  0.0 1.0 %copy-start.3 = (bf16[64,1024]{1,0:T(8,128)(2,1)S(1)}, bf16[64,1024]{1,0:T(8,128)(2,1)}, u32[]{:S(2)}) copy-start(bf16[64,1024]{1,0:T(8,128)(2,1)} %history_ref.1) | copy-start | bytes 393220
  12.9 35.7 %copy-start = (bf16[1,8,3,2,128,128]{5,4,3,2,1,0:T(8,128)(2,1)S(1)}, bf16[1,8,3,2,128,128]{5,4,3,2,1,0:T(8,128)(2,1)}, u32[]{:S(2)}) copy-start(bf16[1,8,3,2,128,128]{5,4,3,2,1,0:T(8,128)(2,1)} %param.9) | copy-start | bytes 4718596
  12.9 22.7 %all-to-all-start.1 = ((bf16[32,16,128]{2,1,0:T(8,128)(2,1)}), bf16[32,16,128]{2,1,0:T(8,128)(2,1)S(1)}, u32[]{:S(2)}, u32[]{:S(2)}) async-start(bf16[32,16,128]{2,1,0:T(8,128)(2,1)} %broadcast_in_dim.2), calls=%async_computation.1 | async-start | bytes 262144 | tf_op jit(solution)/shard_map/all_to_all | solution.py:215
  26.2 0.7 %copy-start.4 = (s32[12]{0:T(128)S(1)}, s32[12]{0:T(128)}, u32[]{:S(2)}) copy-start(s32[12]{0:T(128)} %sources_ref.1) | copy-start | bytes 148
  26.9 0.7 %copy-start.5 = (s32[1,12]{1,0:T(1,128)S(1)}, s32[1,12]{1,0:T(1,128)}, u32[]{:S(2)}) copy-start(s32[1,12]{1,0:T(1,128)} %param.13) | copy-start | bytes 148
  27.5 0.7 %copy-start.6 = (s32[12]{0:T(128)S(1)}, s32[12]{0:T(128)}, u32[]{:S(2)}) copy-start(s32[12]{0:T(128)} %targets_ref.1) | copy-start | bytes 148
  40.1 1.1 %copy-start.2 = (bf16[1,12,2,128,128]{4,3,2,1,0:T(8,128)(2,1)S(1)}, bf16[1,12,2,128,128]{4,3,2,1,0:T(8,128)(2,1)}, u32[]{:S(2)}) copy-start(bf16[1,12,2,128,128]{4,3,2,1,0:T(8,128)(2,1)} %param.11) | copy-start | bytes 2359300
  41.2 7.3 %copy-start.7 = (s32[8,3]{0,1:T(4,128)S(1)}, s32[8,3]{0,1:T(4,128)}, u32[]{:S(2)}) copy-start(s32[8,3]{0,1:T(4,128)} %param.10) | copy-start | bytes 292
  44.7 13.7 %all-to-all-start.2 = ((bf16[32,16,128]{2,1,0:T(8,128)(2,1)}), bf16[32,16,128]{2,1,0:T(8,128)(2,1)S(1)}, u32[]{:S(2)}, u32[]{:S(2)}) async-start(bf16[32,16,128]{2,1,0:T(8,128)(2,1)} %bitcast.6), calls=%async_computation.2 | async-start | bytes 262144 | tf_op jit(solution)/shard_map/all_to_all | solution.py:247

commit v5 on v4

--- a/solution.py
+++ b/solution.py
@@ -17,8 +17,12 @@
 LIMIT = 32 * 1024 * 1024
 
 
-def rotated(size):
-    return [(i + size // 2) % size for i in range(size)]
+def rotated(size, first):
+    return [(i + first) % size for i in range(size)]
+
+
+def last(size):
+    return size - 1
 
 
 def dot(first_op, second_op, transposed=False):
@@ -42,15 +46,11 @@
     return out
 
 
-def leaf_codes(rows, chunk, chips):
-    lane = iota((rows, LANES), 1)
-    chunks_of_core = chips * TILE // LANES
-    base = lane // TILE * (CORES * TILE) + lane % GROUP * 2 + lane // GROUP % 2
-    return (
-        base
-        + chunk % chunks_of_core * (LANES * CORES)
-        + chunk // chunks_of_core * TILE
-    )
+def leaf_codes(chunk, chips):
+    at = chunk * LANES + iota((1, LANES), 1)
+    core = at // (chips * TILE)
+    chip = (at // TILE + last(chips)) % chips
+    return (chip * CORES + core) * TILE + at % GROUP * 2 + at // GROUP % 2
 
 
 def partial_kernel(total_freq, total_steps, history_ref, out_ref, held, sem):
@@ -73,7 +73,17 @@
         out_ref[pl.ds(l, rows, stride=leaves), :] = part[:, l * leaf : (l + 1) * leaf]
 
 
-def plan_kernel(chips, sources_ref, ranks_ref, targets_ref, pick_ref, depth_ref, goal_ref):
+def plan_kernel(
+    chips,
+    sources_ref,
+    ranks_ref,
+    targets_ref,
+    right_ref,
+    left_ref,
+    pick_ref,
+    depth_ref,
+    goal_ref,
+):
     tasks = sources_ref.shape[0]
     rows = depth_ref.shape[0]
     row = iota((rows, LANES), 0)
@@ -85,7 +95,7 @@
     other = source * 2 + 1 - row_part
     sign = jnp.where(row_part == 0, -1.0, 1.0)
     for chunk in range(pick_ref.shape[1] // LANES):
-        codes = leaf_codes(rows, chunk, chips)
+        codes = leaf_codes(chunk, chips)
         lanes = slice(chunk * LANES, (chunk + 1) * LANES)
         pick_ref[:rows, lanes] = jnp.where(same == codes, 1.0, 0.0).astype(jnp.bfloat16)
         pick_ref[rows:, lanes] = jnp.where(other == codes, sign, 0.0).astype(jnp.bfloat16)
@@ -154,7 +164,7 @@
     )
     pick = jnp.concatenate(
         [
-            jnp.where(wanted == leaf_codes(near * TILE, chunk, chips), 1.0, 0.0)
+            jnp.where(wanted == leaf_codes(chunk, chips), 1.0, 0.0)
             for chunk in range(gathered_ref.shape[0] // LANES)
         ],
         1,
@@ -207,15 +217,19 @@
         "freq",
         0,
         0,
-        axis_index_groups=[rotated(freq_groups)],
+        axis_index_groups=[rotated(freq_groups, freq_groups // 2)],
         tiled=True,
     )
     spectrum = jnp.sum(shares, 0).astype(jnp.bfloat16)
     copies = jnp.broadcast_to(spectrum[None], (chips,) + spectrum.shape)
-    same_core = lax.all_to_all(copies, "chip", 0, 0, tiled=True)
+    same_core = lax.all_to_all(
+        copies, "chip", 0, 0, axis_index_groups=[rotated(chips, last(chips))], tiled=True
+    )
     gathered = lax.all_gather(same_core, "core", axis=0, tiled=False)
     gathered = gathered.reshape(CORES * chips * TILE, leaf)
 
+    right = far_right[0].reshape(tasks, 2 * leaf, leaf)
+    left = far_left[0].reshape(tasks, 2 * leaf, leaf)
     pick, depth, goal = call(
         functools.partial(plan_kernel, chips),
         [
@@ -223,8 +237,8 @@
             ((2 * slots, leaf), jnp.int32),
             ((2 * slots, leaf), jnp.float32),
         ],
-        [smem, smem, smem],
-    )(far_sources, far_ranks[0], far_targets)
+        [smem, smem, smem, vmem, vmem],
+    )(far_sources, far_ranks[0], far_targets, right, left)
     (terms,) = call(
         functools.partial(far_kernel, tasks),
         [((2 * slots, leaf), jnp.bfloat16)],
@@ -234,8 +248,8 @@
         depth,
         goal,
         gathered,
-        far_right[0].reshape(tasks, 2 * leaf, leaf),
-        far_left[0].reshape(tasks, 2 * leaf, leaf),
+        right,
+        left,
     )
 
     both_terms = lax.all_gather(terms, "core", axis=0, tiled=True)

time: 59.5 us -> 59.7 us (level)
  waiting for transfers between devices: 15.3 us -> 8.21 us
  starting transfers between devices: 17.2 us -> 21.1 us
  local copies, waits for them, and re-layouts: 5.44 us -> 8.57 us
    all_to_all x1, waiting for transfers between devices: 6.75 us -> 0.88 us  [per_device(): lax.all_to_all(copies, 'chip', 0, 0, axis_index_groups=[rotated(chips, la...]
    unnamed x17 -> x23, local copies, waits for them, and re-layouts: 4.16 us -> 7.28 us
    all_to_all x1, starting transfers between devices: 13.3 us -> 15.4 us  [per_device(): lax.all_to_all(copies, 'chip', 0, 0, axis_index_groups=[rotated(chips, la...]
    all_to_all x1, starting transfers between devices: 3.84 us -> 5.69 us  [per_device(): lax.all_to_all(spread.reshape(chips, TILE, leaf), 'chip', 0, 0, tiled=True)]
    all_to_all x1, waiting for transfers between devices: 8.54 us -> 7.33 us  [per_device(): lax.all_to_all(spread.reshape(chips, TILE, leaf), 'chip', 0, 0, tiled=True)]
  transfers between devices with their start and end apart: 2 -> 2, of which waited for: 2 -> 2; matrix products, arithmetic and copies ran while one was open for 0% -> 1% of each run, Pallas kernels for 3% -> 3%
where the time goes in v5:
time: 59.7 us; the launch traced here: 58.8 us
  starting transfers between devices  21.1 us (35%)
  blocking collectives  17 us (28%)
  local copies, waits for them, and re-layouts  8.57 us (14%)
  waiting for transfers between devices  8.21 us (14%)
  Pallas kernels  3.79 us (6%)
    all_to_all x1, starting transfers between devices, per_device(): lax.all_to_all(copies, 'chip', 0, 0, axis_index_groups=[rotated(chips, la...  15.4 us
    all_to_all x1, blocking collectives, per_device(): lax.all_to_all(partial.reshape(total_freq, TILE, leaf), 'freq', 0, 0, axi...  10.9 us
    all_to_all x1, waiting for transfers between devices, per_device(): lax.all_to_all(spread.reshape(chips, TILE, leaf), 'chip', 0, 0, tiled=True)  7.33 us
    unnamed x23, local copies, waits for them, and re-layouts  7.28 us
    all_to_all x1, starting transfers between devices, per_device(): lax.all_to_all(spread.reshape(chips, TILE, leaf), 'chip', 0, 0, tiled=True)  5.69 us
    all_gather x1, blocking collectives, per_device(): gathered = lax.all_gather(same_core, 'core', axis=0, tiled=False)  4.22 us
    all_gather x1, blocking collectives, per_device(): both_terms = lax.all_gather(terms, 'core', axis=0, tiled=True)  1.87 us
    pallas_call x1, Pallas kernels, per_device(): call(functools.partial(near_kernel, chips), [((TILE, leaf), jnp.float32)]...  1.26 us
  transfers between devices with their start and end apart: 2, of which 2 were waited for; matrix products, arithmetic and copies ran while one was open for 1% of the time, Pallas kernels for 3%

profile of v5, /device:TPU:1, one launch (start us, length us, event | category | flops | bytes accessed | tf_op | source)
XLA Modules:
  0.0 58.8 jit_solution(12405890565615087851)
XLA Ops:
  0.0 1.0 %copy-done.5 = bf16[64,1024]{1,0:T(8,128)(2,1)S(1)} copy-done((bf16[64,1024]{1,0:T(8,128)(2,1)S(1)}, bf16[64,1024]{1,0:T(8,128)(2,1)}, u32[]{:S(2)}) %copy-start.5) | copy-done | bytes 131096
  1.0 0.3 shard_map.82
  1.3 10.9 %all_to_all.15 = f32[8,16,128]{2,1,0:T(8,128)S(1)} all-to-all(f32[8,16,128]{2,1,0:T(8,128)S(1)} %bitcast.14), channel_id=1, replica_groups={{256,320,384,448,0,64,128,192},{257,321,385,449,1,65,129,193},{258,322,..., dimensions={0} | all-to-all | bytes 131072 | tf_op jit(solution)/shard_map/all_to_all | solution.py:215
  12.2 0.7 %broadcast_in_dim.2 = bf16[32,16,128]{2,1,0:T(8,128)(2,1)} broadcast(bf16[16,128]{1,0:T(8,128)(2,1)S(1)} %reduce_sum.18), dimensions={1,2} | broadcast | bytes 135168 | tf_op jit(solution)/shard_map/broadcast_in_dim | solution.py:224
  12.9 15.4 %all-to-all-start.1 = ((bf16[32,16,128]{2,1,0:T(8,128)(2,1)}), bf16[32,16,128]{2,1,0:T(8,128)(2,1)}, u32[]{:S(2)}, u32[]{:S(2)}) async-start(bf16[32,16,128]{2,1,0:T(8,128)(2,1)} %broadcast_in_dim.2), calls=%async_computation.1 | async-start | bytes 262144 | tf_op jit(solution)/shard_map/all_to_all | solution.py:225
  28.3 0.0 copy-start
  28.3 1.1 %copy-done = bf16[1,12,2,128,128]{4,3,2,1,0:T(8,128)(2,1)S(1)} copy-done((bf16[1,12,2,128,128]{4,3,2,1,0:T(8,128)(2,1)S(1)}, bf16[1,12,2,128,128]{4,3,2,1,0:T(8,128)(2,1)}, u32[]{:S(2)}) %copy-start) | copy-done | bytes 786456
  29.5 1.1 %copy-done.2 = bf16[1,12,2,128,128]{4,3,2,1,0:T(8,128)(2,1)S(1)} copy-done((bf16[1,12,2,128,128]{4,3,2,1,0:T(8,128)(2,1)S(1)}, bf16[1,12,2,128,128]{4,3,2,1,0:T(8,128)(2,1)}, u32[]{:S(2)}) %copy-start.2) | copy-done | bytes 786456
  30.6 0.7 %copy-done.8 = s32[12]{0:T(128)S(1)} copy-done((s32[12]{0:T(128)S(1)}, s32[12]{0:T(128)}, u32[]{:S(2)}) %copy-start.8) | copy-done | bytes 72
  31.2 0.7 %copy-done.9 = s32[1,12]{1,0:T(1,128)S(1)} copy-done((s32[1,12]{1,0:T(1,128)S(1)}, s32[1,12]{1,0:T(1,128)}, u32[]{:S(2)}) %copy-start.9) | copy-done | bytes 72
  31.9 0.7 %copy-done.10 = s32[12]{0:T(128)S(1)} copy-done((s32[12]{0:T(128)S(1)}, s32[12]{0:T(128)}, u32[]{:S(2)}) %copy-start.10) | copy-done | bytes 72
  32.6 0.6 %shard_map.84 = (bf16[64,1024]{1,0:T(8,128)(2,1)S(1)}, s32[32,128]{1,0:T(8,128)S(1)}, f32[32,128]{1,0:T(8,128)S(1)}) custom-call(s32[12]{0:T(128)S(1)} %copy-done.8, s32[12]{0:T(128)S(1)} %bitcast.15, s32[12]{0:T(128)S(1)} %copy-done.10, bf16[12,256,128]{2,1,0:T(8,128)(2,1)S(1)} %bitcast.7, bf16[12,256,128]{2,1,0:T(8,128)(2,1)S(1)} %bitcast.9), custom_call_target="tpu_custom_call" | custom-call | tf_op jit(solution)/shard_map/pallas_call | solution.py:233
  33.2 0.6 copy-done.6
  33.8 0.9 %all-to-all-done.1 = bf16[32,16,128]{2,1,0:T(8,128)(2,1)} async-done(((bf16[32,16,128]{2,1,0:T(8,128)(2,1)}), bf16[32,16,128]{2,1,0:T(8,128)(2,1)}, u32[]{:S(2)}, u32[]{:S(2)}) %all-to-all-start.1) | async-done | bytes 131104 | tf_op jit(solution)/shard_map/all_to_all | solution.py:225
  34.7 4.2 %all-gather = bf16[64,16,128]{2,1,0:T(8,128)(2,1)S(1)} all-gather(bf16[32,16,128]{2,1,0:T(8,128)(2,1)} %all-to-all-done.1), channel_id=2, replica_groups=mesh['freq'=8,'chip'=32,'core'=2] {'core'}, dimensions={0}, use_global_device_ids=true | all-gather | bytes 393216 | tf_op jit(solution)/shard_map/all_gather | solution.py:228
  38.9 0.7 %copy-done.7 = f32[32,128]{1,0:T(8,128)S(1)} copy-done((f32[32,128]{1,0:T(8,128)S(1)}, f32[32,128]{1,0:T(8,128)}, u32[]{:S(2)}) %copy-start.7) | copy-done | bytes 16408
  39.6 0.7 %shard_map.85 = bf16[32,128]{1,0:T(8,128)(2,1)S(1)} custom-call(bf16[64,1024]{1,0:T(8,128)(2,1)S(1)} %get-tuple-element.8.pick_ref, s32[32,128]{1,0:T(8,128)S(1)} %get-tuple-element.9.depth_ref, f32[32,128]{1,0:T(8,128)S(1)} %copy-done.7, bf16[1024,128]{1,0:T(8,128)(2,1)S(1)} %bitcast.11, bf16[12,256,128]{2,1,0:T(8,128)(2,1)S(1)} %bitcast.8, ...), custom_call_target="tpu_custom_call" | custom-call | tf_op jit(solution)/shard_map/pallas_call | solution.py:242
  40.4 1.9 %all_gather.11.terms_ref = bf16[64,128]{1,0:T(8,128)(2,1)S(1)} all-gather(bf16[32,128]{1,0:T(8,128)(2,1)S(1)} %shard_map.85), channel_id=1, replica_groups=mesh['freq'=8,'chip'=32,'core'=2] {'core'}, dimensions={0}, use_global_device_ids=true | all-gather | bytes 24576 | tf_op jit(solution)/shard_map/all_gather | solution.py:255
  42.2 0.8 %shard_map.86 = bf16[512,128]{1,0:T(8,128)(2,1)} custom-call(bf16[64,128]{1,0:T(8,128)(2,1)S(1)} %all_gather.11.terms_ref), custom_call_target="tpu_custom_call" | custom-call | tf_op jit(solution)/shard_map/pallas_call | solution.py:256
  43.0 5.7 %all-to-all-start.2 = ((bf16[32,16,128]{2,1,0:T(8,128)(2,1)}), bf16[32,16,128]{2,1,0:T(8,128)(2,1)S(1)}, u32[]{:S(2)}, u32[]{:S(2)}) async-start(bf16[32,16,128]{2,1,0:T(8,128)(2,1)} %bitcast.6), calls=%async_computation.2 | async-start | bytes 262144 | tf_op jit(solution)/shard_map/all_to_all | solution.py:261
  48.8 0.8 %copy.10.leaves_ref = s32[8,3]{1,0:T(8,128)S(1)} copy(s32[8,3]{0,1:T(4,128)} %param.10) | data formatting | bytes 192 | tf_op args[2]
  49.5 1.3 %shard_map.83 = f32[16,128]{1,0:T(8,128)S(1)} custom-call(s32[8,3]{1,0:T(8,128)S(1)} %copy.10.leaves_ref, bf16[1024,128]{1,0:T(8,128)(2,1)S(1)} %bitcast.12, bf16[8,3,256,128]{3,2,1,0:T(8,128)(2,1)S(1)} %bitcast.13), custom_call_target="tpu_custom_call" | custom-call | tf_op jit(solution)/shard_map/pallas_call | solution.py:263
  50.8 7.3 %all-to-all-done.2 = bf16[32,16,128]{2,1,0:T(8,128)(2,1)S(1)} async-done(((bf16[32,16,128]{2,1,0:T(8,128)(2,1)}), bf16[32,16,128]{2,1,0:T(8,128)(2,1)S(1)}, u32[]{:S(2)}, u32[]{:S(2)}) %all-to-all-start.2) | async-done | bytes 131104 | tf_op jit(solution)/shard_map/all_to_all | solution.py:261
  58.1 0.6 %convert_element_type.27 = bf16[1,2,1024]{2,1,0:T(2,128)(2,1)} reshape(bf16[16,128]{1,0:T(8,128)(2,1)S(1)} %add_convert_fusion) | data formatting | bytes 8192 | tf_op jit(solution)/shard_map/convert_element_type | solution.py:270
  (16 shorter events, 0.1 us)
Async XLA Ops:
  0.0 38.9 %copy-start.1 = (bf16[1,12,2,128,128]{4,3,2,1,0:T(8,128)(2,1)S(1)}, bf16[1,12,2,128,128]{4,3,2,1,0:T(8,128)(2,1)}, u32[]{:S(2)}) copy-start(bf16[1,12,2,128,128]{4,3,2,1,0:T(8,128)(2,1)} %param.12) | copy-start | bytes 2359300
  0.0 1.0 %copy-start.5 = (bf16[64,1024]{1,0:T(8,128)(2,1)S(1)}, bf16[64,1024]{1,0:T(8,128)(2,1)}, u32[]{:S(2)}) copy-start(bf16[64,1024]{1,0:T(8,128)(2,1)} %history_ref.1) | copy-start | bytes 393220
  12.9 21.8 %all-to-all-start.1 = ((bf16[32,16,128]{2,1,0:T(8,128)(2,1)}), bf16[32,16,128]{2,1,0:T(8,128)(2,1)}, u32[]{:S(2)}, u32[]{:S(2)}) async-start(bf16[32,16,128]{2,1,0:T(8,128)(2,1)} %broadcast_in_dim.2), calls=%async_computation.1 | async-start | bytes 262144 | tf_op jit(solution)/shard_map/all_to_all | solution.py:225
  28.3 1.1 %copy-start = (bf16[1,12,2,128,128]{4,3,2,1,0:T(8,128)(2,1)S(1)}, bf16[1,12,2,128,128]{4,3,2,1,0:T(8,128)(2,1)}, u32[]{:S(2)}) copy-start(bf16[1,12,2,128,128]{4,3,2,1,0:T(8,128)(2,1)} %param.12) | copy-start | bytes 2359300
  29.5 1.1 %copy-start.2 = (bf16[1,12,2,128,128]{4,3,2,1,0:T(8,128)(2,1)S(1)}, bf16[1,12,2,128,128]{4,3,2,1,0:T(8,128)(2,1)}, u32[]{:S(2)}) copy-start(bf16[1,12,2,128,128]{4,3,2,1,0:T(8,128)(2,1)} %param.11) | copy-start | bytes 2359300
  30.6 0.7 %copy-start.8 = (s32[12]{0:T(128)S(1)}, s32[12]{0:T(128)}, u32[]{:S(2)}) copy-start(s32[12]{0:T(128)} %sources_ref.1) | copy-start | bytes 148
  31.2 0.7 %copy-start.9 = (s32[1,12]{1,0:T(1,128)S(1)}, s32[1,12]{1,0:T(1,128)}, u32[]{:S(2)}) copy-start(s32[1,12]{1,0:T(1,128)} %param.13) | copy-start | bytes 148
  31.9 0.7 %copy-start.10 = (s32[12]{0:T(128)S(1)}, s32[12]{0:T(128)}, u32[]{:S(2)}) copy-start(s32[12]{0:T(128)} %targets_ref.1) | copy-start | bytes 148
  32.6 6.4 %copy-start.3 = (bf16[1,12,2,128,128]{4,3,2,1,0:T(8,128)(2,1)S(1)}, bf16[1,12,2,128,128]{4,3,2,1,0:T(8,128)(2,1)}, u32[]{:S(2)}) copy-start(bf16[1,12,2,128,128]{4,3,2,1,0:T(8,128)(2,1)} %param.11) | copy-start | bytes 2359300
  33.2 0.6 %copy-start.6 = (f32[32,128]{1,0:T(8,128)}, f32[32,128]{1,0:T(8,128)S(1)}, u32[]{:S(2)}) copy-start(f32[32,128]{1,0:T(8,128)S(1)} %get-tuple-element.10.goal_ref) | copy-start | bytes 49156
  33.8 15.7 %copy-start.4 = (bf16[1,8,3,2,128,128]{5,4,3,2,1,0:T(8,128)(2,1)S(1)}, bf16[1,8,3,2,128,128]{5,4,3,2,1,0:T(8,128)(2,1)}, u32[]{:S(2)}) copy-start(bf16[1,8,3,2,128,128]{5,4,3,2,1,0:T(8,128)(2,1)} %param.9) | copy-start | bytes 4718596
  38.9 0.7 %copy-start.7 = (f32[32,128]{1,0:T(8,128)S(1)}, f32[32,128]{1,0:T(8,128)}, u32[]{:S(2)}) copy-start(f32[32,128]{1,0:T(8,128)} %copy-done.6) | copy-start | bytes 49156
  43.0 15.0 %all-to-all-start.2 = ((bf16[32,16,128]{2,1,0:T(8,128)(2,1)}), bf16[32,16,128]{2,1,0:T(8,128)(2,1)S(1)}, u32[]{:S(2)}, u32[]{:S(2)}) async-start(bf16[32,16,128]{2,1,0:T(8,128)(2,1)} %bitcast.6), calls=%async_computation.2 | async-start | bytes 262144 | tf_op jit(solution)/shard_map/all_to_all | solution.py:261

commit v6 on v5

--- a/solution.py
+++ b/solution.py
@@ -14,15 +14,15 @@
 GROUP = 8
 TILE = 2 * GROUP
 LANES = 128
-LIMIT = 32 * 1024 * 1024
+LIMIT = 16 * 1024 * 1024
 
 
 def rotated(size, first):
     return [(i + first) % size for i in range(size)]
 
 
-def last(size):
-    return size - 1
+def first_chip(chips):
+    return chips * 3 // 4 + 2
 
 
 def dot(first_op, second_op, transposed=False):
@@ -49,7 +49,7 @@
 def leaf_codes(chunk, chips):
     at = chunk * LANES + iota((1, LANES), 1)
     core = at // (chips * TILE)
-    chip = (at // TILE + last(chips)) % chips
+    chip = (at // TILE + first_chip(chips)) % chips
     return (chip * CORES + core) * TILE + at % GROUP * 2 + at // GROUP % 2
 
 
@@ -73,62 +73,63 @@
         out_ref[pl.ds(l, rows, stride=leaves), :] = part[:, l * leaf : (l + 1) * leaf]
 
 
-def plan_kernel(
-    chips,
-    sources_ref,
-    ranks_ref,
-    targets_ref,
-    right_ref,
-    left_ref,
-    pick_ref,
-    depth_ref,
-    goal_ref,
-):
-    tasks = sources_ref.shape[0]
-    rows = depth_ref.shape[0]
+def plan_kernel(chips, tasks, index_ref, left_ref, pick_ref, held_ref, sem):
+    copy = pltpu.make_async_copy(left_ref, held_ref, sem)
+    copy.start()
+    rows = pick_ref.shape[0] // 2
     row = iota((rows, LANES), 0)
-    row_task = row // TILE * GROUP + row % GROUP
+    lane = iota((rows, LANES), 1)
     row_part = row // GROUP % 2
-    source = chosen(row_task, [sources_ref[t] for t in range(tasks)], -1)
-    depth_ref[...] = chosen(row_task, [ranks_ref[t] for t in range(tasks)], 0)
+    own = lane == row // TILE * GROUP + row % GROUP
+    index = index_ref[...].astype(jnp.float32)
+
+    def by_row(at):
+        return jnp.sum(jnp.where(own, index[at : at + 1], 0.0), 1, keepdims=True)
+
+    source = by_row(0).astype(jnp.int32)
     same = source * 2 + row_part
     other = source * 2 + 1 - row_part
     sign = jnp.where(row_part == 0, -1.0, 1.0)
-    for chunk in range(pick_ref.shape[1] // LANES):
+    chunks = pick_ref.shape[1] // LANES - 1
+    for chunk in range(chunks):
         codes = leaf_codes(chunk, chips)
         lanes = slice(chunk * LANES, (chunk + 1) * LANES)
         pick_ref[:rows, lanes] = jnp.where(same == codes, 1.0, 0.0).astype(jnp.bfloat16)
         pick_ref[rows:, lanes] = jnp.where(other == codes, sign, 0.0).astype(jnp.bfloat16)
-    lane = iota((rows, LANES), 1) % rows
-    lane_task = lane // TILE * GROUP + lane % GROUP
-    target = chosen(lane_task, [targets_ref[t] for t in range(tasks)], -1)
+    extra = slice(chunks * LANES, (chunks + 1) * LANES)
+    pick_ref[:rows, extra] = jnp.broadcast_to(by_row(1), (rows, LANES)).astype(jnp.bfloat16)
+    target = jnp.sum(jnp.where(row == lane % rows, by_row(2), 0.0), 0, keepdims=True)
+    target = target.astype(jnp.int32)
     spare = tasks // GROUP * TILE + tasks % GROUP
-    goal_ref[...] = jnp.where(
-        row == spare, target >> 3, jnp.where(row == spare + 1, target & 7, 0)
-    ).astype(jnp.float32)
-
-
-def far_kernel(tasks, pick_ref, depth_ref, goal_ref, gathered_ref, right_ref, left_ref, out_ref):
-    picked = dot(pick_ref[...], gathered_ref[...]).astype(jnp.bfloat16)
+    goal = jnp.where(row == spare, target >> 3, jnp.where(row == spare + 1, target & 7, 0))
+    pick_ref[rows:, extra] = goal.astype(jnp.float32).astype(jnp.bfloat16)
+    copy.wait()
+
+
+def far_kernel(tasks, pick_ref, gathered_ref, right_ref, left_ref, out_ref):
+    columns = gathered_ref.shape[0]
+    picked = dot(pick_ref[:, :columns], gathered_ref[...]).astype(jnp.bfloat16)
+    extra = pick_ref[:, columns:].astype(jnp.float32)
     half = picked.shape[0] // 2
     pair = jnp.concatenate([picked[:half], picked[half:]], 1)
     leaf = left_ref.shape[-1]
     own = iota((TILE, leaf), 0) % GROUP
-    lane = iota((TILE, leaf), 1)
+    lane = iota((TILE, leaf), 1).astype(jnp.float32)
     for start in range(0, tasks, GROUP):
         rows = slice(2 * start, 2 * start + TILE)
         here = range(start, min(start + GROUP, tasks))
         coeff = jnp.zeros((TILE, leaf), jnp.float32)
         for t in here:
             coeff = jnp.where(own == t - start, dot(pair[rows], right_ref[t]), coeff)
-        coeff = jnp.where(lane < depth_ref[rows, :], coeff, 0.0).astype(jnp.bfloat16)
+        coeff = jnp.where(lane < extra[rows], coeff, 0.0).astype(jnp.bfloat16)
         direct = jnp.zeros((TILE, leaf), jnp.float32)
         crossed = jnp.zeros((TILE, leaf), jnp.float32)
         for t in here:
             both = dot(coeff, left_ref[t], True)
             direct = jnp.where(own == t - start, both[:, :leaf], direct)
             crossed = jnp.where(own == t - start, both[:, leaf:], crossed)
-        terms = turn(direct, crossed) + goal_ref[rows, :]
+        goal = extra[half + 2 * start : half + 2 * start + TILE]
+        terms = turn(direct, crossed) + goal
         out_ref[rows, :] = terms.astype(jnp.bfloat16)
 
 
@@ -148,7 +149,11 @@
     row = iota((TILE, columns), 0)
     base = (lax.axis_index("core") * GROUP + row % GROUP) * 2 + row // GROUP
     place = jnp.concatenate(
-        [jnp.where(code - chip * (CORES * TILE) == base, 1.0, 0.0) for chip in range(chips)], 0
+        [
+            jnp.where(code - chip * (CORES * TILE) == base, 1.0, 0.0)
+            for chip in rotated(chips, first_chip(chips))
+        ],
+        0,
     )
     out_ref[...] = dot(place.astype(jnp.bfloat16), terms).astype(jnp.bfloat16)
 
@@ -181,13 +186,16 @@
     out_ref[...] = turn(direct, crossed)
 
 
-def call(kernel, outs, spaces, scratch=()):
+def call(kernel, outs, spaces, scratch=(), hide=2):
     return pl.pallas_call(
         kernel,
         out_shape=[jax.ShapeDtypeStruct(shape, dtype) for shape, dtype in outs],
         in_specs=[pl.BlockSpec(memory_space=space) for space in spaces],
         out_specs=[pl.BlockSpec(memory_space=pltpu.VMEM) for _ in outs],
         scratch_shapes=scratch,
+        cost_estimate=pl.CostEstimate(
+            flops=0, transcendentals=0, bytes_accessed=hide * 1024 * 1024
+        ),
         compiler_params=pltpu.CompilerParams(vmem_limit_bytes=LIMIT),
     )
 
@@ -223,32 +231,32 @@
     spectrum = jnp.sum(shares, 0).astype(jnp.bfloat16)
     copies = jnp.broadcast_to(spectrum[None], (chips,) + spectrum.shape)
     same_core = lax.all_to_all(
-        copies, "chip", 0, 0, axis_index_groups=[rotated(chips, last(chips))], tiled=True
+        copies, "chip", 0, 0, axis_index_groups=[rotated(chips, first_chip(chips))], tiled=True
     )
     gathered = lax.all_gather(same_core, "core", axis=0, tiled=False)
     gathered = gathered.reshape(CORES * chips * TILE, leaf)
 
-    right = far_right[0].reshape(tasks, 2 * leaf, leaf)
+    index = jnp.stack([far_sources, far_ranks[0], far_targets])
+    index = jnp.pad(index, ((0, GROUP - index.shape[0]), (0, LANES - tasks)), constant_values=-1)
     left = far_left[0].reshape(tasks, 2 * leaf, leaf)
-    pick, depth, goal = call(
-        functools.partial(plan_kernel, chips),
+    pick, left = call(
+        functools.partial(plan_kernel, chips, tasks),
         [
-            ((4 * slots, gathered.shape[0]), jnp.bfloat16),
-            ((2 * slots, leaf), jnp.int32),
-            ((2 * slots, leaf), jnp.float32),
+            ((4 * slots, gathered.shape[0] + LANES), jnp.bfloat16),
+            (left.shape, left.dtype),
         ],
-        [smem, smem, smem, vmem, vmem],
-    )(far_sources, far_ranks[0], far_targets, right, left)
+        [vmem, pl.ANY],
+        [pltpu.SemaphoreType.DMA],
+        hide=8,
+    )(index, left)
     (terms,) = call(
         functools.partial(far_kernel, tasks),
         [((2 * slots, leaf), jnp.bfloat16)],
-        [vmem] * 6,
+        [vmem] * 4,
     )(
         pick,
-        depth,
-        goal,
         gathered,
-        right,
+        far_right[0].reshape(tasks, 2 * leaf, leaf),
         left,
     )
 
@@ -258,7 +266,14 @@
         [((chips * TILE, leaf), jnp.bfloat16)],
         [vmem],
     )(both_terms)
-    arrived = lax.all_to_all(spread.reshape(chips, TILE, leaf), "chip", 0, 0, tiled=True)
+    arrived = lax.all_to_all(
+        spread.reshape(chips, TILE, leaf),
+        "chip",
+        0,
+        0,
+        axis_index_groups=[rotated(chips, first_chip(chips))],
+        tiled=True,
+    )
 
     (near_field,) = call(
         functools.partial(near_kernel, chips),

time: 59.7 us -> 56.2 us (0.941); the launches traced: 58.8 us -> 55.9 us
  local copies, waits for them, and re-layouts: 8.57 us -> 4.14 us
  starting transfers between devices: 21.1 us -> 24.6 us
  waiting for transfers between devices: 8.21 us -> 6.08 us
  other arithmetic: 0.05 us -> 0.75 us
    unnamed x23 -> x9, local copies, waits for them, and re-layouts: 7.28 us -> 2.87 us
    all_to_all x2, starting transfers between devices: 21.1 us -> 24.6 us  [the longest x1 15.7 us: per_device(): lax.all_to_all(copies, 'chip', 0, 0, axis_index_groups=[rotated(chips, fi...]
    all_to_all x2, waiting for transfers between devices: 8.21 us -> 6.08 us  [the longest x1 3.27 us: per_device(): lax.all_to_all(spread.reshape(chips, TILE, leaf), 'chip', 0, 0, axis_inde...]
    another operation x0 -> x1, other arithmetic: none -> 0.7 us  [per_device(): index = jnp.stack([far_sources, far_ranks[0], far_targets])]
  transfers between devices with their start and end apart: 2 -> 2, of which waited for: 2 -> 2; matrix products, arithmetic and copies ran while one was open for 1% -> 3% of each run, Pallas kernels for 3% -> 3%
where the time goes in v6:
time: 56.2 us; the launch traced here: 55.9 us
  starting transfers between devices  24.6 us (44%)
  blocking collectives  16.9 us (30%)
  waiting for transfers between devices  6.08 us (11%)
  local copies, waits for them, and re-layouts  4.14 us (7%)
  Pallas kernels  3.33 us (6%)
  other arithmetic  0.75 us (1%)
    all_to_all x1, starting transfers between devices, per_device(): lax.all_to_all(copies, 'chip', 0, 0, axis_index_groups=[rotated(chips, fi...  15.7 us
    all_to_all x1, blocking collectives, per_device(): lax.all_to_all(partial.reshape(total_freq, TILE, leaf), 'freq', 0, 0, axi...  10.9 us
    all_to_all x1, starting transfers between devices, per_device(): lax.all_to_all(spread.reshape(chips, TILE, leaf), 'chip', 0, 0, axis_inde...  8.92 us
    all_gather x1, blocking collectives, per_device(): gathered = lax.all_gather(same_core, 'core', axis=0, tiled=False)  4.15 us
    all_to_all x1, waiting for transfers between devices, per_device(): lax.all_to_all(spread.reshape(chips, TILE, leaf), 'chip', 0, 0, axis_inde...  3.27 us
    unnamed x9, local copies, waits for them, and re-layouts  2.87 us
    all_to_all x1, waiting for transfers between devices, per_device(): lax.all_to_all(copies, 'chip', 0, 0, axis_index_groups=[rotated(chips, fi...  2.82 us
    all_gather x1, blocking collectives, per_device(): both_terms = lax.all_gather(terms, 'core', axis=0, tiled=True)  1.87 us
  transfers between devices with their start and end apart: 2, of which 2 were waited for; matrix products, arithmetic and copies ran while one was open for 3% of the time, Pallas kernels for 3%

profile of v6, /device:TPU:1, one launch (start us, length us, event | category | flops | bytes accessed | tf_op | source)
XLA Modules:
  0.0 55.9 jit_solution(4790536241399579574)
XLA Ops:
  0.0 0.0 copy-start.2
  0.0 0.0 copy-start.3
  0.0 1.0 %copy-done.3 = bf16[64,1024]{1,0:T(8,128)(2,1)S(1)} copy-done((bf16[64,1024]{1,0:T(8,128)(2,1)S(1)}, bf16[64,1024]{1,0:T(8,128)(2,1)}, u32[]{:S(2)}) %copy-start.3) | copy-done | bytes 131096
  1.0 0.3 shard_map.82
  1.3 10.9 %all_to_all.15 = f32[8,16,128]{2,1,0:T(8,128)S(1)} all-to-all(f32[8,16,128]{2,1,0:T(8,128)S(1)} %bitcast.13), channel_id=1, replica_groups={{256,320,384,448,0,64,128,192},{257,321,385,449,1,65,129,193},{258,322,..., dimensions={0} | all-to-all | bytes 131072 | tf_op jit(solution)/shard_map/all_to_all | solution.py:223
  12.2 0.7 %broadcast_in_dim.2 = bf16[32,16,128]{2,1,0:T(8,128)(2,1)} broadcast(bf16[16,128]{1,0:T(8,128)(2,1)S(1)} %reduce_sum.18), dimensions={1,2} | broadcast | bytes 135168 | tf_op jit(solution)/shard_map/broadcast_in_dim | solution.py:232
  12.9 15.7 %all-to-all-start.1 = ((bf16[32,16,128]{2,1,0:T(8,128)(2,1)}), bf16[32,16,128]{2,1,0:T(8,128)(2,1)}, u32[]{:S(2)}, u32[]{:S(2)}) async-start(bf16[32,16,128]{2,1,0:T(8,128)(2,1)} %broadcast_in_dim.2), calls=%async_computation.1 | async-start | bytes 262144 | tf_op jit(solution)/shard_map/all_to_all | solution.py:233
  28.6 0.7 %pad_add_fusion = s32[3,12]{1,0:T(4,128)S(1)} fusion(s32[1,12]{1,0:T(1,128)} %bitcast.14, s32[1,12]{1,0:T(1,128)} %param.13, s32[1,12]{1,0:T(1,128)} %bitcast.15), kind=kLoop, calls=%fused_computation.2 | loop fusion | flops 72 | bytes 288 | tf_op jit(solution)/shard_map/stack | solution.py:239
  29.3 0.0 copy-start.1
  29.3 1.1 %copy-done.1 = bf16[1,12,2,128,128]{4,3,2,1,0:T(8,128)(2,1)S(1)} copy-done((bf16[1,12,2,128,128]{4,3,2,1,0:T(8,128)(2,1)S(1)}, bf16[1,12,2,128,128]{4,3,2,1,0:T(8,128)(2,1)}, u32[]{:S(2)}) %copy-start.1) | copy-done | bytes 786456
  30.4 0.2 shard_map.84
  30.6 0.0 copy-start
  30.6 2.8 %all-to-all-done.1 = bf16[32,16,128]{2,1,0:T(8,128)(2,1)} async-done(((bf16[32,16,128]{2,1,0:T(8,128)(2,1)}), bf16[32,16,128]{2,1,0:T(8,128)(2,1)}, u32[]{:S(2)}, u32[]{:S(2)}) %all-to-all-start.1) | async-done | bytes 131104 | tf_op jit(solution)/shard_map/all_to_all | solution.py:233
  33.4 4.1 %all-gather = bf16[64,16,128]{2,1,0:T(8,128)(2,1)S(1)} all-gather(bf16[32,16,128]{2,1,0:T(8,128)(2,1)} %all-to-all-done.1), channel_id=2, replica_groups=mesh['freq'=8,'chip'=32,'core'=2] {'core'}, dimensions={0}, use_global_device_ids=true | all-gather | bytes 393216 | tf_op jit(solution)/shard_map/all_gather | solution.py:236
  37.6 0.0 copy-done.2
  37.6 0.7 %shard_map.85 = bf16[32,128]{1,0:T(8,128)(2,1)S(1)} custom-call(bf16[64,1152]{1,0:T(8,128)(2,1)S(1)} %get-tuple-element.7.pick_ref, bf16[1024,128]{1,0:T(8,128)(2,1)S(1)} %bitcast.8, bf16[12,256,128]{2,1,0:T(8,128)(2,1)S(1)} %bitcast.12, bf16[12,256,128]{2,1,0:T(8,128)(2,1)S(1)} %get-tuple-element.8.left_ref), custom_call_target="tpu_custom_call" | custom-call | bytes 2097152 | tf_op jit(solution)/shard_map/pallas_call | solution.py:252
  38.3 1.9 %all_gather.11.terms_ref = bf16[64,128]{1,0:T(8,128)(2,1)S(1)} all-gather(bf16[32,128]{1,0:T(8,128)(2,1)S(1)} %shard_map.85), channel_id=1, replica_groups=mesh['freq'=8,'chip'=32,'core'=2] {'core'}, dimensions={0}, use_global_device_ids=true | all-gather | bytes 24576 | tf_op jit(solution)/shard_map/all_gather | solution.py:263
  40.2 0.8 %shard_map.86 = bf16[512,128]{1,0:T(8,128)(2,1)} custom-call(bf16[64,128]{1,0:T(8,128)(2,1)S(1)} %all_gather.11.terms_ref), custom_call_target="tpu_custom_call" | custom-call | bytes 2097152 | tf_op jit(solution)/shard_map/pallas_call | solution.py:264
  41.0 8.9 %all-to-all-start.2 = ((bf16[32,16,128]{2,1,0:T(8,128)(2,1)}), bf16[32,16,128]{2,1,0:T(8,128)(2,1)S(1)}, u32[]{:S(2)}, u32[]{:S(2)}) async-start(bf16[32,16,128]{2,1,0:T(8,128)(2,1)} %bitcast.7), calls=%async_computation.2 | async-start | bytes 262144 | tf_op jit(solution)/shard_map/all_to_all | solution.py:269
  49.9 0.8 %copy.10.leaves_ref = s32[8,3]{1,0:T(8,128)S(1)} copy(s32[8,3]{0,1:T(4,128)} %param.10) | data formatting | bytes 192 | tf_op args[2]
  50.7 0.0 copy-done
  50.7 1.3 %shard_map.83 = f32[16,128]{1,0:T(8,128)S(1)} custom-call(s32[8,3]{1,0:T(8,128)S(1)} %copy.10.leaves_ref, bf16[1024,128]{1,0:T(8,128)(2,1)S(1)} %bitcast.9, bf16[8,3,256,128]{3,2,1,0:T(8,128)(2,1)S(1)} %bitcast.10), custom_call_target="tpu_custom_call" | custom-call | bytes 2097152 | tf_op jit(solution)/shard_map/pallas_call | solution.py:278
  52.0 3.3 %all-to-all-done.2 = bf16[32,16,128]{2,1,0:T(8,128)(2,1)S(1)} async-done(((bf16[32,16,128]{2,1,0:T(8,128)(2,1)}), bf16[32,16,128]{2,1,0:T(8,128)(2,1)S(1)}, u32[]{:S(2)}, u32[]{:S(2)}) %all-to-all-start.2) | async-done | bytes 131104 | tf_op jit(solution)/shard_map/all_to_all | solution.py:269
  55.3 0.6 %convert_element_type.27 = bf16[1,2,1024]{2,1,0:T(2,128)(2,1)} reshape(bf16[16,128]{1,0:T(8,128)(2,1)S(1)} %add_convert_fusion) | data formatting | bytes 8192 | tf_op jit(solution)/shard_map/convert_element_type | solution.py:285
  (4 shorter events, 0.1 us)
Async XLA Ops:
  0.0 37.6 %copy-start.2 = (bf16[1,12,2,128,128]{4,3,2,1,0:T(8,128)(2,1)S(1)}, bf16[1,12,2,128,128]{4,3,2,1,0:T(8,128)(2,1)}, u32[]{:S(2)}) copy-start(bf16[1,12,2,128,128]{4,3,2,1,0:T(8,128)(2,1)} %param.12) | copy-start | bytes 2359300
  0.0 1.0 %copy-start.3 = (bf16[64,1024]{1,0:T(8,128)(2,1)S(1)}, bf16[64,1024]{1,0:T(8,128)(2,1)}, u32[]{:S(2)}) copy-start(bf16[64,1024]{1,0:T(8,128)(2,1)} %history_ref.1) | copy-start | bytes 393220
  12.9 20.5 %all-to-all-start.1 = ((bf16[32,16,128]{2,1,0:T(8,128)(2,1)}), bf16[32,16,128]{2,1,0:T(8,128)(2,1)}, u32[]{:S(2)}, u32[]{:S(2)}) async-start(bf16[32,16,128]{2,1,0:T(8,128)(2,1)} %broadcast_in_dim.2), calls=%async_computation.1 | async-start | bytes 262144 | tf_op jit(solution)/shard_map/all_to_all | solution.py:233
  29.3 1.1 %copy-start.1 = (bf16[1,12,2,128,128]{4,3,2,1,0:T(8,128)(2,1)S(1)}, bf16[1,12,2,128,128]{4,3,2,1,0:T(8,128)(2,1)}, u32[]{:S(2)}) copy-start(bf16[1,12,2,128,128]{4,3,2,1,0:T(8,128)(2,1)} %param.11) | copy-start | bytes 2359300
  30.6 20.1 %copy-start = (bf16[1,8,3,2,128,128]{5,4,3,2,1,0:T(8,128)(2,1)S(1)}, bf16[1,8,3,2,128,128]{5,4,3,2,1,0:T(8,128)(2,1)}, u32[]{:S(2)}) copy-start(bf16[1,8,3,2,128,128]{5,4,3,2,1,0:T(8,128)(2,1)} %param.9) | copy-start | bytes 4718596
  41.0 14.2 %all-to-all-start.2 = ((bf16[32,16,128]{2,1,0:T(8,128)(2,1)}), bf16[32,16,128]{2,1,0:T(8,128)(2,1)S(1)}, u32[]{:S(2)}, u32[]{:S(2)}) async-start(bf16[32,16,128]{2,1,0:T(8,128)(2,1)} %bitcast.7), calls=%async_computation.2 | async-start | bytes 262144 | tf_op jit(solution)/shard_map/all_to_all | solution.py:269

commit v7 on v6

v7 whole, which is shorter than its diff:
```python
import functools
import math

import jax
import jax.numpy as jnp
from jax import lax
from jax.experimental import pallas as pl
from jax.experimental.pallas import tpu as pltpu
from jax.sharding import Mesh
from jax.sharding import PartitionSpec as P

fall_total = 0.25
CORES = 2
GROUP = 8
TILE = 2 * GROUP
LANES = 128


def rotated(size, first):
    return [(i + first) % size for i in range(size)]


def first_chip(chips):
    return chips * 3 // 4 + 2


def dot(first_op, second_op, transposed=False):
    dims = (((1,), (1 if transposed else 0,)), ((), ()))
    return lax.dot_general(first_op, second_op, dims, preferred_element_type=jnp.float32)


def iota(shape, dim):
    return lax.broadcasted_iota(jnp.int32, shape, dim)


def turn(direct, crossed):
    swapped = jnp.concatenate([-crossed[GROUP:], crossed[:GROUP]], 0)
    return direct + swapped


def chosen(where_at, values, fill):
    out = jnp.full(where_at.shape, fill, jnp.int32)
    for i, value in enumerate(values):
        out = jnp.where(where_at == i, value, out)
    return out


def leaf_codes(chunk, chips):
    at = chunk * LANES + iota((1, LANES), 1)
    core = at // (chips * TILE)
    chip = (at // TILE + first_chip(chips)) % chips
    return (chip * CORES + core) * TILE + at % GROUP * 2 + at // GROUP % 2


def plan(chips, pick_ref, sources_ref, ranks_ref, targets_ref, leaves_ref):
    tasks = sources_ref.shape[1]
    near, leaves = leaves_ref.shape
    rows = 2 * (-(-tasks // GROUP) * GROUP)
    row = iota((rows, LANES), 0)
    lane = iota((rows, LANES), 1)
    task = row // TILE * GROUP + row % GROUP
    part = row // GROUP % 2

    def by_row(ref):
        value = ref[...].astype(jnp.float32)
        found = jnp.where(iota((rows, tasks), 1) == task[:, :tasks], value, 0.0)
        return jnp.where(task < tasks, jnp.sum(found, 1, keepdims=True), -1.0)

    source = by_row(sources_ref).astype(jnp.int32)
    wanted = leaves_ref[...].astype(jnp.float32)
    own = iota((TILE, leaves), 1) == iota((TILE, leaves), 0) % GROUP
    listed = [
        jnp.sum(jnp.where(own, wanted[n : n + 1], 0.0), 1, keepdims=True) for n in range(near)
    ]
    near_part = iota((TILE, LANES), 0) // GROUP
    near_codes = [leaf.astype(jnp.int32) * 2 + near_part for leaf in listed]
    direct = source * 2 + part
    turned = source * 2 + 1 - part
    sign = jnp.where(part == 0, -1.0, 1.0)
    chunks = pick_ref.shape[1] // LANES - 1
    for chunk in range(chunks):
        codes = leaf_codes(chunk, chips)
        lanes = slice(chunk * LANES, (chunk + 1) * LANES)
        pick_ref[:rows, lanes] = jnp.where(direct == codes, 1.0, 0.0).astype(jnp.bfloat16)
        pick_ref[rows : 2 * rows, lanes] = jnp.where(turned == codes, sign, 0.0).astype(
            jnp.bfloat16
        )
        for n in range(near):
            pick_ref[2 * rows + n * TILE : 2 * rows + (n + 1) * TILE, lanes] = jnp.where(
                near_codes[n] == codes, 1.0, 0.0
            ).astype(jnp.bfloat16)
    extra = slice(chunks * LANES, (chunks + 1) * LANES)
    pick_ref[:rows, extra] = by_row(ranks_ref).astype(jnp.bfloat16)
    target = jnp.sum(jnp.where(row == lane % rows, by_row(targets_ref), 0.0), 0, keepdims=True)
    target = target.astype(jnp.int32)
    spare = tasks // GROUP * TILE + tasks % GROUP
    goal = jnp.where(row == spare, target >> 3, jnp.where(row == spare + 1, target & 7, 0))
    pick_ref[rows : 2 * rows, extra] = goal.astype(jnp.float32).astype(jnp.bfloat16)
    pick_ref[2 * rows :, extra] = jnp.zeros((near * TILE, LANES), jnp.bfloat16)


def partial_kernel(total_freq, total_steps, chips, *refs):
    count = (len(refs) - 3) // 2
    out_ref, pick_ref = refs[count : count + 2]
    history_ref, *index_refs = refs[count + 2 : -1]
    copies = [
        pltpu.make_async_copy(refs[i], refs[count + 2 + i], refs[-1].at[i]) for i in range(count)
    ]
    for copy in copies:
        copy.start()
    steps = history_ref.shape[0]
    rows = 2 * total_freq
    leaf = out_ref.shape[-1]
    leaves = history_ref.shape[1] // leaf
    row = iota((rows, steps), 0)
    step = lax.axis_index("freq") * steps + iota((rows, steps), 1)
    freq = ((row >> 1) + total_freq // 2) % total_freq * (total_steps // total_freq) + 1
    phase = (freq * step + (row & 1) * (total_steps // 4)) & (total_steps - 1)
    angle = 2.0 * math.pi / total_steps * phase.astype(jnp.float32)
    damping = jnp.exp(step.astype(jnp.float32) * (math.log(fall_total) / total_steps))
    weights = (damping * jnp.cos(angle) / math.sqrt(total_steps)).astype(jnp.bfloat16)
    for copy in copies:
        copy.wait()
    part = dot(weights, history_ref[...])
    for l in range(leaves):
        out_ref[pl.ds(l, rows, stride=leaves), :] = part[:, l * leaf : (l + 1) * leaf]
    plan(chips, pick_ref, *index_refs)


def block_kernel(tasks, pick_ref, gathered_ref, right_ref, left_ref, blocks_ref, out_ref, near_ref):
    columns = gathered_ref.shape[0]
    picked = dot(pick_ref[:, :columns], gathered_ref[...]).astype(jnp.bfloat16)
    half = out_ref.shape[0]
    extra = pick_ref[: 2 * half, columns:].astype(jnp.float32)
    pair = jnp.concatenate([picked[:half], picked[half : 2 * half]], 1)
    leaf = left_ref.shape[-1]
    own = iota((TILE, leaf), 0) % GROUP
    lane = iota((TILE, leaf), 1).astype(jnp.float32)
    coeffs = []
    for start in range(0, tasks, GROUP):
        rows = slice(2 * start, 2 * start + TILE)
        coeff = jnp.zeros((TILE, leaf), jnp.float32)
        for t in range(start, min(start + GROUP, tasks)):
            coeff = jnp.where(own == t - start, dot(pair[rows], right_ref[t]), coeff)
        coeffs.append(jnp.where(lane < extra[rows], coeff, 0.0).astype(jnp.bfloat16))
    for start, coeff in zip(range(0, tasks, GROUP), coeffs):
        rows = slice(2 * start, 2 * start + TILE)
        direct = jnp.zeros((TILE, leaf), jnp.float32)
        crossed = jnp.zeros((TILE, leaf), jnp.float32)
        for t in range(start, min(start + GROUP, tasks)):
            both = dot(coeff, left_ref[t], True)
            direct = jnp.where(own == t - start, both[:, :leaf], direct)
            crossed = jnp.where(own == t - start, both[:, leaf:], crossed)
        goal = extra[half + 2 * start : half + 2 * start + TILE]
        terms = turn(direct, crossed) + goal
        out_ref[rows, :] = terms.astype(jnp.bfloat16)
    leaves, near = blocks_ref.shape[:2]
    direct = jnp.zeros((TILE, leaf), jnp.float32)
    crossed = jnp.zeros((TILE, leaf), jnp.float32)
    for n in range(near):
        view = picked[2 * half + TILE * n : 2 * half + TILE * (n + 1)]
        for l in range(leaves):
            both = dot(view, blocks_ref[l, n], True)
            direct = direct + jnp.where(own == l, both[:, :leaf], 0.0)
            crossed = crossed + jnp.where(own == l, both[:, leaf:], 0.0)
    near_ref[...] = turn(direct, crossed)


def spectrum_kernel(shares_ref, out_ref):
    spectrum = jnp.sum(shares_ref[...], 0).astype(jnp.bfloat16)
    for chip in range(out_ref.shape[0]):
        out_ref[chip] = spectrum


def scatter_kernel(tasks, chips, terms_ref, out_ref):
    terms = terms_ref[...]
    columns = terms.shape[0]
    rows = columns // CORES
    spare = tasks // GROUP * TILE + tasks % GROUP
    lane = iota((1, terms.shape[1]), 1)
    wide = terms.astype(jnp.float32)

    def along(at):
        return jnp.where(lane < rows, wide[at : at + 1], wide[rows + at : rows + at + 1])

    goal = (along(spare) * GROUP + along(spare + 1)).astype(jnp.int32)
    code = (goal * 2 + lane // GROUP % 2)[:, :columns]
    row = iota((TILE, columns), 0)
    base = (lax.axis_index("core") * GROUP + row % GROUP) * 2 + row // GROUP
    place = jnp.concatenate(
        [
            jnp.where(code - chip * (CORES * TILE) == base, 1.0, 0.0)
            for chip in rotated(chips, first_chip(chips))
        ],
        0,
    )
    out_ref[...] = dot(place.astype(jnp.bfloat16), terms).astype(jnp.bfloat16)


def call(kernel, outs, spaces, scratch=(), limit=16, flops=0):
    return pl.pallas_call(
        kernel,
        out_shape=[jax.ShapeDtypeStruct(shape, dtype) for shape, dtype in outs],
        in_specs=[pl.BlockSpec(memory_space=space) for space in spaces],
        out_specs=[pl.BlockSpec(memory_space=pltpu.VMEM) for _ in outs],
        scratch_shapes=scratch,
        cost_estimate=pl.CostEstimate(flops=flops, transcendentals=0, bytes_accessed=2**20),
        compiler_params=pltpu.CompilerParams(vmem_limit_bytes=limit * 2**20),
    )


def per_device(
    history, near_blocks, near_leaves, far_left, far_right, far_ranks, far_targets, far_sources
):
    vmem = pltpu.VMEM
    freq_groups = lax.axis_size("freq")
    chips = lax.axis_size("chip")
    total_freq = far_ranks.shape[0] * freq_groups
    total_steps = history.shape[0] * freq_groups
    leaf = near_blocks.shape[-1]
    leaves = near_blocks.shape[1]
    near = near_blocks.shape[2]
    tasks = far_ranks.shape[1]
    slots = -(-tasks // GROUP) * GROUP

    arrays = (
        history,
        far_sources.reshape(1, tasks),
        far_ranks,
        far_targets.reshape(1, tasks),
        near_leaves.T,
    )
    partial, pick = call(
        functools.partial(partial_kernel, total_freq, total_steps, chips),
        [
            ((total_freq * TILE, leaf), jnp.float32),
            ((4 * slots + near * TILE, CORES * chips * TILE + LANES), jnp.bfloat16),
        ],
        [pl.ANY] * len(arrays),
        [
            *[pltpu.VMEM(array.shape, array.dtype) for array in arrays],
            pltpu.SemaphoreType.DMA((len(arrays),)),
        ],
        limit=60,
    )(*arrays)
    shares = lax.all_to_all(
        partial.reshape(total_freq, TILE, leaf),
        "freq",
        0,
        0,
        axis_index_groups=[rotated(freq_groups, freq_groups // 2)],
        tiled=True,
    )
    (copies,) = call(
        spectrum_kernel, [((chips, TILE, leaf), jnp.bfloat16)], [vmem], flops=20_000_000_000
    )(shares)
    same_core = lax.all_to_all(
        copies, "chip", 0, 0, axis_index_groups=[rotated(chips, first_chip(chips))], tiled=True
    )
    gathered = lax.all_gather(same_core, "core", axis=0, tiled=False)
    gathered = gathered.reshape(CORES * chips * TILE, leaf)

    terms, near_field = call(
        functools.partial(block_kernel, tasks),
        [((2 * slots, leaf), jnp.bfloat16), ((TILE, leaf), jnp.float32)],
        [vmem] * 5,
    )(
        pick,
        gathered,
        far_right[0].reshape(tasks, 2 * leaf, leaf),
        far_left[0].reshape(tasks, 2 * leaf, leaf),
        near_blocks[0].reshape(leaves, near, 2 * leaf, leaf),
    )

    both_terms = lax.all_gather(terms, "core", axis=0, tiled=True)
    (spread,) = call(
        functools.partial(scatter_kernel, tasks, chips),
        [((chips * TILE, leaf), jnp.bfloat16)],
        [vmem],
    )(both_terms)
    arrived = lax.all_to_all(
        spread.reshape(chips, TILE, leaf),
        "chip",
        0,
        0,
        axis_index_groups=[rotated(chips, first_chip(chips))],
        tiled=True,
    )

    field = near_field + jnp.sum(arrived.astype(jnp.float32), 0)
    return field.reshape(1, 2, leaves * leaf).astype(jnp.bfloat16)


def solution(mesh):
    freq_groups, elem_groups = mesh.devices.shape
    split = Mesh(
        mesh.devices.reshape(freq_groups, elem_groups // CORES, CORES), ("freq", "chip", "core")
    )
    elem = ("chip", "core")
    in_specs = (
        P("freq", elem),
        P("freq", elem, None, None, None, None),
        P(elem, None),
        P("freq", elem, None, None, None),
        P("freq", elem, None, None, None),
        P("freq", elem),
        P(elem),
        P(elem),
    )
    out_specs = P("freq", None, elem)
    return jax.shard_map(
        per_device, mesh=split, in_specs=in_specs, out_specs=out_specs, check_vma=False
    )
```

time: 56.2 us -> 54.8 us (0.975)
  blocking collectives: 16.9 us -> 50.7 us
  starting transfers between devices: 24.6 us -> 0 us
  waiting for transfers between devices: 6.08 us -> 0 us
  local copies, waits for them, and re-layouts: 4.14 us -> 0.62 us
  other arithmetic: 0.75 us -> 0.04 us
    all_to_all x0 -> x2, blocking collectives: none -> 32.9 us  [the longest x1 19.6 us: per_device(): lax.all_to_all(copies, 'chip', 0, 0, axis_index_groups=[rotated(chips, fi...]
    all_to_all x2 -> x0, starting transfers between devices: 24.6 us -> none  [the longest x1 15.7 us: per_device(): lax.all_to_all(copies, 'chip', 0, 0, axis_index_groups=[rotated(chips, fi...]
    all_to_all x2 -> x0, waiting for transfers between devices: 6.08 us -> none  [the longest x1 3.27 us: per_device(): lax.all_to_all(spread.reshape(chips, TILE, leaf), 'chip', 0, 0, axis_inde...]
    unnamed x9 -> x8, local copies, waits for them, and re-layouts: 2.87 us -> 0.01 us
    all_to_all x1, blocking collectives: 10.9 us -> 11.8 us  [per_device(): lax.all_to_all(partial.reshape(total_freq, TILE, leaf), 'freq', 0, 0, axi...]
    another operation x1 -> x0, other arithmetic: 0.7 us -> none  [per_device(): index = jnp.stack([far_sources, far_ranks[0], far_targets])]
    broadcast_in_dim x1 -> x0, local copies, waits for them, and re-layouts: 0.65 us -> none  [per_device(): copies = jnp.broadcast_to(spectrum[None], (chips,) + spectrum.shape)]
    pallas_call x1, Pallas kernels: 0.82 us -> 0.17 us  [per_device(): call(functools.partial(scatter_kernel, tasks, chips), [((chips * TILE, le...]
  transfers between devices with their start and end apart: 2 -> 0, of which waited for: 2 -> 0; matrix products, arithmetic and copies ran while one was open for 3% -> 0% of each run, Pallas kernels for 3% -> 0%
where the time goes in v7:
time: 54.8 us; the launch traced here: 54.5 us
  blocking collectives  50.7 us (93%)
  Pallas kernels  3.04 us (6%)
  local copies, waits for them, and re-layouts  0.62 us (1%)
    all_to_all x1, blocking collectives, per_device(): lax.all_to_all(copies, 'chip', 0, 0, axis_index_groups=[rotated(chips, fi...  19.6 us
    all_to_all x1, blocking collectives, per_device(): lax.all_to_all(spread.reshape(chips, TILE, leaf), 'chip', 0, 0, axis_inde...  13.3 us
    all_to_all x1, blocking collectives, per_device(): lax.all_to_all(partial.reshape(total_freq, TILE, leaf), 'freq', 0, 0, axi...  11.8 us
    all_gather x1, blocking collectives, per_device(): gathered = lax.all_gather(same_core, 'core', axis=0, tiled=False)  4.18 us
    all_gather x1, blocking collectives, per_device(): both_terms = lax.all_gather(terms, 'core', axis=0, tiled=True)  1.86 us
    pallas_call x1, Pallas kernels, per_device(): call(functools.partial(partial_kernel, total_freq, total_steps, chips), [...  1.8 us

profile of v7, /device:TPU:1, one launch (start us, length us, event | category | flops | bytes accessed | tf_op | source)
XLA Modules:
  0.0 54.5 jit_solution(3625245685068678)
XLA Ops:
  0.0 1.8 %shard_map.82 = (f32[128,128]{1,0:T(8,128)}, bf16[112,1152]{1,0:T(8,128)(2,1)}) custom-call(bf16[64,1024]{1,0:T(8,128)(2,1)} %refs_0_.1, s32[1,12]{1,0:T(1,128)} %bitcast.16, s32[1,12]{1,0:T(1,128)} %refs_2_.1, s32[1,12]{1,0:T(1,128)} %bitcast.17, s32[3,8]{1,0:T(4,128)} %bitcast.15), custom_call_target="tpu_custom_call" | custom-call | bytes 1048576 | tf_op jit(solution)/shard_map/pallas_call | solution.py:233
  1.8 11.8 %all_to_all.15.shares_ref = f32[8,16,128]{2,1,0:T(8,128)S(1)} all-to-all(f32[8,16,128]{2,1,0:T(8,128)} %bitcast.14), channel_id=1, replica_groups={{256,320,384,448,0,64,128,192},{257,321,385,449,1,65,129,193},{258,322,..., dimensions={0} | all-to-all | bytes 131072 | tf_op jit(solution)/shard_map/all_to_all | solution.py:246
  13.6 0.0 copy-start
  13.6 0.0 copy-start.1
  13.6 0.0 copy-start.2
  13.6 0.0 copy-start.3
  13.6 19.6 %all_to_all.16 = bf16[32,16,128]{2,1,0:T(8,128)(2,1)S(1)} all-to-all(bf16[32,16,128]{2,1,0:T(8,128)(2,1)S(1)} %shard_map.83), channel_id=1, replica_groups={{52,54,56,58,60,62,0,2,4,6,8,10,12,14,16,18,20,22,24,26,28,30,32,34,36,..., dimensions={0} | all-to-all | bytes 262144 | tf_op jit(solution)/shard_map/all_to_all | solution.py:257
  33.2 4.2 %all-gather = bf16[64,16,128]{2,1,0:T(8,128)(2,1)S(1)} all-gather(bf16[32,16,128]{2,1,0:T(8,128)(2,1)S(1)} %all_to_all.16), channel_id=2, replica_groups=mesh['freq'=8,'chip'=32,'core'=2] {'core'}, dimensions={0}, use_global_device_ids=true | all-gather | bytes 393216 | tf_op jit(solution)/shard_map/all_gather | solution.py:260
  37.4 0.0 copy-done
  37.4 0.0 copy-done.1
  37.4 0.0 copy-done.2
  37.4 0.0 copy-done.3
  37.4 1.1 %shard_map.84 = (bf16[32,128]{1,0:T(8,128)(2,1)S(1)}, f32[16,128]{1,0:T(8,128)S(1)}) custom-call(bf16[112,1152]{1,0:T(8,128)(2,1)S(1)} %copy-done.3, bf16[1024,128]{1,0:T(8,128)(2,1)S(1)} %bitcast.10, bf16[12,256,128]{2,1,0:T(8,128)(2,1)S(1)} %bitcast.11, bf16[12,256,128]{2,1,0:T(8,128)(2,1)S(1)} %bitcast.12, bf16[8,3,256,128]{3,2,1,0:T(8,128)(2,1)S(1)} %bitcast.9), custom_call_target="tpu_custom_call" | custom-call | bytes 1048576 | tf_op jit(solution)/shard_map/pallas_call | solution.py:263
  38.5 1.9 %all_gather.11.terms_ref = bf16[64,128]{1,0:T(8,128)(2,1)S(1)} all-gather(bf16[32,128]{1,0:T(8,128)(2,1)S(1)} %get-tuple-element.12), channel_id=1, replica_groups=mesh['freq'=8,'chip'=32,'core'=2] {'core'}, dimensions={0}, use_global_device_ids=true | all-gather | bytes 24576 | tf_op jit(solution)/shard_map/all_gather | solution.py:275
  40.3 0.2 shard_map.85
  40.5 13.3 %all_to_all.17 = bf16[32,16,128]{2,1,0:T(8,128)(2,1)S(1)} all-to-all(bf16[32,16,128]{2,1,0:T(8,128)(2,1)S(1)} %bitcast.13), channel_id=1, replica_groups={{52,54,56,58,60,62,0,2,4,6,8,10,12,14,16,18,20,22,24,26,28,30,32,34,36,..., dimensions={0} | all-to-all | bytes 262144 | tf_op jit(solution)/shard_map/all_to_all | solution.py:281
  53.9 0.6 %convert_element_type.19 = bf16[1,2,1024]{2,1,0:T(2,128)(2,1)} reshape(bf16[16,128]{1,0:T(8,128)(2,1)S(1)} %add_convert_fusion) | data formatting | bytes 8192 | tf_op jit(solution)/shard_map/convert_element_type | solution.py:291
  (3 shorter events, 0.1 us)
Async XLA Ops:
  13.6 23.8 %copy-start = (bf16[1,8,3,2,128,128]{5,4,3,2,1,0:T(8,128)(2,1)S(1)}, bf16[1,8,3,2,128,128]{5,4,3,2,1,0:T(8,128)(2,1)}, u32[]{:S(2)}) copy-start(bf16[1,8,3,2,128,128]{5,4,3,2,1,0:T(8,128)(2,1)} %param.9) | copy-start | bytes 4718596
  13.6 23.8 %copy-start.1 = (bf16[1,12,2,128,128]{4,3,2,1,0:T(8,128)(2,1)S(1)}, bf16[1,12,2,128,128]{4,3,2,1,0:T(8,128)(2,1)}, u32[]{:S(2)}) copy-start(bf16[1,12,2,128,128]{4,3,2,1,0:T(8,128)(2,1)} %param.12) | copy-start | bytes 2359300
  13.6 23.8 %copy-start.2 = (bf16[1,12,2,128,128]{4,3,2,1,0:T(8,128)(2,1)S(1)}, bf16[1,12,2,128,128]{4,3,2,1,0:T(8,128)(2,1)}, u32[]{:S(2)}) copy-start(bf16[1,12,2,128,128]{4,3,2,1,0:T(8,128)(2,1)} %param.11) | copy-start | bytes 2359300
  13.6 23.8 %copy-start.3 = (bf16[112,1152]{1,0:T(8,128)(2,1)S(1)}, bf16[112,1152]{1,0:T(8,128)(2,1)}, u32[]{:S(2)}) copy-start(bf16[112,1152]{1,0:T(8,128)(2,1)} %get-tuple-element.9.pick_ref) | copy-start | bytes 774148

commit v8 on v7

--- a/solution.py
+++ b/solution.py
@@ -33,16 +33,8 @@
     return lax.broadcasted_iota(jnp.int32, shape, dim)
 
 
-def turn(direct, crossed):
-    swapped = jnp.concatenate([-crossed[GROUP:], crossed[:GROUP]], 0)
-    return direct + swapped
-
-
-def chosen(where_at, values, fill):
-    out = jnp.full(where_at.shape, fill, jnp.int32)
-    for i, value in enumerate(values):
-        out = jnp.where(where_at == i, value, out)
-    return out
+def times_i(tile):
+    return jnp.concatenate([-tile[GROUP:], tile[:GROUP]], 0)
 
 
 def leaf_codes(chunk, chips):
@@ -66,37 +58,29 @@
         found = jnp.where(iota((rows, tasks), 1) == task[:, :tasks], value, 0.0)
         return jnp.where(task < tasks, jnp.sum(found, 1, keepdims=True), -1.0)
 
-    source = by_row(sources_ref).astype(jnp.int32)
     wanted = leaves_ref[...].astype(jnp.float32)
     own = iota((TILE, leaves), 1) == iota((TILE, leaves), 0) % GROUP
     listed = [
         jnp.sum(jnp.where(own, wanted[n : n + 1], 0.0), 1, keepdims=True) for n in range(near)
     ]
     near_part = iota((TILE, LANES), 0) // GROUP
-    near_codes = [leaf.astype(jnp.int32) * 2 + near_part for leaf in listed]
-    direct = source * 2 + part
-    turned = source * 2 + 1 - part
-    sign = jnp.where(part == 0, -1.0, 1.0)
-    chunks = pick_ref.shape[1] // LANES - 1
+    codes_of_rows = jnp.concatenate(
+        [by_row(sources_ref).astype(jnp.int32) * 2 + part]
+        + [leaf.astype(jnp.int32) * 2 + near_part for leaf in listed],
+        0,
+    )
+    chunks = pick_ref.shape[1] // LANES - 2
     for chunk in range(chunks):
-        codes = leaf_codes(chunk, chips)
-        lanes = slice(chunk * LANES, (chunk + 1) * LANES)
-        pick_ref[:rows, lanes] = jnp.where(direct == codes, 1.0, 0.0).astype(jnp.bfloat16)
-        pick_ref[rows : 2 * rows, lanes] = jnp.where(turned == codes, sign, 0.0).astype(
-            jnp.bfloat16
-        )
-        for n in range(near):
-            pick_ref[2 * rows + n * TILE : 2 * rows + (n + 1) * TILE, lanes] = jnp.where(
-                near_codes[n] == codes, 1.0, 0.0
-            ).astype(jnp.bfloat16)
-    extra = slice(chunks * LANES, (chunks + 1) * LANES)
-    pick_ref[:rows, extra] = by_row(ranks_ref).astype(jnp.bfloat16)
+        pick_ref[:, chunk * LANES : (chunk + 1) * LANES] = jnp.where(
+            codes_of_rows == leaf_codes(chunk, chips), 1.0, 0.0
+        ).astype(jnp.bfloat16)
     target = jnp.sum(jnp.where(row == lane % rows, by_row(targets_ref), 0.0), 0, keepdims=True)
     target = target.astype(jnp.int32)
     spare = tasks // GROUP * TILE + tasks % GROUP
     goal = jnp.where(row == spare, target >> 3, jnp.where(row == spare + 1, target & 7, 0))
-    pick_ref[rows : 2 * rows, extra] = goal.astype(jnp.float32).astype(jnp.bfloat16)
-    pick_ref[2 * rows :, extra] = jnp.zeros((near * TILE, LANES), jnp.bfloat16)
+    extra = jnp.concatenate([by_row(ranks_ref), goal.astype(jnp.float32)], 1)
+    pick_ref[:rows, chunks * LANES :] = extra.astype(jnp.bfloat16)
+    pick_ref[rows:, chunks * LANES :] = jnp.zeros((near * TILE, 2 * LANES), jnp.bfloat16)
 
 
 def partial_kernel(total_freq, total_steps, chips, *refs):
@@ -129,10 +113,8 @@
 
 def block_kernel(tasks, pick_ref, gathered_ref, right_ref, left_ref, blocks_ref, out_ref, near_ref):
     columns = gathered_ref.shape[0]
-    picked = dot(pick_ref[:, :columns], gathered_ref[...]).astype(jnp.bfloat16)
-    half = out_ref.shape[0]
-    extra = pick_ref[: 2 * half, columns:].astype(jnp.float32)
-    pair = jnp.concatenate([picked[:half], picked[half : 2 * half]], 1)
+    picked = dot(pick_ref[:, :columns], gathered_ref[...])
+    extra = pick_ref[: out_ref.shape[0], columns:].astype(jnp.float32)
     leaf = left_ref.shape[-1]
     own = iota((TILE, leaf), 0) % GROUP
     lane = iota((TILE, leaf), 1).astype(jnp.float32)
@@ -140,9 +122,10 @@
     for start in range(0, tasks, GROUP):
         rows = slice(2 * start, 2 * start + TILE)
         coeff = jnp.zeros((TILE, leaf), jnp.float32)
+        pair = jnp.concatenate([picked[rows], times_i(picked[rows])], 1).astype(jnp.bfloat16)
         for t in range(start, min(start + GROUP, tasks)):
-            coeff = jnp.where(own == t - start, dot(pair[rows], right_ref[t]), coeff)
-        coeffs.append(jnp.where(lane < extra[rows], coeff, 0.0).astype(jnp.bfloat16))
+            coeff = jnp.where(own == t - start, dot(pair, right_ref[t]), coeff)
+        coeffs.append(jnp.where(lane < extra[rows, :leaf], coeff, 0.0).astype(jnp.bfloat16))
     for start, coeff in zip(range(0, tasks, GROUP), coeffs):
         rows = slice(2 * start, 2 * start + TILE)
         direct = jnp.zeros((TILE, leaf), jnp.float32)
@@ -151,25 +134,34 @@
             both = dot(coeff, left_ref[t], True)
             direct = jnp.where(own == t - start, both[:, :leaf], direct)
             crossed = jnp.where(own == t - start, both[:, leaf:], crossed)
-        goal = extra[half + 2 * start : half + 2 * start + TILE]
-        terms = turn(direct, crossed) + goal
+        terms = direct + times_i(crossed) + extra[rows, leaf:]
         out_ref[rows, :] = terms.astype(jnp.bfloat16)
     leaves, near = blocks_ref.shape[:2]
     direct = jnp.zeros((TILE, leaf), jnp.float32)
     crossed = jnp.zeros((TILE, leaf), jnp.float32)
     for n in range(near):
-        view = picked[2 * half + TILE * n : 2 * half + TILE * (n + 1)]
+        at = out_ref.shape[0] + TILE * n
+        view = picked[at : at + TILE].astype(jnp.bfloat16)
         for l in range(leaves):
             both = dot(view, blocks_ref[l, n], True)
             direct = direct + jnp.where(own == l, both[:, :leaf], 0.0)
             crossed = crossed + jnp.where(own == l, both[:, leaf:], 0.0)
-    near_ref[...] = turn(direct, crossed)
+    near_ref[...] = direct + times_i(crossed)
 
 
 def spectrum_kernel(shares_ref, out_ref):
     spectrum = jnp.sum(shares_ref[...], 0).astype(jnp.bfloat16)
     for chip in range(out_ref.shape[0]):
         out_ref[chip] = spectrum
+
+
+def field_kernel(arrived_ref, near_ref, out_ref):
+    total = near_ref[...] + jnp.sum(arrived_ref[...].astype(jnp.float32), 0)
+    parts = [
+        jnp.concatenate([total[l : l + 1], total[GROUP + l : GROUP + l + 1]], 0)
+        for l in range(GROUP)
+    ]
+    out_ref[...] = jnp.concatenate(parts, 1).astype(jnp.bfloat16)
 
 
 def scatter_kernel(tasks, chips, terms_ref, out_ref):
@@ -234,15 +226,14 @@
         functools.partial(partial_kernel, total_freq, total_steps, chips),
         [
             ((total_freq * TILE, leaf), jnp.float32),
-            ((4 * slots + near * TILE, CORES * chips * TILE + LANES), jnp.bfloat16),
+            ((2 * slots + near * TILE, CORES * chips * TILE + 2 * LANES), jnp.bfloat16),
         ],
         [pl.ANY] * len(arrays),
         [
             *[pltpu.VMEM(array.shape, array.dtype) for array in arrays],
             pltpu.SemaphoreType.DMA((len(arrays),)),
         ],
-        limit=60,
-    )(*arrays)
+    )(*[pltpu.with_memory_space_constraint(array, pltpu.HBM) for array in arrays])
     shares = lax.all_to_all(
         partial.reshape(total_freq, TILE, leaf),
         "freq",
@@ -287,8 +278,10 @@
         tiled=True,
     )
 
-    field = near_field + jnp.sum(arrived.astype(jnp.float32), 0)
-    return field.reshape(1, 2, leaves * leaf).astype(jnp.bfloat16)
+    (field,) = call(field_kernel, [((2, leaves * leaf), jnp.bfloat16)], [vmem, vmem])(
+        arrived, near_field
+    )
+    return field[None]
 
 
 def solution(mesh):

time: 54.8 us -> 53 us (0.967)
  blocking collectives: 50.7 us -> 49.8 us
  local copies, waits for them, and re-layouts: 0.62 us -> 0.01 us
    all_to_all x1, blocking collectives: 11.8 us -> 10.9 us  [per_device(): lax.all_to_all(partial.reshape(total_freq, TILE, leaf), 'freq', 0, 0, axi...]
    pallas_call x1, Pallas kernels: 1.8 us -> 1.09 us  [per_device(): call(functools.partial(partial_kernel, total_freq, total_steps, chips), [...]
    pallas_call x0 -> x1, Pallas kernels: none -> 0.64 us  [per_device(): call(field_kernel, [((2, leaves * leaf), jnp.bfloat16)], [vmem, vmem])]
    convert_element_type x1 -> x0, local copies, waits for them, and re-layouts: 0.6 us -> none  [per_device(): return field.reshape(1, 2, leaves * leaf).astype(jnp.bfloat16)]
where the time goes in v8:
time: 53 us; the launch traced here: 52.8 us
  blocking collectives  49.8 us (94%)
  Pallas kernels  2.95 us (6%)
    all_to_all x1, blocking collectives, per_device(): lax.all_to_all(copies, 'chip', 0, 0, axis_index_groups=[rotated(chips, fi...  19.6 us
    all_to_all x1, blocking collectives, per_device(): lax.all_to_all(spread.reshape(chips, TILE, leaf), 'chip', 0, 0, axis_inde...  13.3 us
    all_to_all x1, blocking collectives, per_device(): lax.all_to_all(partial.reshape(total_freq, TILE, leaf), 'freq', 0, 0, axi...  10.9 us
    all_gather x1, blocking collectives, per_device(): gathered = lax.all_gather(same_core, 'core', axis=0, tiled=False)  4.18 us
    all_gather x1, blocking collectives, per_device(): both_terms = lax.all_gather(terms, 'core', axis=0, tiled=True)  1.86 us
    pallas_call x1, Pallas kernels, per_device(): call(functools.partial(partial_kernel, total_freq, total_steps, chips), [...  1.09 us

profile of v8, /device:TPU:1, one launch (start us, length us, event | category | flops | bytes accessed | tf_op | source)
XLA Modules:
  0.0 52.8 jit_solution(4303574277126678388)
XLA Ops:
  0.0 1.1 %shard_map.82 = (f32[128,128]{1,0:T(8,128)S(1)}, bf16[80,1280]{1,0:T(8,128)(2,1)S(1)}) custom-call(bf16[64,1024]{1,0:T(8,128)(2,1)} %refs_0_.1, s32[1,12]{1,0:T(1,128)} %bitcast.17, s32[1,12]{1,0:T(1,128)} %refs_2_.1, s32[1,12]{1,0:T(1,128)} %bitcast.18, s32[3,8]{1,0:T(4,128)} %bitcast.16), custom_call_target="tpu_custom_call" | custom-call | bytes 1048576 | tf_op jit(solution)/shard_map/pallas_call | solution.py:225
  1.1 10.9 %all_to_all.15.shares_ref = f32[8,16,128]{2,1,0:T(8,128)S(1)} all-to-all(f32[8,16,128]{2,1,0:T(8,128)S(1)} %bitcast.15), channel_id=1, replica_groups={{256,320,384,448,0,64,128,192},{257,321,385,449,1,65,129,193},{258,322,..., dimensions={0} | all-to-all | bytes 131072 | tf_op jit(solution)/shard_map/all_to_all | solution.py:237
  12.0 0.0 copy-start
  12.0 0.0 copy-start.1
  12.0 0.0 copy-start.2
  12.0 19.6 %all_to_all.16 = bf16[32,16,128]{2,1,0:T(8,128)(2,1)S(1)} all-to-all(bf16[32,16,128]{2,1,0:T(8,128)(2,1)S(1)} %shard_map.83), channel_id=1, replica_groups={{52,54,56,58,60,62,0,2,4,6,8,10,12,14,16,18,20,22,24,26,28,30,32,34,36,..., dimensions={0} | all-to-all | bytes 262144 | tf_op jit(solution)/shard_map/all_to_all | solution.py:248
  31.6 4.2 %all-gather = bf16[64,16,128]{2,1,0:T(8,128)(2,1)S(1)} all-gather(bf16[32,16,128]{2,1,0:T(8,128)(2,1)S(1)} %all_to_all.16), channel_id=2, replica_groups=mesh['freq'=8,'chip'=32,'core'=2] {'core'}, dimensions={0}, use_global_device_ids=true | all-gather | bytes 393216 | tf_op jit(solution)/shard_map/all_gather | solution.py:251
  35.8 0.0 copy-done
  35.8 0.0 copy-done.1
  35.8 0.0 copy-done.2
  35.8 1.0 %shard_map.84 = (bf16[32,128]{1,0:T(8,128)(2,1)S(1)}, f32[16,128]{1,0:T(8,128)S(1)}) custom-call(bf16[80,1280]{1,0:T(8,128)(2,1)S(1)} %get-tuple-element.9.pick_ref, bf16[1024,128]{1,0:T(8,128)(2,1)S(1)} %bitcast.11, bf16[12,256,128]{2,1,0:T(8,128)(2,1)S(1)} %bitcast.12, bf16[12,256,128]{2,1,0:T(8,128)(2,1)S(1)} %bitcast.13, ...), custom_call_target="tpu_custom_call" | custom-call | bytes 1048576 | tf_op jit(solution)/shard_map/pallas_call | solution.py:254
  36.8 1.9 %all_gather.11.terms_ref = bf16[64,128]{1,0:T(8,128)(2,1)S(1)} all-gather(bf16[32,128]{1,0:T(8,128)(2,1)S(1)} %get-tuple-element.11), channel_id=1, replica_groups=mesh['freq'=8,'chip'=32,'core'=2] {'core'}, dimensions={0}, use_global_device_ids=true | all-gather | bytes 24576 | tf_op jit(solution)/shard_map/all_gather | solution.py:266
  38.7 0.2 shard_map.85
  38.9 13.3 %all_to_all.17.arrived_ref = bf16[32,16,128]{2,1,0:T(8,128)(2,1)S(1)} all-to-all(bf16[32,16,128]{2,1,0:T(8,128)(2,1)S(1)} %bitcast.14), channel_id=1, replica_groups={{52,54,56,58,60,62,0,2,4,6,8,10,12,14,16,18,20,22,24,26,28,30,32,34,36,..., dimensions={0} | all-to-all | bytes 262144 | tf_op jit(solution)/shard_map/all_to_all | solution.py:272
  52.2 0.6 %shard_map.86 = bf16[2,1024]{1,0:T(2,128)(2,1)} custom-call(bf16[32,16,128]{2,1,0:T(8,128)(2,1)S(1)} %all_to_all.17.arrived_ref, f32[16,128]{1,0:T(8,128)S(1)} %get-tuple-element.12.near_ref), custom_call_target="tpu_custom_call" | custom-call | bytes 1048576 | tf_op jit(solution)/shard_map/pallas_call | solution.py:281
  (1 shorter events, 0.0 us)
Async XLA Ops:
  12.0 23.8 %copy-start = (bf16[1,8,3,2,128,128]{5,4,3,2,1,0:T(8,128)(2,1)S(1)}, bf16[1,8,3,2,128,128]{5,4,3,2,1,0:T(8,128)(2,1)}, u32[]{:S(2)}) copy-start(bf16[1,8,3,2,128,128]{5,4,3,2,1,0:T(8,128)(2,1)} %param.9) | copy-start | bytes 4718596
  12.0 23.8 %copy-start.1 = (bf16[1,12,2,128,128]{4,3,2,1,0:T(8,128)(2,1)S(1)}, bf16[1,12,2,128,128]{4,3,2,1,0:T(8,128)(2,1)}, u32[]{:S(2)}) copy-start(bf16[1,12,2,128,128]{4,3,2,1,0:T(8,128)(2,1)} %param.12) | copy-start | bytes 2359300
  12.0 23.8 %copy-start.2 = (bf16[1,12,2,128,128]{4,3,2,1,0:T(8,128)(2,1)S(1)}, bf16[1,12,2,128,128]{4,3,2,1,0:T(8,128)(2,1)}, u32[]{:S(2)}) copy-start(bf16[1,12,2,128,128]{4,3,2,1,0:T(8,128)(2,1)} %param.11) | copy-start | bytes 2359300

commit v9 on v8

--- a/solution.py
+++ b/solution.py
@@ -21,7 +21,7 @@
 
 
 def first_chip(chips):
-    return chips * 3 // 4 + 2
+    return chips // 2 + 2
 
 
 def dot(first_op, second_op, transposed=False):
@@ -103,11 +103,12 @@
     angle = 2.0 * math.pi / total_steps * phase.astype(jnp.float32)
     damping = jnp.exp(step.astype(jnp.float32) * (math.log(fall_total) / total_steps))
     weights = (damping * jnp.cos(angle) / math.sqrt(total_steps)).astype(jnp.bfloat16)
-    for copy in copies:
-        copy.wait()
+    copies[0].wait()
     part = dot(weights, history_ref[...])
     for l in range(leaves):
         out_ref[pl.ds(l, rows, stride=leaves), :] = part[:, l * leaf : (l + 1) * leaf]
+    for copy in copies[1:]:
+        copy.wait()
     plan(chips, pick_ref, *index_refs)
 
 
@@ -118,35 +119,42 @@
     leaf = left_ref.shape[-1]
     own = iota((TILE, leaf), 0) % GROUP
     lane = iota((TILE, leaf), 1).astype(jnp.float32)
-    coeffs = []
-    for start in range(0, tasks, GROUP):
-        rows = slice(2 * start, 2 * start + TILE)
+    leaves, near = blocks_ref.shape[:2]
+    views = [
+        picked[out_ref.shape[0] + TILE * n : out_ref.shape[0] + TILE * (n + 1)].astype(jnp.bfloat16)
+        for n in range(near)
+    ]
+
+    def near_part(n):
+        kept = jnp.zeros((TILE, 2 * leaf), jnp.float32)
+        wide_own = iota((TILE, 2 * leaf), 0) % GROUP
+        for l in range(leaves):
+            kept = jnp.where(wide_own == l, dot(views[n], blocks_ref[l, n], True), kept)
+        return kept
+
+    groups = [
+        (slice(2 * start, 2 * start + TILE), start, min(start + GROUP, tasks))
+        for start in range(0, tasks, GROUP)
+    ]
+    coeffs, near_sums = [], near_part(0)
+    for rows, start, stop in groups:
         coeff = jnp.zeros((TILE, leaf), jnp.float32)
         pair = jnp.concatenate([picked[rows], times_i(picked[rows])], 1).astype(jnp.bfloat16)
-        for t in range(start, min(start + GROUP, tasks)):
+        for t in range(start, stop):
             coeff = jnp.where(own == t - start, dot(pair, right_ref[t]), coeff)
         coeffs.append(jnp.where(lane < extra[rows, :leaf], coeff, 0.0).astype(jnp.bfloat16))
-    for start, coeff in zip(range(0, tasks, GROUP), coeffs):
-        rows = slice(2 * start, 2 * start + TILE)
+    for n in range(1, near):
+        near_sums = near_sums + near_part(n)
+    for (rows, start, stop), coeff in zip(groups, coeffs):
         direct = jnp.zeros((TILE, leaf), jnp.float32)
         crossed = jnp.zeros((TILE, leaf), jnp.float32)
-        for t in range(start, min(start + GROUP, tasks)):
+        for t in range(start, stop):
             both = dot(coeff, left_ref[t], True)
             direct = jnp.where(own == t - start, both[:, :leaf], direct)
             crossed = jnp.where(own == t - start, both[:, leaf:], crossed)
         terms = direct + times_i(crossed) + extra[rows, leaf:]
         out_ref[rows, :] = terms.astype(jnp.bfloat16)
-    leaves, near = blocks_ref.shape[:2]
-    direct = jnp.zeros((TILE, leaf), jnp.float32)
-    crossed = jnp.zeros((TILE, leaf), jnp.float32)
-    for n in range(near):
-        at = out_ref.shape[0] + TILE * n
-        view = picked[at : at + TILE].astype(jnp.bfloat16)
-        for l in range(leaves):
-            both = dot(view, blocks_ref[l, n], True)
-            direct = direct + jnp.where(own == l, both[:, :leaf], 0.0)
-            crossed = crossed + jnp.where(own == l, both[:, leaf:], 0.0)
-    near_ref[...] = direct + times_i(crossed)
+    near_ref[...] = near_sums[:, :leaf] + times_i(near_sums[:, leaf:])
 
 
 def spectrum_kernel(shares_ref, out_ref):

time: 53 us -> 53.7 us (1.013)
  blocking collectives: 49.8 us -> 50.4 us
    all_to_all x1, blocking collectives: 13.3 us -> 13.9 us  [per_device(): lax.all_to_all(spread.reshape(chips, TILE, leaf), 'chip', 0, 0, axis_inde...]
where the time goes in v9:
time: 53.7 us; the launch traced here: 53.5 us
  blocking collectives  50.4 us (94%)
  Pallas kernels  3.02 us (6%)
    all_to_all x1, blocking collectives, per_device(): lax.all_to_all(copies, 'chip', 0, 0, axis_index_groups=[rotated(chips, fi...  19.6 us
    all_to_all x1, blocking collectives, per_device(): lax.all_to_all(spread.reshape(chips, TILE, leaf), 'chip', 0, 0, axis_inde...  13.9 us
    all_to_all x1, blocking collectives, per_device(): lax.all_to_all(partial.reshape(total_freq, TILE, leaf), 'freq', 0, 0, axi...  10.9 us
    all_gather x1, blocking collectives, per_device(): gathered = lax.all_gather(same_core, 'core', axis=0, tiled=False)  4.21 us
    all_gather x1, blocking collectives, per_device(): both_terms = lax.all_gather(terms, 'core', axis=0, tiled=True)  1.86 us
    pallas_call x1, Pallas kernels, per_device(): call(functools.partial(partial_kernel, total_freq, total_steps, chips), [...  1.22 us

profile of v9, /device:TPU:1, one launch (start us, length us, event | category | flops | bytes accessed | tf_op | source)
XLA Modules:
  0.0 53.5 jit_solution(18246590791915061683)
XLA Ops:
  0.0 1.2 %shard_map.82 = (f32[128,128]{1,0:T(8,128)S(1)}, bf16[80,1280]{1,0:T(8,128)(2,1)S(1)}) custom-call(bf16[64,1024]{1,0:T(8,128)(2,1)} %refs_0_.1, s32[1,12]{1,0:T(1,128)} %bitcast.17, s32[1,12]{1,0:T(1,128)} %refs_2_.1, s32[1,12]{1,0:T(1,128)} %bitcast.18, s32[3,8]{1,0:T(4,128)} %bitcast.16), custom_call_target="tpu_custom_call" | custom-call | bytes 1048576 | tf_op jit(solution)/shard_map/pallas_call | solution.py:233
  1.2 10.9 %all_to_all.15.shares_ref = f32[8,16,128]{2,1,0:T(8,128)S(1)} all-to-all(f32[8,16,128]{2,1,0:T(8,128)S(1)} %bitcast.15), channel_id=1, replica_groups={{256,320,384,448,0,64,128,192},{257,321,385,449,1,65,129,193},{258,322,..., dimensions={0} | all-to-all | bytes 131072 | tf_op jit(solution)/shard_map/all_to_all | solution.py:245
  12.1 0.0 copy-start
  12.1 0.0 copy-start.1
  12.1 0.0 copy-start.2
  12.1 19.6 %all_to_all.16 = bf16[32,16,128]{2,1,0:T(8,128)(2,1)S(1)} all-to-all(bf16[32,16,128]{2,1,0:T(8,128)(2,1)S(1)} %shard_map.83), channel_id=1, replica_groups={{36,38,40,42,44,46,48,50,52,54,56,58,60,62,0,2,4,6,8,10,12,14,16,18,20,..., dimensions={0} | all-to-all | bytes 262144 | tf_op jit(solution)/shard_map/all_to_all | solution.py:256
  31.7 4.2 %all-gather = bf16[64,16,128]{2,1,0:T(8,128)(2,1)S(1)} all-gather(bf16[32,16,128]{2,1,0:T(8,128)(2,1)S(1)} %all_to_all.16), channel_id=2, replica_groups=mesh['freq'=8,'chip'=32,'core'=2] {'core'}, dimensions={0}, use_global_device_ids=true | all-gather | bytes 393216 | tf_op jit(solution)/shard_map/all_gather | solution.py:259
  35.9 0.0 copy-done
  35.9 0.0 copy-done.1
  36.0 0.0 copy-done.2
  36.0 1.0 %shard_map.84 = (bf16[32,128]{1,0:T(8,128)(2,1)S(1)}, f32[16,128]{1,0:T(8,128)S(1)}) custom-call(bf16[80,1280]{1,0:T(8,128)(2,1)S(1)} %get-tuple-element.9.pick_ref, bf16[1024,128]{1,0:T(8,128)(2,1)S(1)} %bitcast.11, bf16[12,256,128]{2,1,0:T(8,128)(2,1)S(1)} %bitcast.12, bf16[12,256,128]{2,1,0:T(8,128)(2,1)S(1)} %bitcast.13, ...), custom_call_target="tpu_custom_call" | custom-call | bytes 1048576 | tf_op jit(solution)/shard_map/pallas_call | solution.py:262
  36.9 1.9 %all_gather.11.terms_ref = bf16[64,128]{1,0:T(8,128)(2,1)S(1)} all-gather(bf16[32,128]{1,0:T(8,128)(2,1)S(1)} %get-tuple-element.11), channel_id=1, replica_groups=mesh['freq'=8,'chip'=32,'core'=2] {'core'}, dimensions={0}, use_global_device_ids=true | all-gather | bytes 24576 | tf_op jit(solution)/shard_map/all_gather | solution.py:274
  38.8 0.2 shard_map.85
  39.0 13.9 %all_to_all.17.arrived_ref = bf16[32,16,128]{2,1,0:T(8,128)(2,1)S(1)} all-to-all(bf16[32,16,128]{2,1,0:T(8,128)(2,1)S(1)} %bitcast.14), channel_id=1, replica_groups={{36,38,40,42,44,46,48,50,52,54,56,58,60,62,0,2,4,6,8,10,12,14,16,18,20,..., dimensions={0} | all-to-all | bytes 262144 | tf_op jit(solution)/shard_map/all_to_all | solution.py:280
  52.9 0.6 %shard_map.86 = bf16[2,1024]{1,0:T(2,128)(2,1)} custom-call(bf16[32,16,128]{2,1,0:T(8,128)(2,1)S(1)} %all_to_all.17.arrived_ref, f32[16,128]{1,0:T(8,128)S(1)} %get-tuple-element.12.near_ref), custom_call_target="tpu_custom_call" | custom-call | bytes 1048576 | tf_op jit(solution)/shard_map/pallas_call | solution.py:289
  (1 shorter events, 0.0 us)
Async XLA Ops:
  12.1 23.8 %copy-start = (bf16[1,8,3,2,128,128]{5,4,3,2,1,0:T(8,128)(2,1)S(1)}, bf16[1,8,3,2,128,128]{5,4,3,2,1,0:T(8,128)(2,1)}, u32[]{:S(2)}) copy-start(bf16[1,8,3,2,128,128]{5,4,3,2,1,0:T(8,128)(2,1)} %param.9) | copy-start | bytes 4718596
  12.1 23.8 %copy-start.1 = (bf16[1,12,2,128,128]{4,3,2,1,0:T(8,128)(2,1)S(1)}, bf16[1,12,2,128,128]{4,3,2,1,0:T(8,128)(2,1)}, u32[]{:S(2)}) copy-start(bf16[1,12,2,128,128]{4,3,2,1,0:T(8,128)(2,1)} %param.12) | copy-start | bytes 2359300
  12.1 23.8 %copy-start.2 = (bf16[1,12,2,128,128]{4,3,2,1,0:T(8,128)(2,1)S(1)}, bf16[1,12,2,128,128]{4,3,2,1,0:T(8,128)(2,1)}, u32[]{:S(2)}) copy-start(bf16[1,12,2,128,128]{4,3,2,1,0:T(8,128)(2,1)} %param.11) | copy-start | bytes 2359300

commit v10 on v9

--- a/solution.py
+++ b/solution.py
@@ -21,7 +21,7 @@
 
 
 def first_chip(chips):
-    return chips // 2 + 2
+    return chips - 1
 
 
 def dot(first_op, second_op, transposed=False):
@@ -103,12 +103,11 @@
     angle = 2.0 * math.pi / total_steps * phase.astype(jnp.float32)
     damping = jnp.exp(step.astype(jnp.float32) * (math.log(fall_total) / total_steps))
     weights = (damping * jnp.cos(angle) / math.sqrt(total_steps)).astype(jnp.bfloat16)
-    copies[0].wait()
+    for copy in copies:
+        copy.wait()
     part = dot(weights, history_ref[...])
     for l in range(leaves):
         out_ref[pl.ds(l, rows, stride=leaves), :] = part[:, l * leaf : (l + 1) * leaf]
-    for copy in copies[1:]:
-        copy.wait()
     plan(chips, pick_ref, *index_refs)
 
 

time: 53.7 us -> 53.2 us (level)
    all_to_all x1, blocking collectives: 13.9 us -> 12.8 us  [per_device(): lax.all_to_all(spread.reshape(chips, TILE, leaf), 'chip', 0, 0, axis_inde...]
    all_to_all x1, blocking collectives: 19.6 us -> 20.5 us  [per_device(): lax.all_to_all(copies, 'chip', 0, 0, axis_index_groups=[rotated(chips, fi...]
where the time goes in v10:
time: 53.2 us; the launch traced here: 52.9 us
  blocking collectives  50 us (94%)
  Pallas kernels  2.9 us (5%)
    all_to_all x1, blocking collectives, per_device(): lax.all_to_all(copies, 'chip', 0, 0, axis_index_groups=[rotated(chips, fi...  20.5 us
    all_to_all x1, blocking collectives, per_device(): lax.all_to_all(spread.reshape(chips, TILE, leaf), 'chip', 0, 0, axis_inde...  12.8 us
    all_to_all x1, blocking collectives, per_device(): lax.all_to_all(partial.reshape(total_freq, TILE, leaf), 'freq', 0, 0, axi...  10.9 us
    all_gather x1, blocking collectives, per_device(): gathered = lax.all_gather(same_core, 'core', axis=0, tiled=False)  4 us
    all_gather x1, blocking collectives, per_device(): both_terms = lax.all_gather(terms, 'core', axis=0, tiled=True)  1.86 us
    pallas_call x1, Pallas kernels, per_device(): call(functools.partial(partial_kernel, total_freq, total_steps, chips), [...  1.09 us

profile of v10, /device:TPU:1, one launch (start us, length us, event | category | flops | bytes accessed | tf_op | source)
XLA Modules:
  0.0 52.9 jit_solution(13242946503191627361)
XLA Ops:
  0.0 1.1 %shard_map.82 = (f32[128,128]{1,0:T(8,128)S(1)}, bf16[80,1280]{1,0:T(8,128)(2,1)S(1)}) custom-call(bf16[64,1024]{1,0:T(8,128)(2,1)} %refs_0_.1, s32[1,12]{1,0:T(1,128)} %bitcast.17, s32[1,12]{1,0:T(1,128)} %refs_2_.1, s32[1,12]{1,0:T(1,128)} %bitcast.18, s32[3,8]{1,0:T(4,128)} %bitcast.16), custom_call_target="tpu_custom_call" | custom-call | bytes 1048576 | tf_op jit(solution)/shard_map/pallas_call | solution.py:232
  1.1 10.9 %all_to_all.15.shares_ref = f32[8,16,128]{2,1,0:T(8,128)S(1)} all-to-all(f32[8,16,128]{2,1,0:T(8,128)S(1)} %bitcast.15), channel_id=1, replica_groups={{256,320,384,448,0,64,128,192},{257,321,385,449,1,65,129,193},{258,322,..., dimensions={0} | all-to-all | bytes 131072 | tf_op jit(solution)/shard_map/all_to_all | solution.py:244
  12.0 0.0 copy-start
  12.0 0.0 copy-start.1
  12.0 0.0 copy-start.2
  12.0 20.5 %all_to_all.16 = bf16[32,16,128]{2,1,0:T(8,128)(2,1)S(1)} all-to-all(bf16[32,16,128]{2,1,0:T(8,128)(2,1)S(1)} %shard_map.83), channel_id=1, replica_groups={{62,0,2,4,6,8,10,12,14,16,18,20,22,24,26,28,30,32,34,36,38,40,42,44,46,..., dimensions={0} | all-to-all | bytes 262144 | tf_op jit(solution)/shard_map/all_to_all | solution.py:255
  32.5 4.0 %all-gather = bf16[64,16,128]{2,1,0:T(8,128)(2,1)S(1)} all-gather(bf16[32,16,128]{2,1,0:T(8,128)(2,1)S(1)} %all_to_all.16), channel_id=2, replica_groups=mesh['freq'=8,'chip'=32,'core'=2] {'core'}, dimensions={0}, use_global_device_ids=true | all-gather | bytes 393216 | tf_op jit(solution)/shard_map/all_gather | solution.py:258
  36.5 0.0 copy-done
  36.5 0.0 copy-done.1
  36.5 0.0 copy-done.2
  36.5 1.0 %shard_map.84 = (bf16[32,128]{1,0:T(8,128)(2,1)S(1)}, f32[16,128]{1,0:T(8,128)S(1)}) custom-call(bf16[80,1280]{1,0:T(8,128)(2,1)S(1)} %get-tuple-element.9.pick_ref, bf16[1024,128]{1,0:T(8,128)(2,1)S(1)} %bitcast.11, bf16[12,256,128]{2,1,0:T(8,128)(2,1)S(1)} %bitcast.12, bf16[12,256,128]{2,1,0:T(8,128)(2,1)S(1)} %bitcast.13, ...), custom_call_target="tpu_custom_call" | custom-call | bytes 1048576 | tf_op jit(solution)/shard_map/pallas_call | solution.py:261
  37.5 1.9 %all_gather.11.terms_ref = bf16[64,128]{1,0:T(8,128)(2,1)S(1)} all-gather(bf16[32,128]{1,0:T(8,128)(2,1)S(1)} %get-tuple-element.11), channel_id=1, replica_groups=mesh['freq'=8,'chip'=32,'core'=2] {'core'}, dimensions={0}, use_global_device_ids=true | all-gather | bytes 24576 | tf_op jit(solution)/shard_map/all_gather | solution.py:273
  39.3 0.2 shard_map.85
  39.5 12.8 %all_to_all.17.arrived_ref = bf16[32,16,128]{2,1,0:T(8,128)(2,1)S(1)} all-to-all(bf16[32,16,128]{2,1,0:T(8,128)(2,1)S(1)} %bitcast.14), channel_id=1, replica_groups={{62,0,2,4,6,8,10,12,14,16,18,20,22,24,26,28,30,32,34,36,38,40,42,44,46,..., dimensions={0} | all-to-all | bytes 262144 | tf_op jit(solution)/shard_map/all_to_all | solution.py:279
  52.3 0.6 %shard_map.86 = bf16[2,1024]{1,0:T(2,128)(2,1)} custom-call(bf16[32,16,128]{2,1,0:T(8,128)(2,1)S(1)} %all_to_all.17.arrived_ref, f32[16,128]{1,0:T(8,128)S(1)} %get-tuple-element.12.near_ref), custom_call_target="tpu_custom_call" | custom-call | bytes 1048576 | tf_op jit(solution)/shard_map/pallas_call | solution.py:288
  (1 shorter events, 0.0 us)
Async XLA Ops:
  12.0 24.5 %copy-start = (bf16[1,8,3,2,128,128]{5,4,3,2,1,0:T(8,128)(2,1)S(1)}, bf16[1,8,3,2,128,128]{5,4,3,2,1,0:T(8,128)(2,1)}, u32[]{:S(2)}) copy-start(bf16[1,8,3,2,128,128]{5,4,3,2,1,0:T(8,128)(2,1)} %param.9) | copy-start | bytes 4718596
  12.0 24.5 %copy-start.1 = (bf16[1,12,2,128,128]{4,3,2,1,0:T(8,128)(2,1)S(1)}, bf16[1,12,2,128,128]{4,3,2,1,0:T(8,128)(2,1)}, u32[]{:S(2)}) copy-start(bf16[1,12,2,128,128]{4,3,2,1,0:T(8,128)(2,1)} %param.12) | copy-start | bytes 2359300
  12.0 24.5 %copy-start.2 = (bf16[1,12,2,128,128]{4,3,2,1,0:T(8,128)(2,1)S(1)}, bf16[1,12,2,128,128]{4,3,2,1,0:T(8,128)(2,1)}, u32[]{:S(2)}) copy-start(bf16[1,12,2,128,128]{4,3,2,1,0:T(8,128)(2,1)} %param.11) | copy-start | bytes 2359300

commit v11 on v10

--- a/solution.py
+++ b/solution.py
@@ -21,7 +21,7 @@
 
 
 def first_chip(chips):
-    return chips - 1
+    return chips - 2
 
 
 def dot(first_op, second_op, transposed=False):

time: 53.2 us -> 52.7 us (level)
    all_to_all x1, blocking collectives: 20.5 us -> 19.8 us  [per_device(): lax.all_to_all(copies, 'chip', 0, 0, axis_index_groups=[rotated(chips, fi...]
where the time goes in v11:
time: 52.7 us; the launch traced here: 52.5 us
  blocking collectives  49.6 us (94%)
  Pallas kernels  2.9 us (6%)
    all_to_all x1, blocking collectives, per_device(): lax.all_to_all(copies, 'chip', 0, 0, axis_index_groups=[rotated(chips, fi...  19.8 us
    all_to_all x1, blocking collectives, per_device(): lax.all_to_all(spread.reshape(chips, TILE, leaf), 'chip', 0, 0, axis_inde...  12.9 us
    all_to_all x1, blocking collectives, per_device(): lax.all_to_all(partial.reshape(total_freq, TILE, leaf), 'freq', 0, 0, axi...  10.9 us
    all_gather x1, blocking collectives, per_device(): gathered = lax.all_gather(same_core, 'core', axis=0, tiled=False)  4.09 us
    all_gather x1, blocking collectives, per_device(): both_terms = lax.all_gather(terms, 'core', axis=0, tiled=True)  1.86 us
    pallas_call x1, Pallas kernels, per_device(): call(functools.partial(partial_kernel, total_freq, total_steps, chips), [...  1.09 us

profile of v11, /device:TPU:1, one launch (start us, length us, event | category | flops | bytes accessed | tf_op | source)
XLA Modules:
  0.0 52.5 jit_solution(14200371247784251289)
XLA Ops:
  0.0 1.1 %shard_map.82 = (f32[128,128]{1,0:T(8,128)S(1)}, bf16[80,1280]{1,0:T(8,128)(2,1)S(1)}) custom-call(bf16[64,1024]{1,0:T(8,128)(2,1)} %refs_0_.1, s32[1,12]{1,0:T(1,128)} %bitcast.17, s32[1,12]{1,0:T(1,128)} %refs_2_.1, s32[1,12]{1,0:T(1,128)} %bitcast.18, s32[3,8]{1,0:T(4,128)} %bitcast.16), custom_call_target="tpu_custom_call" | custom-call | bytes 1048576 | tf_op jit(solution)/shard_map/pallas_call | solution.py:232
  1.1 10.9 %all_to_all.15.shares_ref = f32[8,16,128]{2,1,0:T(8,128)S(1)} all-to-all(f32[8,16,128]{2,1,0:T(8,128)S(1)} %bitcast.15), channel_id=1, replica_groups={{256,320,384,448,0,64,128,192},{257,321,385,449,1,65,129,193},{258,322,..., dimensions={0} | all-to-all | bytes 131072 | tf_op jit(solution)/shard_map/all_to_all | solution.py:244
  12.0 0.0 copy-start
  12.0 0.0 copy-start.1
  12.0 0.0 copy-start.2
  12.0 19.8 %all_to_all.16 = bf16[32,16,128]{2,1,0:T(8,128)(2,1)S(1)} all-to-all(bf16[32,16,128]{2,1,0:T(8,128)(2,1)S(1)} %shard_map.83), channel_id=1, replica_groups={{60,62,0,2,4,6,8,10,12,14,16,18,20,22,24,26,28,30,32,34,36,38,40,42,44,..., dimensions={0} | all-to-all | bytes 262144 | tf_op jit(solution)/shard_map/all_to_all | solution.py:255
  31.8 4.1 %all-gather = bf16[64,16,128]{2,1,0:T(8,128)(2,1)S(1)} all-gather(bf16[32,16,128]{2,1,0:T(8,128)(2,1)S(1)} %all_to_all.16), channel_id=2, replica_groups=mesh['freq'=8,'chip'=32,'core'=2] {'core'}, dimensions={0}, use_global_device_ids=true | all-gather | bytes 393216 | tf_op jit(solution)/shard_map/all_gather | solution.py:258
  35.9 0.0 copy-done
  35.9 0.0 copy-done.1
  35.9 0.0 copy-done.2
  35.9 1.0 %shard_map.84 = (bf16[32,128]{1,0:T(8,128)(2,1)S(1)}, f32[16,128]{1,0:T(8,128)S(1)}) custom-call(bf16[80,1280]{1,0:T(8,128)(2,1)S(1)} %get-tuple-element.9.pick_ref, bf16[1024,128]{1,0:T(8,128)(2,1)S(1)} %bitcast.11, bf16[12,256,128]{2,1,0:T(8,128)(2,1)S(1)} %bitcast.12, bf16[12,256,128]{2,1,0:T(8,128)(2,1)S(1)} %bitcast.13, ...), custom_call_target="tpu_custom_call" | custom-call | bytes 1048576 | tf_op jit(solution)/shard_map/pallas_call | solution.py:261
  36.9 1.9 %all_gather.11.terms_ref = bf16[64,128]{1,0:T(8,128)(2,1)S(1)} all-gather(bf16[32,128]{1,0:T(8,128)(2,1)S(1)} %get-tuple-element.11), channel_id=1, replica_groups=mesh['freq'=8,'chip'=32,'core'=2] {'core'}, dimensions={0}, use_global_device_ids=true | all-gather | bytes 24576 | tf_op jit(solution)/shard_map/all_gather | solution.py:273
  38.8 0.2 shard_map.85
  38.9 12.9 %all_to_all.17.arrived_ref = bf16[32,16,128]{2,1,0:T(8,128)(2,1)S(1)} all-to-all(bf16[32,16,128]{2,1,0:T(8,128)(2,1)S(1)} %bitcast.14), channel_id=1, replica_groups={{60,62,0,2,4,6,8,10,12,14,16,18,20,22,24,26,28,30,32,34,36,38,40,42,44,..., dimensions={0} | all-to-all | bytes 262144 | tf_op jit(solution)/shard_map/all_to_all | solution.py:279
  51.9 0.6 %shard_map.86 = bf16[2,1024]{1,0:T(2,128)(2,1)} custom-call(bf16[32,16,128]{2,1,0:T(8,128)(2,1)S(1)} %all_to_all.17.arrived_ref, f32[16,128]{1,0:T(8,128)S(1)} %get-tuple-element.12.near_ref), custom_call_target="tpu_custom_call" | custom-call | bytes 1048576 | tf_op jit(solution)/shard_map/pallas_call | solution.py:288
  (1 shorter events, 0.0 us)
Async XLA Ops:
  12.0 23.9 %copy-start = (bf16[1,8,3,2,128,128]{5,4,3,2,1,0:T(8,128)(2,1)S(1)}, bf16[1,8,3,2,128,128]{5,4,3,2,1,0:T(8,128)(2,1)}, u32[]{:S(2)}) copy-start(bf16[1,8,3,2,128,128]{5,4,3,2,1,0:T(8,128)(2,1)} %param.9) | copy-start | bytes 4718596
  12.0 23.9 %copy-start.1 = (bf16[1,12,2,128,128]{4,3,2,1,0:T(8,128)(2,1)S(1)}, bf16[1,12,2,128,128]{4,3,2,1,0:T(8,128)(2,1)}, u32[]{:S(2)}) copy-start(bf16[1,12,2,128,128]{4,3,2,1,0:T(8,128)(2,1)} %param.12) | copy-start | bytes 2359300
  12.0 23.9 %copy-start.2 = (bf16[1,12,2,128,128]{4,3,2,1,0:T(8,128)(2,1)S(1)}, bf16[1,12,2,128,128]{4,3,2,1,0:T(8,128)(2,1)}, u32[]{:S(2)}) copy-start(bf16[1,12,2,128,128]{4,3,2,1,0:T(8,128)(2,1)} %param.11) | copy-start | bytes 2359300

commit v12 on v11

--- a/solution.py
+++ b/solution.py
@@ -20,8 +20,12 @@
     return [(i + first) % size for i in range(size)]
 
 
-def first_chip(chips):
-    return chips - 2
+def chip_at(place, chips):
+    return (place * 5 + chips - 2) % chips
+
+
+def chip_order(chips):
+    return [chip_at(place, chips) for place in range(chips)]
 
 
 def dot(first_op, second_op, transposed=False):
@@ -40,7 +44,7 @@
 def leaf_codes(chunk, chips):
     at = chunk * LANES + iota((1, LANES), 1)
     core = at // (chips * TILE)
-    chip = (at // TILE + first_chip(chips)) % chips
+    chip = chip_at(at // TILE % chips, chips)
     return (chip * CORES + core) * TILE + at % GROUP * 2 + at // GROUP % 2
 
 
@@ -189,7 +193,7 @@
     place = jnp.concatenate(
         [
             jnp.where(code - chip * (CORES * TILE) == base, 1.0, 0.0)
-            for chip in rotated(chips, first_chip(chips))
+            for chip in chip_order(chips)
         ],
         0,
     )
@@ -253,7 +257,7 @@
         spectrum_kernel, [((chips, TILE, leaf), jnp.bfloat16)], [vmem], flops=20_000_000_000
     )(shares)
     same_core = lax.all_to_all(
-        copies, "chip", 0, 0, axis_index_groups=[rotated(chips, first_chip(chips))], tiled=True
+        copies, "chip", 0, 0, axis_index_groups=[chip_order(chips)], tiled=True
     )
     gathered = lax.all_gather(same_core, "core", axis=0, tiled=False)
     gathered = gathered.reshape(CORES * chips * TILE, leaf)
@@ -281,7 +285,7 @@
         "chip",
         0,
         0,
-        axis_index_groups=[rotated(chips, first_chip(chips))],
+        axis_index_groups=[chip_order(chips)],
         tiled=True,
     )
 

time: 52.7 us -> 52.2 us (level)
  blocking collectives: 49.6 us -> 48.9 us
    all_to_all x1, blocking collectives: 12.9 us -> 12.3 us  [per_device(): lax.all_to_all(spread.reshape(chips, TILE, leaf), 'chip', 0, 0, axis_inde...]
where the time goes in v12:
time: 52.2 us; the launch traced here: 51.8 us
  blocking collectives  48.9 us (94%)
  Pallas kernels  2.9 us (6%)
    all_to_all x1, blocking collectives, per_device(): lax.all_to_all(copies, 'chip', 0, 0, axis_index_groups=[chip_order(chips)...  19.5 us
    all_to_all x1, blocking collectives, per_device(): lax.all_to_all(spread.reshape(chips, TILE, leaf), 'chip', 0, 0, axis_inde...  12.3 us
    all_to_all x1, blocking collectives, per_device(): lax.all_to_all(partial.reshape(total_freq, TILE, leaf), 'freq', 0, 0, axi...  10.9 us
    all_gather x1, blocking collectives, per_device(): gathered = lax.all_gather(same_core, 'core', axis=0, tiled=False)  4.34 us
    all_gather x1, blocking collectives, per_device(): both_terms = lax.all_gather(terms, 'core', axis=0, tiled=True)  1.86 us
    pallas_call x1, Pallas kernels, per_device(): call(functools.partial(partial_kernel, total_freq, total_steps, chips), [...  1.09 us

profile of v12, /device:TPU:1, one launch (start us, length us, event | category | flops | bytes accessed | tf_op | source)
XLA Modules:
  0.0 51.8 jit_solution(860589558340846038)
XLA Ops:
  0.0 1.1 %shard_map.82 = (f32[128,128]{1,0:T(8,128)S(1)}, bf16[80,1280]{1,0:T(8,128)(2,1)S(1)}) custom-call(bf16[64,1024]{1,0:T(8,128)(2,1)} %refs_0_.1, s32[1,12]{1,0:T(1,128)} %bitcast.17, s32[1,12]{1,0:T(1,128)} %refs_2_.1, s32[1,12]{1,0:T(1,128)} %bitcast.18, s32[3,8]{1,0:T(4,128)} %bitcast.16), custom_call_target="tpu_custom_call" | custom-call | bytes 1048576 | tf_op jit(solution)/shard_map/pallas_call | solution.py:236
  1.1 10.9 %all_to_all.15.shares_ref = f32[8,16,128]{2,1,0:T(8,128)S(1)} all-to-all(f32[8,16,128]{2,1,0:T(8,128)S(1)} %bitcast.15), channel_id=1, replica_groups={{256,320,384,448,0,64,128,192},{257,321,385,449,1,65,129,193},{258,322,..., dimensions={0} | all-to-all | bytes 131072 | tf_op jit(solution)/shard_map/all_to_all | solution.py:248
  12.0 0.0 copy-start
  12.0 0.0 copy-start.1
  12.0 0.0 copy-start.2
  12.0 19.5 %all_to_all.16 = bf16[32,16,128]{2,1,0:T(8,128)(2,1)S(1)} all-to-all(bf16[32,16,128]{2,1,0:T(8,128)(2,1)S(1)} %shard_map.83), channel_id=1, replica_groups={{60,6,16,26,36,46,56,2,12,22,32,42,52,62,8,18,28,38,48,58,4,14,24,34,44..., dimensions={0} | all-to-all | bytes 262144 | tf_op jit(solution)/shard_map/all_to_all | solution.py:259
  31.5 4.3 %all-gather = bf16[64,16,128]{2,1,0:T(8,128)(2,1)S(1)} all-gather(bf16[32,16,128]{2,1,0:T(8,128)(2,1)S(1)} %all_to_all.16), channel_id=2, replica_groups=mesh['freq'=8,'chip'=32,'core'=2] {'core'}, dimensions={0}, use_global_device_ids=true | all-gather | bytes 393216 | tf_op jit(solution)/shard_map/all_gather | solution.py:262
  35.8 0.0 copy-done
  35.8 0.0 copy-done.1
  35.8 0.0 copy-done.2
  35.8 1.0 %shard_map.84 = (bf16[32,128]{1,0:T(8,128)(2,1)S(1)}, f32[16,128]{1,0:T(8,128)S(1)}) custom-call(bf16[80,1280]{1,0:T(8,128)(2,1)S(1)} %get-tuple-element.9.pick_ref, bf16[1024,128]{1,0:T(8,128)(2,1)S(1)} %bitcast.11, bf16[12,256,128]{2,1,0:T(8,128)(2,1)S(1)} %bitcast.12, bf16[12,256,128]{2,1,0:T(8,128)(2,1)S(1)} %bitcast.13, ...), custom_call_target="tpu_custom_call" | custom-call | bytes 1048576 | tf_op jit(solution)/shard_map/pallas_call | solution.py:265
  36.8 1.9 %all_gather.11.terms_ref = bf16[64,128]{1,0:T(8,128)(2,1)S(1)} all-gather(bf16[32,128]{1,0:T(8,128)(2,1)S(1)} %get-tuple-element.11), channel_id=1, replica_groups=mesh['freq'=8,'chip'=32,'core'=2] {'core'}, dimensions={0}, use_global_device_ids=true | all-gather | bytes 24576 | tf_op jit(solution)/shard_map/all_gather | solution.py:277
  38.7 0.2 shard_map.85
  38.9 12.3 %all_to_all.17.arrived_ref = bf16[32,16,128]{2,1,0:T(8,128)(2,1)S(1)} all-to-all(bf16[32,16,128]{2,1,0:T(8,128)(2,1)S(1)} %bitcast.14), channel_id=1, replica_groups={{60,6,16,26,36,46,56,2,12,22,32,42,52,62,8,18,28,38,48,58,4,14,24,34,44..., dimensions={0} | all-to-all | bytes 262144 | tf_op jit(solution)/shard_map/all_to_all | solution.py:283
  51.2 0.6 %shard_map.86 = bf16[2,1024]{1,0:T(2,128)(2,1)} custom-call(bf16[32,16,128]{2,1,0:T(8,128)(2,1)S(1)} %all_to_all.17.arrived_ref, f32[16,128]{1,0:T(8,128)S(1)} %get-tuple-element.12.near_ref), custom_call_target="tpu_custom_call" | custom-call | bytes 1048576 | tf_op jit(solution)/shard_map/pallas_call | solution.py:292
  (1 shorter events, 0.0 us)
Async XLA Ops:
  12.0 23.9 %copy-start = (bf16[1,8,3,2,128,128]{5,4,3,2,1,0:T(8,128)(2,1)S(1)}, bf16[1,8,3,2,128,128]{5,4,3,2,1,0:T(8,128)(2,1)}, u32[]{:S(2)}) copy-start(bf16[1,8,3,2,128,128]{5,4,3,2,1,0:T(8,128)(2,1)} %param.9) | copy-start | bytes 4718596
  12.0 23.9 %copy-start.1 = (bf16[1,12,2,128,128]{4,3,2,1,0:T(8,128)(2,1)S(1)}, bf16[1,12,2,128,128]{4,3,2,1,0:T(8,128)(2,1)}, u32[]{:S(2)}) copy-start(bf16[1,12,2,128,128]{4,3,2,1,0:T(8,128)(2,1)} %param.12) | copy-start | bytes 2359300
  12.0 23.9 %copy-start.2 = (bf16[1,12,2,128,128]{4,3,2,1,0:T(8,128)(2,1)S(1)}, bf16[1,12,2,128,128]{4,3,2,1,0:T(8,128)(2,1)}, u32[]{:S(2)}) copy-start(bf16[1,12,2,128,128]{4,3,2,1,0:T(8,128)(2,1)} %param.11) | copy-start | bytes 2359300

commit v13 on v11

--- a/solution.py
+++ b/solution.py
@@ -14,14 +14,19 @@
 GROUP = 8
 TILE = 2 * GROUP
 LANES = 128
+GATHER_STRIDE, SUM_STRIDE = 23, 5
 
 
 def rotated(size, first):
     return [(i + first) % size for i in range(size)]
 
 
-def first_chip(chips):
-    return chips - 2
+def chip_at(place, chips, stride):
+    return (place * stride + chips - 2) % chips
+
+
+def chip_order(chips, stride):
+    return [chip_at(place, chips, stride) for place in range(chips)]
 
 
 def dot(first_op, second_op, transposed=False):
@@ -40,7 +45,7 @@
 def leaf_codes(chunk, chips):
     at = chunk * LANES + iota((1, LANES), 1)
     core = at // (chips * TILE)
-    chip = (at // TILE + first_chip(chips)) % chips
+    chip = chip_at(at // TILE % chips, chips, GATHER_STRIDE)
     return (chip * CORES + core) * TILE + at % GROUP * 2 + at // GROUP % 2
 
 
@@ -189,7 +194,7 @@
     place = jnp.concatenate(
         [
             jnp.where(code - chip * (CORES * TILE) == base, 1.0, 0.0)
-            for chip in rotated(chips, first_chip(chips))
+            for chip in chip_order(chips, SUM_STRIDE)
         ],
         0,
     )
@@ -253,7 +258,7 @@
         spectrum_kernel, [((chips, TILE, leaf), jnp.bfloat16)], [vmem], flops=20_000_000_000
     )(shares)
     same_core = lax.all_to_all(
-        copies, "chip", 0, 0, axis_index_groups=[rotated(chips, first_chip(chips))], tiled=True
+        copies, "chip", 0, 0, axis_index_groups=[chip_order(chips, GATHER_STRIDE)], tiled=True
     )
     gathered = lax.all_gather(same_core, "core", axis=0, tiled=False)
     gathered = gathered.reshape(CORES * chips * TILE, leaf)
@@ -281,7 +286,7 @@
         "chip",
         0,
         0,
-        axis_index_groups=[rotated(chips, first_chip(chips))],
+        axis_index_groups=[chip_order(chips, SUM_STRIDE)],
         tiled=True,
     )
 

time: 52.7 us -> 52 us (0.987)
  blocking collectives: 49.6 us -> 48.8 us
    all_to_all x1, blocking collectives: 12.9 us -> 11.9 us  [per_device(): lax.all_to_all(spread.reshape(chips, TILE, leaf), 'chip', 0, 0, axis_inde...]
where the time goes in v13:
time: 52 us; the launch traced here: 51.7 us
  blocking collectives  48.8 us (94%)
  Pallas kernels  2.9 us (6%)
    all_to_all x1, blocking collectives, per_device(): lax.all_to_all(copies, 'chip', 0, 0, axis_index_groups=[chip_order(chips,...  19.7 us
    all_to_all x1, blocking collectives, per_device(): lax.all_to_all(spread.reshape(chips, TILE, leaf), 'chip', 0, 0, axis_inde...  11.9 us
    all_to_all x1, blocking collectives, per_device(): lax.all_to_all(partial.reshape(total_freq, TILE, leaf), 'freq', 0, 0, axi...  10.9 us
    all_gather x1, blocking collectives, per_device(): gathered = lax.all_gather(same_core, 'core', axis=0, tiled=False)  4.49 us
    all_gather x1, blocking collectives, per_device(): both_terms = lax.all_gather(terms, 'core', axis=0, tiled=True)  1.86 us
    pallas_call x1, Pallas kernels, per_device(): call(functools.partial(partial_kernel, total_freq, total_steps, chips), [...  1.09 us

profile of v13, /device:TPU:1, one launch (start us, length us, event | category | flops | bytes accessed | tf_op | source)
XLA Modules:
  0.0 51.7 jit_solution(6919776628309093493)
XLA Ops:
  0.0 1.1 %shard_map.82 = (f32[128,128]{1,0:T(8,128)S(1)}, bf16[80,1280]{1,0:T(8,128)(2,1)S(1)}) custom-call(bf16[64,1024]{1,0:T(8,128)(2,1)} %refs_0_.1, s32[1,12]{1,0:T(1,128)} %bitcast.17, s32[1,12]{1,0:T(1,128)} %refs_2_.1, s32[1,12]{1,0:T(1,128)} %bitcast.18, s32[3,8]{1,0:T(4,128)} %bitcast.16), custom_call_target="tpu_custom_call" | custom-call | bytes 1048576 | tf_op jit(solution)/shard_map/pallas_call | solution.py:237
  1.1 10.9 %all_to_all.15.shares_ref = f32[8,16,128]{2,1,0:T(8,128)S(1)} all-to-all(f32[8,16,128]{2,1,0:T(8,128)S(1)} %bitcast.15), channel_id=1, replica_groups={{256,320,384,448,0,64,128,192},{257,321,385,449,1,65,129,193},{258,322,..., dimensions={0} | all-to-all | bytes 131072 | tf_op jit(solution)/shard_map/all_to_all | solution.py:249
  12.0 0.0 copy-start
  12.0 0.0 copy-start.1
  12.0 0.0 copy-start.2
  12.0 19.7 %all_to_all.16 = bf16[32,16,128]{2,1,0:T(8,128)(2,1)S(1)} all-to-all(bf16[32,16,128]{2,1,0:T(8,128)(2,1)S(1)} %shard_map.83), channel_id=1, replica_groups={{60,42,24,6,52,34,16,62,44,26,8,54,36,18,0,46,28,10,56,38,20,2,48,30,12..., dimensions={0} | all-to-all | bytes 262144 | tf_op jit(solution)/shard_map/all_to_all | solution.py:260
  31.7 4.5 %all-gather = bf16[64,16,128]{2,1,0:T(8,128)(2,1)S(1)} all-gather(bf16[32,16,128]{2,1,0:T(8,128)(2,1)S(1)} %all_to_all.16), channel_id=2, replica_groups=mesh['freq'=8,'chip'=32,'core'=2] {'core'}, dimensions={0}, use_global_device_ids=true | all-gather | bytes 393216 | tf_op jit(solution)/shard_map/all_gather | solution.py:263
  36.2 0.0 copy-done
  36.2 0.0 copy-done.1
  36.2 0.0 copy-done.2
  36.2 1.0 %shard_map.84 = (bf16[32,128]{1,0:T(8,128)(2,1)S(1)}, f32[16,128]{1,0:T(8,128)S(1)}) custom-call(bf16[80,1280]{1,0:T(8,128)(2,1)S(1)} %get-tuple-element.9.pick_ref, bf16[1024,128]{1,0:T(8,128)(2,1)S(1)} %bitcast.11, bf16[12,256,128]{2,1,0:T(8,128)(2,1)S(1)} %bitcast.12, bf16[12,256,128]{2,1,0:T(8,128)(2,1)S(1)} %bitcast.13, ...), custom_call_target="tpu_custom_call" | custom-call | bytes 1048576 | tf_op jit(solution)/shard_map/pallas_call | solution.py:266
  37.2 1.9 %all_gather.11.terms_ref = bf16[64,128]{1,0:T(8,128)(2,1)S(1)} all-gather(bf16[32,128]{1,0:T(8,128)(2,1)S(1)} %get-tuple-element.11), channel_id=1, replica_groups=mesh['freq'=8,'chip'=32,'core'=2] {'core'}, dimensions={0}, use_global_device_ids=true | all-gather | bytes 24576 | tf_op jit(solution)/shard_map/all_gather | solution.py:278
  39.1 0.2 shard_map.85
  39.2 11.9 %all_to_all.17.arrived_ref = bf16[32,16,128]{2,1,0:T(8,128)(2,1)S(1)} all-to-all(bf16[32,16,128]{2,1,0:T(8,128)(2,1)S(1)} %bitcast.14), channel_id=1, replica_groups={{60,6,16,26,36,46,56,2,12,22,32,42,52,62,8,18,28,38,48,58,4,14,24,34,44..., dimensions={0} | all-to-all | bytes 262144 | tf_op jit(solution)/shard_map/all_to_all | solution.py:284
  51.1 0.6 %shard_map.86 = bf16[2,1024]{1,0:T(2,128)(2,1)} custom-call(bf16[32,16,128]{2,1,0:T(8,128)(2,1)S(1)} %all_to_all.17.arrived_ref, f32[16,128]{1,0:T(8,128)S(1)} %get-tuple-element.12.near_ref), custom_call_target="tpu_custom_call" | custom-call | bytes 1048576 | tf_op jit(solution)/shard_map/pallas_call | solution.py:293
  (1 shorter events, 0.0 us)
Async XLA Ops:
  12.0 24.2 %copy-start = (bf16[1,8,3,2,128,128]{5,4,3,2,1,0:T(8,128)(2,1)S(1)}, bf16[1,8,3,2,128,128]{5,4,3,2,1,0:T(8,128)(2,1)}, u32[]{:S(2)}) copy-start(bf16[1,8,3,2,128,128]{5,4,3,2,1,0:T(8,128)(2,1)} %param.9) | copy-start | bytes 4718596
  12.0 24.2 %copy-start.1 = (bf16[1,12,2,128,128]{4,3,2,1,0:T(8,128)(2,1)S(1)}, bf16[1,12,2,128,128]{4,3,2,1,0:T(8,128)(2,1)}, u32[]{:S(2)}) copy-start(bf16[1,12,2,128,128]{4,3,2,1,0:T(8,128)(2,1)} %param.12) | copy-start | bytes 2359300
  12.0 24.2 %copy-start.2 = (bf16[1,12,2,128,128]{4,3,2,1,0:T(8,128)(2,1)S(1)}, bf16[1,12,2,128,128]{4,3,2,1,0:T(8,128)(2,1)}, u32[]{:S(2)}) copy-start(bf16[1,12,2,128,128]{4,3,2,1,0:T(8,128)(2,1)} %param.11) | copy-start | bytes 2359300

commit v14 on v13

--- a/solution.py
+++ b/solution.py
@@ -14,6 +14,7 @@
 GROUP = 8
 TILE = 2 * GROUP
 LANES = 128
+PARTS = 4
 GATHER_STRIDE, SUM_STRIDE = 23, 5
 
 
@@ -92,8 +93,16 @@
     count = (len(refs) - 3) // 2
     out_ref, pick_ref = refs[count : count + 2]
     history_ref, *index_refs = refs[count + 2 : -1]
+    width = history_ref.shape[1] // PARTS
+    columns = [pl.ds(part * width, width) for part in range(PARTS)]
     copies = [
-        pltpu.make_async_copy(refs[i], refs[count + 2 + i], refs[-1].at[i]) for i in range(count)
+        pltpu.make_async_copy(
+            refs[0].at[:, columns[part]], history_ref.at[:, columns[part]], refs[-1].at[part]
+        )
+        for part in range(PARTS)
+    ] + [
+        pltpu.make_async_copy(refs[i], refs[count + 2 + i], refs[-1].at[PARTS + i - 1])
+        for i in range(1, count)
     ]
     for copy in copies:
         copy.start()
@@ -243,7 +252,7 @@
         [pl.ANY] * len(arrays),
         [
             *[pltpu.VMEM(array.shape, array.dtype) for array in arrays],
-            pltpu.SemaphoreType.DMA((len(arrays),)),
+            pltpu.SemaphoreType.DMA((PARTS + len(arrays) - 1,)),
         ],
     )(*[pltpu.with_memory_space_constraint(array, pltpu.HBM) for array in arrays])
     shares = lax.all_to_all(

time: 52 us -> 52 us (level)
  no operation moved by 1% of the time
where the time goes in v14:
time: 52 us; the launch traced here: 51.7 us
  blocking collectives  48.8 us (94%)
  Pallas kernels  2.83 us (5%)
    all_to_all x1, blocking collectives, per_device(): lax.all_to_all(copies, 'chip', 0, 0, axis_index_groups=[chip_order(chips,...  19.7 us
    all_to_all x1, blocking collectives, per_device(): lax.all_to_all(spread.reshape(chips, TILE, leaf), 'chip', 0, 0, axis_inde...  11.9 us
    all_to_all x1, blocking collectives, per_device(): lax.all_to_all(partial.reshape(total_freq, TILE, leaf), 'freq', 0, 0, axi...  10.9 us
    all_gather x1, blocking collectives, per_device(): gathered = lax.all_gather(same_core, 'core', axis=0, tiled=False)  4.49 us
    all_gather x1, blocking collectives, per_device(): both_terms = lax.all_gather(terms, 'core', axis=0, tiled=True)  1.86 us

profile of v14, /device:TPU:1, one launch (start us, length us, event | category | flops | bytes accessed | tf_op | source)
XLA Modules:
  0.0 51.7 jit_solution(9911037272984144878)
XLA Ops:
  0.0 1.0 %shard_map.82 = (f32[128,128]{1,0:T(8,128)S(1)}, bf16[80,1280]{1,0:T(8,128)(2,1)S(1)}) custom-call(bf16[64,1024]{1,0:T(8,128)(2,1)} %refs_0_.1, s32[1,12]{1,0:T(1,128)} %bitcast.17, s32[1,12]{1,0:T(1,128)} %refs_2_.1, s32[1,12]{1,0:T(1,128)} %bitcast.18, s32[3,8]{1,0:T(4,128)} %bitcast.16), custom_call_target="tpu_custom_call" | custom-call | bytes 1048576 | tf_op jit(solution)/shard_map/pallas_call | solution.py:246
  1.0 10.9 %all_to_all.15.shares_ref = f32[8,16,128]{2,1,0:T(8,128)S(1)} all-to-all(f32[8,16,128]{2,1,0:T(8,128)S(1)} %bitcast.15), channel_id=1, replica_groups={{256,320,384,448,0,64,128,192},{257,321,385,449,1,65,129,193},{258,322,..., dimensions={0} | all-to-all | bytes 131072 | tf_op jit(solution)/shard_map/all_to_all | solution.py:258
  11.9 0.0 copy-start
  11.9 0.0 copy-start.1
  11.9 0.0 copy-start.2
  11.9 19.7 %all_to_all.16 = bf16[32,16,128]{2,1,0:T(8,128)(2,1)S(1)} all-to-all(bf16[32,16,128]{2,1,0:T(8,128)(2,1)S(1)} %shard_map.83), channel_id=1, replica_groups={{60,42,24,6,52,34,16,62,44,26,8,54,36,18,0,46,28,10,56,38,20,2,48,30,12..., dimensions={0} | all-to-all | bytes 262144 | tf_op jit(solution)/shard_map/all_to_all | solution.py:269
  31.6 4.5 %all-gather = bf16[64,16,128]{2,1,0:T(8,128)(2,1)S(1)} all-gather(bf16[32,16,128]{2,1,0:T(8,128)(2,1)S(1)} %all_to_all.16), channel_id=2, replica_groups=mesh['freq'=8,'chip'=32,'core'=2] {'core'}, dimensions={0}, use_global_device_ids=true | all-gather | bytes 393216 | tf_op jit(solution)/shard_map/all_gather | solution.py:272
  36.1 0.0 copy-done
  36.1 0.0 copy-done.1
  36.1 0.0 copy-done.2
  36.1 1.0 %shard_map.84 = (bf16[32,128]{1,0:T(8,128)(2,1)S(1)}, f32[16,128]{1,0:T(8,128)S(1)}) custom-call(bf16[80,1280]{1,0:T(8,128)(2,1)S(1)} %get-tuple-element.9.pick_ref, bf16[1024,128]{1,0:T(8,128)(2,1)S(1)} %bitcast.11, bf16[12,256,128]{2,1,0:T(8,128)(2,1)S(1)} %bitcast.12, bf16[12,256,128]{2,1,0:T(8,128)(2,1)S(1)} %bitcast.13, ...), custom_call_target="tpu_custom_call" | custom-call | bytes 1048576 | tf_op jit(solution)/shard_map/pallas_call | solution.py:275
  37.1 1.9 %all_gather.11.terms_ref = bf16[64,128]{1,0:T(8,128)(2,1)S(1)} all-gather(bf16[32,128]{1,0:T(8,128)(2,1)S(1)} %get-tuple-element.11), channel_id=1, replica_groups=mesh['freq'=8,'chip'=32,'core'=2] {'core'}, dimensions={0}, use_global_device_ids=true | all-gather | bytes 24576 | tf_op jit(solution)/shard_map/all_gather | solution.py:287
  39.0 0.2 shard_map.85
  39.2 11.9 %all_to_all.17.arrived_ref = bf16[32,16,128]{2,1,0:T(8,128)(2,1)S(1)} all-to-all(bf16[32,16,128]{2,1,0:T(8,128)(2,1)S(1)} %bitcast.14), channel_id=1, replica_groups={{60,6,16,26,36,46,56,2,12,22,32,42,52,62,8,18,28,38,48,58,4,14,24,34,44..., dimensions={0} | all-to-all | bytes 262144 | tf_op jit(solution)/shard_map/all_to_all | solution.py:293
  51.0 0.6 %shard_map.86 = bf16[2,1024]{1,0:T(2,128)(2,1)} custom-call(bf16[32,16,128]{2,1,0:T(8,128)(2,1)S(1)} %all_to_all.17.arrived_ref, f32[16,128]{1,0:T(8,128)S(1)} %get-tuple-element.12.near_ref), custom_call_target="tpu_custom_call" | custom-call | bytes 1048576 | tf_op jit(solution)/shard_map/pallas_call | solution.py:302
  (1 shorter events, 0.0 us)
Async XLA Ops:
  11.9 24.2 %copy-start = (bf16[1,8,3,2,128,128]{5,4,3,2,1,0:T(8,128)(2,1)S(1)}, bf16[1,8,3,2,128,128]{5,4,3,2,1,0:T(8,128)(2,1)}, u32[]{:S(2)}) copy-start(bf16[1,8,3,2,128,128]{5,4,3,2,1,0:T(8,128)(2,1)} %param.9) | copy-start | bytes 4718596
  11.9 24.2 %copy-start.1 = (bf16[1,12,2,128,128]{4,3,2,1,0:T(8,128)(2,1)S(1)}, bf16[1,12,2,128,128]{4,3,2,1,0:T(8,128)(2,1)}, u32[]{:S(2)}) copy-start(bf16[1,12,2,128,128]{4,3,2,1,0:T(8,128)(2,1)} %param.12) | copy-start | bytes 2359300
  11.9 24.2 %copy-start.2 = (bf16[1,12,2,128,128]{4,3,2,1,0:T(8,128)(2,1)S(1)}, bf16[1,12,2,128,128]{4,3,2,1,0:T(8,128)(2,1)}, u32[]{:S(2)}) copy-start(bf16[1,12,2,128,128]{4,3,2,1,0:T(8,128)(2,1)} %param.11) | copy-start | bytes 2359300

commit v15 on v14

--- a/solution.py
+++ b/solution.py
@@ -86,7 +86,6 @@
     goal = jnp.where(row == spare, target >> 3, jnp.where(row == spare + 1, target & 7, 0))
     extra = jnp.concatenate([by_row(ranks_ref), goal.astype(jnp.float32)], 1)
     pick_ref[:rows, chunks * LANES :] = extra.astype(jnp.bfloat16)
-    pick_ref[rows:, chunks * LANES :] = jnp.zeros((near * TILE, 2 * LANES), jnp.bfloat16)
 
 
 def partial_kernel(total_freq, total_steps, chips, *refs):
@@ -149,13 +148,14 @@
         (slice(2 * start, 2 * start + TILE), start, min(start + GROUP, tasks))
         for start in range(0, tasks, GROUP)
     ]
-    coeffs, near_sums = [], near_part(0)
+    coeffs = []
     for rows, start, stop in groups:
         coeff = jnp.zeros((TILE, leaf), jnp.float32)
         pair = jnp.concatenate([picked[rows], times_i(picked[rows])], 1).astype(jnp.bfloat16)
         for t in range(start, stop):
             coeff = jnp.where(own == t - start, dot(pair, right_ref[t]), coeff)
         coeffs.append(jnp.where(lane < extra[rows, :leaf], coeff, 0.0).astype(jnp.bfloat16))
+    near_sums = near_part(0)
     for n in range(1, near):
         near_sums = near_sums + near_part(n)
     for (rows, start, stop), coeff in zip(groups, coeffs):

time: 52 us -> 52 us (level)
  no operation moved by 1% of the time
where the time goes in v15:
time: 52 us; the launch traced here: 51.7 us
  blocking collectives  48.8 us (94%)
  Pallas kernels  2.84 us (5%)
    all_to_all x1, blocking collectives, per_device(): lax.all_to_all(copies, 'chip', 0, 0, axis_index_groups=[chip_order(chips,...  19.7 us
    all_to_all x1, blocking collectives, per_device(): lax.all_to_all(spread.reshape(chips, TILE, leaf), 'chip', 0, 0, axis_inde...  11.9 us
    all_to_all x1, blocking collectives, per_device(): lax.all_to_all(partial.reshape(total_freq, TILE, leaf), 'freq', 0, 0, axi...  10.9 us
    all_gather x1, blocking collectives, per_device(): gathered = lax.all_gather(same_core, 'core', axis=0, tiled=False)  4.49 us
    all_gather x1, blocking collectives, per_device(): both_terms = lax.all_gather(terms, 'core', axis=0, tiled=True)  1.86 us

profile of v15, /device:TPU:1, one launch (start us, length us, event | category | flops | bytes accessed | tf_op | source)
XLA Modules:
  0.0 51.7 jit_solution(5831823979842870102)
XLA Ops:
  0.0 1.0 %shard_map.82 = (f32[128,128]{1,0:T(8,128)S(1)}, bf16[80,1280]{1,0:T(8,128)(2,1)S(1)}) custom-call(bf16[64,1024]{1,0:T(8,128)(2,1)} %refs_0_.1, s32[1,12]{1,0:T(1,128)} %bitcast.17, s32[1,12]{1,0:T(1,128)} %refs_2_.1, s32[1,12]{1,0:T(1,128)} %bitcast.18, s32[3,8]{1,0:T(4,128)} %bitcast.16), custom_call_target="tpu_custom_call" | custom-call | bytes 1048576 | tf_op jit(solution)/shard_map/pallas_call | solution.py:246
  1.0 10.9 %all_to_all.15.shares_ref = f32[8,16,128]{2,1,0:T(8,128)S(1)} all-to-all(f32[8,16,128]{2,1,0:T(8,128)S(1)} %bitcast.15), channel_id=1, replica_groups={{256,320,384,448,0,64,128,192},{257,321,385,449,1,65,129,193},{258,322,..., dimensions={0} | all-to-all | bytes 131072 | tf_op jit(solution)/shard_map/all_to_all | solution.py:258
  11.9 0.0 copy-start
  11.9 0.0 copy-start.1
  11.9 0.0 copy-start.2
  11.9 19.7 %all_to_all.16 = bf16[32,16,128]{2,1,0:T(8,128)(2,1)S(1)} all-to-all(bf16[32,16,128]{2,1,0:T(8,128)(2,1)S(1)} %shard_map.83), channel_id=1, replica_groups={{60,42,24,6,52,34,16,62,44,26,8,54,36,18,0,46,28,10,56,38,20,2,48,30,12..., dimensions={0} | all-to-all | bytes 262144 | tf_op jit(solution)/shard_map/all_to_all | solution.py:269
  31.6 4.5 %all-gather = bf16[64,16,128]{2,1,0:T(8,128)(2,1)S(1)} all-gather(bf16[32,16,128]{2,1,0:T(8,128)(2,1)S(1)} %all_to_all.16), channel_id=2, replica_groups=mesh['freq'=8,'chip'=32,'core'=2] {'core'}, dimensions={0}, use_global_device_ids=true | all-gather | bytes 393216 | tf_op jit(solution)/shard_map/all_gather | solution.py:272
  36.1 0.0 copy-done
  36.1 0.0 copy-done.1
  36.1 0.0 copy-done.2
  36.1 1.0 %shard_map.84 = (bf16[32,128]{1,0:T(8,128)(2,1)S(1)}, f32[16,128]{1,0:T(8,128)S(1)}) custom-call(bf16[80,1280]{1,0:T(8,128)(2,1)S(1)} %get-tuple-element.9.pick_ref, bf16[1024,128]{1,0:T(8,128)(2,1)S(1)} %bitcast.11, bf16[12,256,128]{2,1,0:T(8,128)(2,1)S(1)} %bitcast.12, bf16[12,256,128]{2,1,0:T(8,128)(2,1)S(1)} %bitcast.13, ...), custom_call_target="tpu_custom_call" | custom-call | bytes 1048576 | tf_op jit(solution)/shard_map/pallas_call | solution.py:275
  37.1 1.9 %all_gather.11.terms_ref = bf16[64,128]{1,0:T(8,128)(2,1)S(1)} all-gather(bf16[32,128]{1,0:T(8,128)(2,1)S(1)} %get-tuple-element.11), channel_id=1, replica_groups=mesh['freq'=8,'chip'=32,'core'=2] {'core'}, dimensions={0}, use_global_device_ids=true | all-gather | bytes 24576 | tf_op jit(solution)/shard_map/all_gather | solution.py:287
  39.0 0.2 shard_map.85
  39.2 11.9 %all_to_all.17.arrived_ref = bf16[32,16,128]{2,1,0:T(8,128)(2,1)S(1)} all-to-all(bf16[32,16,128]{2,1,0:T(8,128)(2,1)S(1)} %bitcast.14), channel_id=1, replica_groups={{60,6,16,26,36,46,56,2,12,22,32,42,52,62,8,18,28,38,48,58,4,14,24,34,44..., dimensions={0} | all-to-all | bytes 262144 | tf_op jit(solution)/shard_map/all_to_all | solution.py:293
  51.0 0.6 %shard_map.86 = bf16[2,1024]{1,0:T(2,128)(2,1)} custom-call(bf16[32,16,128]{2,1,0:T(8,128)(2,1)S(1)} %all_to_all.17.arrived_ref, f32[16,128]{1,0:T(8,128)S(1)} %get-tuple-element.12.near_ref), custom_call_target="tpu_custom_call" | custom-call | bytes 1048576 | tf_op jit(solution)/shard_map/pallas_call | solution.py:302
  (1 shorter events, 0.0 us)
Async XLA Ops:
  11.9 24.2 %copy-start = (bf16[1,8,3,2,128,128]{5,4,3,2,1,0:T(8,128)(2,1)S(1)}, bf16[1,8,3,2,128,128]{5,4,3,2,1,0:T(8,128)(2,1)}, u32[]{:S(2)}) copy-start(bf16[1,8,3,2,128,128]{5,4,3,2,1,0:T(8,128)(2,1)} %param.9) | copy-start | bytes 4718596
  11.9 24.2 %copy-start.1 = (bf16[1,12,2,128,128]{4,3,2,1,0:T(8,128)(2,1)S(1)}, bf16[1,12,2,128,128]{4,3,2,1,0:T(8,128)(2,1)}, u32[]{:S(2)}) copy-start(bf16[1,12,2,128,128]{4,3,2,1,0:T(8,128)(2,1)} %param.12) | copy-start | bytes 2359300
  11.9 24.2 %copy-start.2 = (bf16[1,12,2,128,128]{4,3,2,1,0:T(8,128)(2,1)S(1)}, bf16[1,12,2,128,128]{4,3,2,1,0:T(8,128)(2,1)}, u32[]{:S(2)}) copy-start(bf16[1,12,2,128,128]{4,3,2,1,0:T(8,128)(2,1)} %param.11) | copy-start | bytes 2359300
